TPU v7x, 32 devices: a whole 2x2x4 slice. The times are simulated.
32 devices in a mesh: grp: 4 (over y, core), dev: 8 (over z, x).
Axes of the slice: x: 2, y: 2, z: 4, core: 2. Of those that a mesh axis runs over, the one named last changes fastest.
Arguments:
- embeddings: bfloat16 [24576, 1024], P(('grp', 'dev')), may hold values from -6 to 6
- level_one: int32 [24576, 1], P(('grp', 'dev')), may hold values from 0 to 3; in each aligned block of 768 rows (0 to 767, 768 to 1535, ...) at most 384 rows name the same one
- centroids: bfloat16 [8192, 1024], P(('grp', 'dev')), may hold values from -6 to 6
Outputs:
- new_centroids: float32 [8192, 1024], P(('grp', 'dev'))
- column_mass: float32 [8192], P(('grp', 'dev'))
Inputs may be any that keep to these rules, and one draw needn't show every extreme that they name: `level_one`: among the rows of one device no level-1 id appears more than 384 times, and every id appears somewhere.
All inputs are finite; a program needn't handle non-finite values.
Results may differ from a plain program's by a relative error of at most 0.018.
Values may be sent and summed in bfloat16 or wider, within the bound.
No kernel may reach another device: no remote copies, remote signals or barrier semaphores. Data moves between devices by JAX's collectives and lax.ppermute only.
A program may use at most 64 MiB of HBM per device.

v0:
```python
import math

import jax
import jax.numpy as jnp
from jax import lax
from jax.sharding import PartitionSpec as P

SWEEPS = 3


def rms_normalize(vectors):
    wide = vectors.astype(jnp.float32)
    inverse = lax.rsqrt(jnp.mean(wide * wide, axis=-1, keepdims=True) + 1e-06)
    return (wide * inverse).astype(jnp.bfloat16)


def body(embeddings, level_one, centroids):
    groups = lax.axis_size("grp")
    local_count = embeddings.shape[0]
    feature_width = embeddings.shape[1]
    capacity = 2 * local_count // groups
    target = level_one[:, 0]
    onehot = (target[:, None] == jnp.arange(groups, dtype=jnp.int32)[None, :]).astype(jnp.int32)
    before = jnp.cumsum(onehot, axis=0) - onehot
    within = jnp.sum(before * onehot, axis=1)
    destination = target * capacity + within
    outgoing = (
        jnp.zeros((groups * capacity, feature_width), jnp.bfloat16).at[destination].set(embeddings)
    )
    present = jnp.zeros((groups * capacity,), jnp.bfloat16).at[destination].set(1.0)
    arrived, arrived_mask = (
        lax.all_to_all(
            outgoing.reshape(groups, capacity, feature_width),
            "grp",
            split_axis=0,
            concat_axis=0,
            tiled=True,
        ),
        lax.all_to_all(
            present.reshape(groups, capacity), "grp", split_axis=0, concat_axis=0, tiled=True
        ),
    )
    group_rows = arrived.reshape(groups * capacity, feature_width)
    valid_mask = arrived_mask.reshape(groups * capacity).astype(jnp.float32)
    normed = rms_normalize(group_rows)
    factor = 3.0 / math.sqrt(feature_width)
    own_normed = rms_normalize(centroids)
    scores = lax.dot_general(
        normed,
        lax.all_gather(own_normed, "dev", axis=0, tiled=True),
        (((1,), (1,)), ((), ())),
        preferred_element_type=jnp.float32,
    )
    weights = (jnp.exp(scores * factor) * valid_mask[:, None]).astype(jnp.bfloat16)
    row_scale = valid_mask
    column_scale = jnp.ones((weights.shape[1],), jnp.float32)
    for sweep_index in range(SWEEPS):
        partial_total = jnp.sum(weights.astype(jnp.float32) * row_scale[:, None], axis=0)
        column_total = lax.psum(partial_total, "dev")
        column_scale = 1.0 / column_total
        row_total = jnp.sum(weights.astype(jnp.float32) * column_scale[None, :], axis=1)
        row_scale = valid_mask / (row_total + 1.0 - valid_mask)
    transport = weights.astype(jnp.float32) * row_scale[:, None] * column_scale[None, :]
    mass_part = jnp.sum(transport, axis=0)
    shared = transport.astype(jnp.bfloat16)
    owners = centroids.shape[0]
    numerator = lax.psum_scatter(
        lax.dot_general(
            shared, group_rows, (((0,), (0,)), ((), ())), preferred_element_type=jnp.float32
        ).astype(jnp.bfloat16),
        "dev",
        scatter_dimension=0,
        tiled=True,
    ).astype(jnp.float32)
    total_mass = lax.psum(mass_part, "dev")
    own_mass = lax.dynamic_slice_in_dim(total_mass, lax.axis_index("dev") * owners, owners, 0)
    return (numerator / own_mass[:, None], own_mass)


def solution(mesh):
    in_specs = (P(("grp", "dev"), None), P(("grp", "dev"), None), P(("grp", "dev"), None))
    out_specs = (P(("grp", "dev"), None), P(("grp", "dev")))
    return jax.shard_map(body, mesh=mesh, in_specs=in_specs, out_specs=out_specs, check_vma=False)
```

profile of v0, /device:TPU:1, one launch (start us, length us, event | category | flops | bytes accessed | tf_op | source)
XLA Modules:
  0.0 279.6 jit_solution(10861742763144971712)
XLA Ops:
  7.2 1.2 fusion.19
  8.4 2.0 fusion.20
  10.5 0.7 reduce.1
  11.2 1.1 reduce-window.6
  12.3 0.2 slice_reduce_fusion
  12.8 0.7 fusion.25
  13.5 8.6 %scatter_custom_fusion.1 = bf16[1536]{0:T(1024)(128)(2,1)S(1)} fusion(s32[768]{0:T(1024)S(1)} %fusion.25, bf16[768]{0:T(1024)(128)(2,1)S(1)} %broadcast.77, bf16[]{:T(256)} %constant.13.clone.1), kind=kCustom, calls=%fused_computation.52 | custom fusion | bytes 3074 | tf_op jit(solution)/shard_map/scatter | solution.py:30
  22.2 0.5 broadcast.93
  22.7 0.7 reduce.9
  23.4 0.7 reshape.125
  24.1 4.3 %all-to-all-start.1 = ((bf16[4,2,192]{2,1,0:T(2,128)(2,1)}), bf16[4,2,192]{2,1,0:T(2,128)(2,1)S(1)}, u32[]{:S(2)}, u32[]{:S(2)}) async-start(bf16[4,2,192]{2,1,0:T(2,128)(2,1)} %reshape.125), calls=%async_computation.1 | async-start | bytes 8192 | tf_op jit(solution)/shard_map/all_to_all | solution.py:39
  28.4 8.5 %scatter_custom_fusion = bf16[1536,1024]{1,0:T(8,128)(2,1)} fusion(s32[768]{0:T(1024)S(1)} %fusion.25, bf16[768,1024]{1,0:T(8,128)(2,1)} %param.3, bf16[]{:T(256)} %constant.13.clone.1), kind=kCustom, calls=%fused_computation.26 | custom fusion | bytes 3146240 | tf_op jit(solution)/shard_map/scatter | solution.py:28
  36.9 3.7 %all-to-all-start = ((bf16[4,384,1024]{2,1,0:T(8,128)(2,1)}), bf16[4,384,1024]{2,1,0:T(8,128)(2,1)S(1)}, u32[]{:S(2)}, u32[]{:S(2)}) async-start(bf16[4,384,1024]{2,1,0:T(8,128)(2,1)} %bitcast.26), calls=%async_computation | async-start | bytes 6291456 | tf_op jit(solution)/shard_map/all_to_all | solution.py:32
  40.6 0.2 reduce-scatter.2.cloned.1.call-start
  40.9 35.8 %all-to-all-done = bf16[4,384,1024]{2,1,0:T(8,128)(2,1)S(1)} async-done(((bf16[4,384,1024]{2,1,0:T(8,128)(2,1)}), bf16[4,384,1024]{2,1,0:T(8,128)(2,1)S(1)}, u32[]{:S(2)}, u32[]{:S(2)}) %all-to-all-start) | async-done | bytes 3145760 | tf_op jit(solution)/shard_map/all_to_all | solution.py:32
  76.7 0.7 multiply_reduce_fusion
  77.4 7.7 %all-gather.2.cloned.1.call-done = bf16[2048,1024]{1,0:T(8,128)(2,1)} async-done(((bf16[256,1024]{1,0:T(8,128)(2,1)}), bf16[2048,1024]{1,0:T(8,128)(2,1)}) %all-gather.2.cloned.1.call-update) | async-done | bytes 4194320 | tf_op jit(solution)/shard_map/all_gather | solution.py:50
  85.1 12.2 %fusion = (f32[2048]{0:T(1024)S(1)}, bf16[1536,2048]{1,0:T(8,128)(2,1)}) fusion(f32[1536]{0:T(1024)S(1)} %reshape.99, bf16[2048,1024]{1,0:T(8,128)(2,1)} %all-gather.2.cloned.1.call-done, bf16[1536,1024]{1,0:T(8,128)(2,1)S(1)} %bitcast.24, f32[1536]{0:T(1024)S(1)} %rsqrt.20), kind=kOutput, calls=%fused_computation.9 | convolution fusion | flops 6466041856 | bytes 13651968 | tf_op jit(solution)/shard_map/dot_general | solution.py:48
  97.3 16.4 %psum.28 = f32[2048]{0:T(1024)S(1)} all-reduce(f32[2048]{0:T(1024)S(1)} %get-tuple-element.2), channel_id=1, replica_groups=mesh['grp'=4,'dev'=8] {'dev'}, use_global_device_ids=true, to_apply=%region_8.9 | all-reduce | flops 2048 | bytes 16384 | tf_op jit(solution)/shard_map/psum | solution.py:59
  113.8 4.3 %fusion.1 = f32[1536]{0:T(1024)S(1)} fusion(bf16[1536,2048]{1,0:T(8,128)(2,1)} %get-tuple-element.3, f32[2048]{0:T(1024)S(1)} %broadcast_divide_fusion.2), kind=kLoop, calls=%fused_computation.10 | loop fusion | flops 9435648 | bytes 6305792 | tf_op jit(solution)/shard_map/reduce_sum | solution.py:61
  118.1 0.3 copy-done
  118.4 1.3 fusion.2
  119.7 13.9 %psum.29 = f32[2048]{0:T(1024)S(1)} all-reduce(f32[2048]{0:T(1024)S(1)} %fusion.2), channel_id=1, replica_groups=mesh['grp'=4,'dev'=8] {'dev'}, use_global_device_ids=true, to_apply=%region_11.12 | all-reduce | flops 2048 | bytes 16384 | tf_op jit(solution)/shard_map/psum | solution.py:59
  133.6 4.1 %fusion.3 = f32[1536]{0:T(1024)S(1)} fusion(bf16[1536,2048]{1,0:T(8,128)(2,1)} %get-tuple-element.3, f32[2048]{0:T(1024)S(1)} %broadcast_divide_fusion.1), kind=kLoop, calls=%fused_computation.12 | loop fusion | flops 9435648 | bytes 6305792 | tf_op jit(solution)/shard_map/reduce_sum | solution.py:61
  137.7 4.1 %fusion.4 = f32[2048]{0:T(1024)S(1)} fusion(bf16[1536,2048]{1,0:T(8,128)(2,1)} %get-tuple-element.3, f32[1536]{0:T(1024)S(1)} %subtract_divide_fusion.1), kind=kLoop, calls=%fused_computation.13 | loop fusion | flops 9435136 | bytes 6305792 | tf_op jit(solution)/shard_map/reduce_sum | solution.py:58
  141.8 15.8 %psum.30 = f32[2048]{0:T(1024)S(1)} all-reduce(f32[2048]{0:T(1024)S(1)} %fusion.4), channel_id=1, replica_groups=mesh['grp'=4,'dev'=8] {'dev'}, use_global_device_ids=true, to_apply=%region_14.15 | all-reduce | flops 2048 | bytes 16384 | tf_op jit(solution)/shard_map/psum | solution.py:59
  157.6 4.1 %fusion.5 = f32[1536]{0:T(1024)S(1)} fusion(bf16[1536,2048]{1,0:T(8,128)(2,1)} %get-tuple-element.3, f32[2048]{0:T(1024)S(1)} %broadcast_divide_fusion), kind=kLoop, calls=%fused_computation.14 | loop fusion | flops 9435648 | bytes 6305792 | tf_op jit(solution)/shard_map/reduce_sum | solution.py:61
  161.8 12.1 %fusion.13 = bf16[2048,1024]{1,0:T(8,128)(2,1)} fusion(bf16[1536,1024]{1,0:T(8,128)(2,1)S(1)} %bitcast.25, bf16[1536,2048]{1,0:T(8,128)(2,1)} %get-tuple-element.3, f32[1536]{0:T(1024)S(1)} %subtract_divide_fusion, f32[2048]{0:T(1024)S(1)} %broadcast_divide_fusion), kind=kOutput, calls=%fused_computation.24 | convolution fusion | flops 6457131008 | bytes 13645824 | tf_op jit(solution)/shard_map/dot_general | solution.py:68
  173.9 4.5 %fusion.7 = f32[2048]{0:T(1024)S(1)} fusion(bf16[1536,2048]{1,0:T(8,128)(2,1)} %get-tuple-element.3, f32[1536]{0:T(1024)S(1)} %subtract_divide_fusion, f32[2048]{0:T(1024)S(1)} %broadcast_divide_fusion), kind=kLoop, calls=%fused_computation.16 | loop fusion | flops 12580864 | bytes 6313984 | tf_op jit(solution)/shard_map/reduce_sum | solution.py:64
  178.4 14.3 %psum.31 = f32[2048]{0:T(1024)S(1)} all-reduce(f32[2048]{0:T(1024)S(1)} %fusion.7), channel_id=1, replica_groups=mesh['grp'=4,'dev'=8] {'dev'}, use_global_device_ids=true, to_apply=%region_18.19 | all-reduce | flops 2048 | bytes 16384 | tf_op jit(solution)/shard_map/psum | solution.py:75
  192.8 77.8 %reduce-scatter.2.cloned.1.call-done = bf16[256,1024]{1,0:T(8,128)(2,1)} async-done(((bf16[2048,1024]{1,0:T(8,128)(2,1)}), bf16[256,1024]{1,0:T(8,128)(2,1)}) %reduce-scatter.2.cloned.1.call-update) | async-done | bytes 524304 | tf_op jit(solution)/shard_map/reduce_scatter | solution.py:67
  270.6 2.2 convert_divide_fusion
  (26 shorter events, 0.7 us)
Async XLA Ops:
  7.2 77.9 %all-gather.2.cloned.1.call-start = ((), (), s32[]{:S(2)}) async-start(), calls=%async_computation.3 | async-start | bytes 4718592 | tf_op jit(solution)/shard_map/all_gather | solution.py:50
  24.1 12.8 %all-to-all-start.1 = ((bf16[4,2,192]{2,1,0:T(2,128)(2,1)}), bf16[4,2,192]{2,1,0:T(2,128)(2,1)S(1)}, u32[]{:S(2)}, u32[]{:S(2)}) async-start(bf16[4,2,192]{2,1,0:T(2,128)(2,1)} %reshape.125), calls=%async_computation.1 | async-start | bytes 8192 | tf_op jit(solution)/shard_map/all_to_all | solution.py:39
  36.9 39.8 %all-to-all-start = ((bf16[4,384,1024]{2,1,0:T(8,128)(2,1)}), bf16[4,384,1024]{2,1,0:T(8,128)(2,1)S(1)}, u32[]{:S(2)}, u32[]{:S(2)}) async-start(bf16[4,384,1024]{2,1,0:T(8,128)(2,1)} %bitcast.26), calls=%async_computation | async-start | bytes 6291456 | tf_op jit(solution)/shard_map/all_to_all | solution.py:32
  40.6 230.0 %reduce-scatter.2.cloned.1.call-start = ((), (), s32[]{:S(2)}) async-start(), calls=%async_computation.4 | async-start | bytes 4718592 | tf_op jit(solution)/shard_map/reduce_scatter | solution.py:67
  113.8 4.6 %copy-start = (bf16[1536,2048]{1,0:T(8,128)(2,1)S(1)}, bf16[1536,2048]{1,0:T(8,128)(2,1)}, u32[]{:S(2)}) copy-start(bf16[1536,2048]{1,0:T(8,128)(2,1)} %get-tuple-element.3) | copy-start | bytes 18874372
  192.8 79.9 %copy-start.1 = (f32[256]{0:T(256)}, f32[256]{0:T(256)S(1)}, u32[]{:S(2)}) copy-start(f32[256]{0:T(256)S(1)} %dynamic_slice.3) | copy-start | bytes 3076
Sparse Core Ops, SparseCore 0:
  10.7 74.3 all-gather.1
  174.0 96.5 reduce-scatter.1
where the time goes:
time: 281 us; the launch traced here: 280 us
  waiting for transfers between devices  121 us (43%)
  blocking collectives  60.5 us (22%)
  other arithmetic  32 us (11%)
  matrix products  24.3 us (9%)
  local copies, waits for them, and re-layouts  19.1 us (7%)
  between operations  14.2 us (5%)
  starting transfers between devices  8.24 us (3%)
    reduce_scatter x1, waiting for transfers between devices, body(): lax.psum_scatter(lax.dot_general(shared, group_rows, (((0,), (0,)), ((),...  77.8 us
    psum x3, blocking collectives, body(): column_total = lax.psum(partial_total, 'dev')  46.2 us
    all_to_all x1, waiting for transfers between devices, body(): lax.all_to_all(outgoing.reshape(groups, capacity, feature_width), 'grp',...  35.8 us
    psum x1, blocking collectives, body(): total_mass = lax.psum(mass_part, 'dev')  14.3 us
    reduce_sum x3, other arithmetic, body(): jnp.sum(weights.astype(jnp.float32) * column_scale[None, :], axis=1)  12.5 us
    dot_general x1, matrix products, body(): lax.dot_general(normed, lax.all_gather(own_normed, 'dev', axis=0, tiled=T...  12.2 us
    dot_general x1, matrix products, body(): lax.dot_general(shared, group_rows, (((0,), (0,)), ((), ())), preferred_e...  12.1 us
    scatter x1, local copies, waits for them, and re-layouts, body(): jnp.zeros((groups * capacity,), jnp.bfloat16).at[destination].set(1.0)  8.62 us
  transfers between devices with their start and end apart: 4, of which 3 were waited for; matrix products, arithmetic and copies ran while one was open for 10% of the time, Pallas kernels for 0%

commit v1 on v0

v1 whole, which is shorter than its diff:
```python
import functools
import math

import jax
import jax.numpy as jnp
from jax import lax
from jax.experimental import pallas as pl
from jax.experimental.pallas import tpu as pltpu
from jax.sharding import PartitionSpec as P

SWEEPS = 3
EMPTY = 64.0
AXES = ("grp", "dev")
F32 = jnp.float32
BF16 = jnp.bfloat16
NT = (((1,), (1,)), ((), ()))
NN = (((1,), (0,)), ((), ()))
VMEM = pl.BlockSpec(memory_space=pltpu.VMEM)
PARAMS = pltpu.CompilerParams(vmem_limit_bytes=40 * 1024 * 1024)


def permutation(groups, peers, move):
    pairs = []
    for grp in range(groups):
        for dev in range(peers):
            pair, side, place, half = move(grp // 2, grp % 2, dev // 2, dev % 2)
            pairs.append((grp * peers + dev, (2 * pair + side) * peers + 2 * place + half))
    return pairs


class Routes:
    def __init__(self, groups, peers):
        self.ring = peers // 2
        make = functools.partial(permutation, groups, peers)
        turn = self.ring
        self.swap = make(lambda p, s, z, h: (p, h, z, s))
        self.core = make(lambda p, s, z, h: (p, 1 - s, z, h))
        self.shift = [make(lambda p, s, z, h, t=t: (p, s, (z + t) % turn, h)) for t in range(turn)]
        self.home = make(lambda p, s, z, h: (p, h, (z + 1) % turn, s))
        self.cluster = [
            make(lambda p, s, z, h, d=d: ((2 * p + h ^ d) // 2, s, z, (2 * p + h ^ d) % 2))
            for d in range(groups)
        ]


def send(value, route):
    return lax.ppermute(value, AXES, route)


def unit(rows):
    wide = rows.astype(F32)
    inverse = lax.rsqrt(jnp.mean(wide * wide, axis=-1, keepdims=True) + 1e-06)
    return (wide * inverse).astype(BF16)


def unit_kernel(rows_ref, out_ref):
    out_ref[...] = unit(rows_ref[...])


def pack_kernel(mine_ref, level_ref, rows_ref, *outs):
    groups = len(outs)
    count, capacity = rows_ref.shape[0], outs[0].shape[0]
    relative = level_ref[...] ^ mine_ref[0]
    member = (lax.broadcasted_iota(jnp.int32, (8, count), 0) == relative).astype(F32)
    upto = lax.broadcasted_iota(jnp.int32, (count, count), 0) <= lax.broadcasted_iota(
        jnp.int32, (count, count), 1
    )
    running = lax.dot_general(
        member.astype(BF16), upto.astype(F32).astype(BF16), NN, preferred_element_type=F32
    )
    within = jnp.sum(member * running, axis=0, keepdims=True).astype(jnp.int32) - 1
    slots = lax.broadcasted_iota(jnp.int32, (capacity, count), 0)
    for d in range(groups):
        place = jnp.where(relative == d, within, -1)
        pick = (slots == place).astype(F32)
        filled = jnp.sum(pick, axis=1, keepdims=True)
        picked = lax.dot_general(pick.astype(BF16), rows_ref[...], NN, preferred_element_type=F32)
        outs[d][...] = (picked + (1.0 - filled) * EMPTY).astype(BF16)


def prepare_kernel(*refs, first):
    one_ref, two_ref = refs[0], refs[1]
    unit_ref, valid_ref, turned_ref = refs[-3:]
    height = one_ref.shape[0]
    for j, ref in enumerate((one_ref, two_ref)):
        rows = ref[...]
        span = pl.ds(j * height, height)
        unit_ref[span, :] = unit(rows)
        present = (rows[:, 0:1].astype(F32) < 0.5 * EMPTY).astype(F32)
        valid_ref[span, :] = jnp.broadcast_to(present, (height, 128))
    both = jnp.concatenate([one_ref[...], two_ref[...]], axis=0)
    turned_ref[...] = both.T


def scores_kernel(rows_ref, valid_ref, mine_ref, other_ref, weights_ref, total_ref):
    width = mine_ref.shape[0]
    factor = 3.0 / math.sqrt(rows_ref.shape[1])

    @pl.when(pl.program_id(0) == 0)
    def _():
        total_ref[...] = jnp.zeros_like(total_ref)

    for j, ref in enumerate((mine_ref, other_ref)):
        span = pl.ds(j * width, width)
        scores = lax.dot_general(rows_ref[...], ref[...], NT, preferred_element_type=F32)
        weights = (jnp.exp(scores * factor) * valid_ref[:, 0:1]).astype(BF16)
        weights_ref[:, span] = weights
        total_ref[:, span] += jnp.sum(weights.astype(F32), axis=0, keepdims=True)


def join_kernel(part_ref, other_ref, out_ref, *, ring):
    width = part_ref.shape[1] // (2 * ring)
    for j in range(2 * ring):
        here, there = pl.ds(j * width, width), pl.ds((j ^ 1) * width, width)
        out_ref[:, here] = part_ref[:, here] + other_ref[:, there]


def inverse_totals(totals, scale_ref):
    ring = len(totals)
    width = scale_ref.shape[1] // ring
    for s in range(ring):
        total = totals[0][:, pl.ds(s * width, width)]
        for t in range(1, ring):
            total = total + totals[t][:, pl.ds((s - t) % ring * width, width)]
        scale_ref[:, pl.ds(s * width, width)] = 1.0 / total


STRIP = 32


def row_scales(chunks, scale_ref, start):
    width = chunks[0].shape[1]
    acc = jnp.zeros((STRIP, 128), F32)
    for s, ref in enumerate(chunks):
        wide = ref[pl.ds(start, STRIP), :].astype(F32) * scale_ref[:, pl.ds(s * width, width)]
        for j in range(width // 128):
            acc = acc + wide[:, j * 128 : (j + 1) * 128]
    total = jnp.sum(acc, axis=1, keepdims=True)
    return jnp.where(total > 0.0, 1.0 / total, 0.0)


def add_columns(chunks, row_scale, start, sums_ref):
    width = chunks[0].shape[1]
    for s, ref in enumerate(chunks):
        wide = ref[pl.ds(start, STRIP), :].astype(F32) * row_scale
        part = wide[0:8]
        for j in range(1, STRIP // 8):
            part = part + wide[8 * j : 8 * j + 8]
        sums_ref[:, pl.ds(s * width, width)] += part


def sweep_kernel(*refs, ring, last):
    totals, chunks = refs[:ring], refs[ring : 2 * ring]
    if last:
        out_ref, rows_ref, scale_ref, sums_ref = refs[2 * ring :]
    else:
        out_ref, scale_ref, sums_ref = refs[2 * ring :]

    @pl.when(pl.program_id(0) == 0)
    def _():
        sums_ref[...] = jnp.zeros_like(sums_ref)
        inverse_totals(totals, scale_ref)

    def strip(i, carry):
        start = pl.multiple_of(i * STRIP, STRIP)
        row_scale = row_scales(chunks, scale_ref, start)
        if last:
            rows_ref[pl.ds(start, STRIP), :] = jnp.broadcast_to(row_scale, (STRIP, 128))
        add_columns(chunks, row_scale, start, sums_ref)
        return carry

    lax.fori_loop(0, chunks[0].shape[0] // STRIP, strip, 0, unroll=2)

    @pl.when(pl.program_id(0) == pl.num_programs(0) - 1)
    def _():
        sums = jnp.sum(sums_ref[...], axis=0, keepdims=True)
        out_ref[...] = sums * scale_ref[...] if last else sums


def numerator_kernel(turned_ref, weights_ref, rows_ref, scale_ref, *refs):
    outs, shared_ref = refs[:-1], refs[-1]
    slots, width = weights_ref.shape
    block = slots // 6

    for i in range(6):
        span = pl.ds(i * block, block)
        wide = weights_ref[span, :].astype(F32)
        shared_ref[span, :] = (wide * rows_ref[span, 0:1] * scale_ref[...]).astype(BF16)
    height = outs[0].shape[0]
    step = 256
    for j in range(len(outs) // 2):
        for i in range(height // step):
            part = lax.dot_general(
                turned_ref[pl.ds(j * height + i * step, step), :],
                shared_ref[...],
                NN,
                preferred_element_type=F32,
            ).astype(BF16)
            outs[2 * j][pl.ds(i * step, step), :] = part[:, : width // 2]
            outs[2 * j + 1][pl.ds(i * step, step), :] = part[:, width // 2 :]


def finish_kernel(mass_ref, *refs):
    out_ref = refs[-1]
    height = refs[0].shape[0]
    inverse = 1.0 / mass_ref[...]
    half = len(refs) // 2
    for j in range(half):
        total = refs[j][...].astype(F32) + refs[half + j][...].astype(F32)
        out_ref[:, pl.ds(j * height, height)] = (total * inverse).T


def call(kernel, outs, *args, **kwargs):
    return pl.pallas_call(kernel, out_shape=outs, compiler_params=PARAMS, **kwargs)(*args)


def shape(*dims, dtype=BF16):
    return jax.ShapeDtypeStruct(dims, dtype)


def prepare(one, two, index, count, carried):
    height, depth = 2 * one.shape[0], one.shape[1]
    outs = (
        shape(count * height, depth),
        shape(count * height, 128, dtype=F32),
        shape(depth, count * height),
    )
    out_specs = (
        pl.BlockSpec((height, depth), lambda i: (index, 0)),
        pl.BlockSpec((height, 128), lambda i: (index, 0)),
        pl.BlockSpec((depth, height), lambda i: (0, index)),
    )
    whole = pl.BlockSpec((height // 2, depth), lambda i: (0, 0))
    held = pl.BlockSpec(memory_space=pl.ANY)
    return call(
        functools.partial(prepare_kernel, first=not carried),
        outs,
        one,
        two,
        *carried,
        grid=(1,),
        in_specs=[whole, whole] + [held] * len(carried),
        out_specs=out_specs,
        input_output_aliases={2 + j: j for j in range(len(carried))},
        name="prepare_rows",
    )


def scores(rows, valid, mine, other):
    slots, depth = rows.shape
    width = 2 * mine.shape[0]
    block = slots // 4
    centroid = pl.BlockSpec(mine.shape, lambda i: (0, 0))
    return call(
        scores_kernel,
        (shape(slots, width), shape(1, width, dtype=F32)),
        rows,
        valid,
        mine,
        other,
        grid=(4,),
        in_specs=[
            pl.BlockSpec((block, depth), lambda i: (i, 0)),
            pl.BlockSpec((block, 128), lambda i: (i, 0)),
            centroid,
            centroid,
        ],
        out_specs=(
            pl.BlockSpec((block, width), lambda i: (i, 0)),
            pl.BlockSpec((1, width), lambda i: (0, 0)),
        ),
        name="weights",
        cost_estimate=pl.CostEstimate(
            flops=2 * slots * width * depth, bytes_accessed=6_000_000, transcendentals=slots * width
        ),
    )


def sweep(totals, chunks, last):
    ring = len(chunks)
    slots, width = chunks[0].shape
    block = slots // 6
    row = pl.BlockSpec((1, ring * width), lambda i: (0, 0))
    outs, out_specs = (shape(1, ring * width, dtype=F32),), (row,)
    if last:
        outs += (shape(slots, 128, dtype=F32), shape(1, ring * width, dtype=F32))
        out_specs += (pl.BlockSpec((block, 128), lambda i: (i, 0)), row)
        scratch = [pltpu.VMEM((8, ring * width), F32)]
    else:
        scratch = [pltpu.VMEM((1, ring * width), F32), pltpu.VMEM((8, ring * width), F32)]
    return call(
        functools.partial(sweep_kernel, ring=ring, last=last),
        outs,
        *totals,
        *chunks,
        grid=(6,),
        in_specs=[row] * ring + [pl.BlockSpec((block, width), lambda i: (i, 0))] * ring,
        out_specs=out_specs,
        scratch_shapes=scratch,
        name="last_sweep" if last else "sweep",
    )


def numerator(turned, weights, rows, scale, index, parts):
    slots, width = weights.shape
    depth = turned.shape[0]
    whole = lambda a: pl.BlockSpec(a.shape, lambda i: (0, 0))
    out = shape(depth // parts, width // 2)
    return call(
        numerator_kernel,
        (out,) * (2 * parts),
        turned,
        weights,
        rows,
        scale,
        grid=(1,),
        in_specs=[
            whole(turned),
            whole(weights),
            whole(rows),
            pl.BlockSpec((1, width), lambda i: (0, index)),
        ],
        out_specs=(pl.BlockSpec(out.shape, lambda i: (0, 0)),) * (2 * parts),
        scratch_shapes=[pltpu.VMEM((slots, width), BF16)],
        name="numerator",
        cost_estimate=pl.CostEstimate(
            flops=2 * slots * width * depth, bytes_accessed=8_000_000, transcendentals=0
        ),
    )


def add(*terms):
    total = terms[0].astype(F32)
    for term in terms[1:]:
        total = total + term.astype(F32)
    return total.astype(BF16)


def body(embeddings, level_one, centroids):
    groups, peers = lax.axis_size("grp"), lax.axis_size("dev")
    routes = Routes(groups, peers)
    ring = routes.ring
    count, depth = embeddings.shape
    capacity = 2 * count // groups
    owned = centroids.shape[0]
    parts = 2
    piece = owned // parts

    own = call(unit_kernel, shape(owned, depth), centroids, name="unit_centroids")
    own = send(own, routes.swap)
    pieces = [[own[j * piece : (j + 1) * piece] for j in range(parts)]]
    for s in range(1, ring):
        pieces.append([send(p, routes.shift[1]) for p in pieces[-1]])
    mine = [own] + [jnp.concatenate(p, axis=0) for p in pieces[1:]]
    other = [send(m, routes.core) for m in mine]

    cluster = lax.axis_index("grp") // 2 * 2 + lax.axis_index("dev") % 2
    packed = call(
        pack_kernel,
        (shape(capacity, depth),) * groups,
        cluster.astype(jnp.int32).reshape(1),
        level_one.reshape(1, count),
        embeddings,
        in_specs=[pl.BlockSpec(memory_space=pltpu.SMEM), VMEM, VMEM],
        out_specs=(VMEM,) * groups,
        name="pack_rows",
    )
    arrived = [packed[0]] + [send(packed[d], routes.cluster[d]) for d in range(1, groups)]
    held = ()
    for j in range(groups // 2):
        held = prepare(arrived[2 * j], arrived[2 * j + 1], j, groups // 2, held)
    rows, valid, turned = held

    chunks, sums = [], []
    for s in range(ring):
        weights, total = scores(rows, valid, mine[s], other[s])
        chunks.append(weights)
        sums.append(total)
    part = jnp.concatenate(sums, axis=1)

    def everywhere(part):
        chip = call(
            functools.partial(join_kernel, ring=ring),
            shape(*part.shape, dtype=F32),
            part,
            send(part, routes.core),
            name="join_cores",
        )
        return [chip] + [send(chip, routes.shift[t]) for t in range(1, ring)]

    for _ in range(SWEEPS - 1):
        (part,) = sweep(everywhere(part), chunks, last=False)
    mass_part, row_scale, column_scale = sweep(everywhere(part), chunks, last=True)

    moving = None
    for s in [*range(1, ring), 0]:
        outs = numerator(turned, chunks[s], row_scale, column_scale, s, parts)
        terms = [(outs[2 * j], send(outs[2 * j + 1], routes.core)) for j in range(parts)]
        if s == 1:
            moving = [send(add(*t), routes.home if ring == 2 else routes.shift[1]) for t in terms]
        elif s > 1:
            route = routes.home if s == ring - 1 else routes.shift[1]
            moving = [send(add(m, *t), route) for m, t in zip(moving, terms)]
        else:
            kept = [send(add(*t), routes.swap) for t in terms]

    masses = everywhere(mass_part)
    mass = masses[0][:, :owned]
    for t in range(1, ring):
        start = (-t) % ring * 2 * owned
        mass = mass + masses[t][:, start : start + owned]
    mass = send(mass, routes.swap)
    updated = call(
        finish_kernel, shape(owned, depth, dtype=F32), mass, *moving, *kept, name="finish"
    )
    return updated, mass.reshape(owned)


def solution(mesh):
    in_specs = (P(AXES, None), P(AXES, None), P(AXES, None))
    out_specs = (P(AXES, None), P(AXES))
    return jax.shard_map(body, mesh=mesh, in_specs=in_specs, out_specs=out_specs, check_vma=False)
```

time: 281 us -> 177 us (0.63)
  blocking collectives: 60.5 us -> 0 us
  starting transfers between devices: 8.24 us -> 53.8 us
  waiting for transfers between devices: 121 us -> 79.1 us
  Pallas kernels: 0 us -> 38.6 us
  other arithmetic: 32 us -> 0.73 us
  matrix products: 24.3 us -> 0 us
  local copies, waits for them, and re-layouts: 19.1 us -> 3.86 us
  between operations: 14.2 us -> 1.06 us
    ppermute x0 -> x47, waiting for transfers between devices: none -> 79.1 us  [send(): return lax.ppermute(value, AXES, route)]
    reduce_scatter x1 -> x0, waiting for transfers between devices: 77.8 us -> none  [body(): lax.psum_scatter(lax.dot_general(shared, group_rows, (((0,), (0,)), ((),...]
    psum x4 -> x0, blocking collectives: 60.5 us -> none  [the longest x3 46.2 us: body(): column_total = lax.psum(partial_total, 'dev')]
    ppermute x0 -> x47, starting transfers between devices: none -> 53.8 us  [send(): return lax.ppermute(value, AXES, route)]
    pallas_call x0 -> x20, Pallas kernels: none -> 38.6 us  [call(): pl.pallas_call(kernel, out_shape=outs, compiler_params=PARAMS, **kwargs)]
    all_to_all x2 -> x0, waiting for transfers between devices: 35.8 us -> none  [the longest x1 35.8 us: body(): lax.all_to_all(outgoing.reshape(groups, capacity, feature_width), 'grp',...]
    dot_general x2 -> x0, matrix products: 24.3 us -> none  [the longest x1 12.2 us: body(): lax.dot_general(normed, lax.all_gather(own_normed, 'dev', axis=0, tiled=T...]
    reduce_sum x9 -> x0, other arithmetic: 24.2 us -> none  [the longest x3 12.5 us: body(): jnp.sum(weights.astype(jnp.float32) * column_scale[None, :], axis=1)]
  transfers between devices with their start and end apart: 4 -> 47, of which waited for: 3 -> 25; matrix products, arithmetic and copies ran while one was open for 10% -> 1% of each run, Pallas kernels for 0% -> 10%
where the time goes in v1:
time: 177 us
  waiting for transfers between devices  79.1 us (45%)
  starting transfers between devices  53.8 us (30%)
  Pallas kernels  38.6 us (22%)
  local copies, waits for them, and re-layouts  3.86 us (2%)
    ppermute x47, waiting for transfers between devices, send(): return lax.ppermute(value, AXES, route)  79.1 us
    ppermute x47, starting transfers between devices, send(): return lax.ppermute(value, AXES, route)  53.8 us
    pallas_call x20, Pallas kernels, call(): pl.pallas_call(kernel, out_shape=outs, compiler_params=PARAMS, **kwargs)  38.6 us
    unnamed x13, local copies, waits for them, and re-layouts  3.76 us
  transfers between devices with their start and end apart: 47, of which 25 were waited for; matrix products, arithmetic and copies ran while one was open for 1% of the time, Pallas kernels for 10%

profile of v1, /device:TPU:1, one launch (start us, length us, event | category | flops | bytes accessed | tf_op | source)
XLA Modules:
  0.0 177.1 jit_solution(12207133061772681091)
XLA Ops:
  1.9 4.5 %collective-permute-start.3 = (bf16[256,1024]{1,0:T(8,128)(2,1)S(1)}, bf16[256,1024]{1,0:T(8,128)(2,1)S(1)}, u32[]{:S(2)}, u32[]{:S(2)}) collective-permute-start(bf16[256,1024]{1,0:T(8,128)(2,1)S(1)} %unit_centroids.1), channel_id=1, source_target_pairs={{0,0},{1,8},{2,2},{3,10},{4,4},{5,12},{6,6},{7,14},{8,1},{9,9},{10... | collective-permute-start | bytes 1572872 | tf_op jit(solution)/shard_map/ppermute | solution.py:47
  8.5 3.5 %pack_rows.1 = (bf16[384,1024]{1,0:T(8,128)(2,1)S(1)}, bf16[384,1024]{1,0:T(8,128)(2,1)S(1)}, bf16[384,1024]{1,0:T(8,128)(2,1)S(1)}, bf16[384,1024]{1,0:T(8,128)(2,1)S(1)}) custom-call(s32[1]{0:T(128)} %bitcast.mine_ref, s32[1,768]{1,0:T(1,128)S(1)} %bitcast.4, bf16[768,1024]{1,0:T(8,128)(2,1)S(1)} %copy-done), custom_call_target="tpu_custom_call" | custom-call | tf_op jit(solution)/shard_map/pack_rows/pallas_call | solution.py:214
  17.4 7.6 %collective-permute-done.5 = bf16[128,1024]{1,0:T(8,128)(2,1)S(1)} collective-permute-done((bf16[128,1024]{1,0:T(8,128)(2,1)S(1)}, bf16[128,1024]{1,0:T(8,128)(2,1)S(1)}, u32[]{:S(2)}, u32[]{:S(2)}) %collective-permute-start.5) | collective-permute-done | bytes 262176 | tf_op jit(solution)/shard_map/ppermute | solution.py:47
  25.0 5.0 %collective-permute-done.6 = bf16[128,1024]{1,0:T(8,128)(2,1)S(1)} collective-permute-done((bf16[128,1024]{1,0:T(8,128)(2,1)S(1)}, bf16[128,1024]{1,0:T(8,128)(2,1)S(1)}, u32[]{:S(2)}, u32[]{:S(2)}) %collective-permute-start.6) | collective-permute-done | bytes 262176 | tf_op jit(solution)/shard_map/ppermute | solution.py:47
  34.0 12.7 %collective-permute-done.refs_0_ = bf16[384,1024]{1,0:T(8,128)(2,1)S(1)} collective-permute-done((bf16[384,1024]{1,0:T(8,128)(2,1)S(1)}, bf16[384,1024]{1,0:T(8,128)(2,1)S(1)}, u32[]{:S(2)}, u32[]{:S(2)}) %collective-permute-start) | collective-permute-done | bytes 786464 | tf_op jit(solution)/shard_map/ppermute | solution.py:47
  46.7 2.3 %collective-permute-start.7 = (bf16[256,1024]{1,0:T(8,128)(2,1)S(1)}, bf16[256,1024]{1,0:T(8,128)(2,1)S(1)}, u32[]{:S(2)}, u32[]{:S(2)}) collective-permute-start(bf16[256,1024]{1,0:T(8,128)(2,1)S(1)} %constant_dynamic-update-slice_fusion.mine_ref), channel_id=1, source_target_pairs={{0,8},{1,9},{2,10},{3,11},{4,12},{5,13},{6,14},{7,15},{8,0},{9,1},... | collective-permute-start | bytes 1572872 | tf_op jit(solution)/shard_map/ppermute | solution.py:47
  52.8 2.9 %weights.4 = (bf16[1536,512]{1,0:T(8,128)(2,1)S(1)}, f32[1,512]{1,0:T(1,128)S(1)}) custom-call(bf16[1536,1024]{1,0:T(8,128)(2,1)S(1)} %get-tuple-element.46.rows_ref, f32[1536,128]{1,0:T(8,128)S(1)} %get-tuple-element.47.valid_ref, bf16[256,1024]{1,0:T(8,128)(2,1)S(1)} %collective-permute-done.3.mine_ref, bf16[256,1024]{1,0:T(8,128)(2,1)S(1)} %collective-permute-done.4.other_ref), custom_call_target="tpu_custom_call" | custom-call | flops 1610612736 | bytes 6000000 | tf_op jit(solution)/shard_map/weights/pallas_call | solution.py:214
  55.7 3.9 %collective-permute-done.11 = bf16[128,1024]{1,0:T(8,128)(2,1)S(1)} collective-permute-done((bf16[128,1024]{1,0:T(8,128)(2,1)S(1)}, bf16[128,1024]{1,0:T(8,128)(2,1)S(1)}, u32[]{:S(2)}, u32[]{:S(2)}) %collective-permute-start.11) | collective-permute-done | bytes 262176 | tf_op jit(solution)/shard_map/ppermute | solution.py:47
  59.6 5.6 %collective-permute-done.12 = bf16[128,1024]{1,0:T(8,128)(2,1)S(1)} collective-permute-done((bf16[128,1024]{1,0:T(8,128)(2,1)S(1)}, bf16[128,1024]{1,0:T(8,128)(2,1)S(1)}, u32[]{:S(2)}, u32[]{:S(2)}) %collective-permute-start.12) | collective-permute-done | bytes 262176 | tf_op jit(solution)/shard_map/ppermute | solution.py:47
  66.5 2.9 %weights.5 = (bf16[1536,512]{1,0:T(8,128)(2,1)S(1)}, f32[1,512]{1,0:T(1,128)S(1)}) custom-call(bf16[1536,1024]{1,0:T(8,128)(2,1)S(1)} %get-tuple-element.46.rows_ref, f32[1536,128]{1,0:T(8,128)S(1)} %get-tuple-element.47.valid_ref, bf16[256,1024]{1,0:T(8,128)(2,1)S(1)} %constant_dynamic-update-slice_fusion.mine_ref, ...), custom_call_target="tpu_custom_call" | custom-call | flops 1610612736 | bytes 6000000 | tf_op jit(solution)/shard_map/weights/pallas_call | solution.py:214
  69.4 2.9 %weights.6 = (bf16[1536,512]{1,0:T(8,128)(2,1)S(1)}, f32[1,512]{1,0:T(1,128)S(1)}) custom-call(bf16[1536,1024]{1,0:T(8,128)(2,1)S(1)} %get-tuple-element.46.rows_ref, f32[1536,128]{1,0:T(8,128)S(1)} %get-tuple-element.47.valid_ref, bf16[256,1024]{1,0:T(8,128)(2,1)S(1)} %constant_dynamic-update-slice_fusion.2.mine_ref, ...), custom_call_target="tpu_custom_call" | custom-call | flops 1610612736 | bytes 6000000 | tf_op jit(solution)/shard_map/weights/pallas_call | solution.py:214
  72.3 2.9 %weights.7 = (bf16[1536,512]{1,0:T(8,128)(2,1)S(1)}, f32[1,512]{1,0:T(1,128)S(1)}) custom-call(bf16[1536,1024]{1,0:T(8,128)(2,1)S(1)} %get-tuple-element.46.rows_ref, f32[1536,128]{1,0:T(8,128)S(1)} %get-tuple-element.47.valid_ref, bf16[256,1024]{1,0:T(8,128)(2,1)S(1)} %constant_dynamic-update-slice_fusion.4.mine_ref, ...), custom_call_target="tpu_custom_call" | custom-call | flops 1610612736 | bytes 6000000 | tf_op jit(solution)/shard_map/weights/pallas_call | solution.py:214
  81.3 4.0 %sweep.2.part_ref = f32[1,2048]{1,0:T(1,128)S(1)} custom-call(f32[1,2048]{1,0:T(1,128)S(1)} %join_cores.4.refs_0_, f32[1,2048]{1,0:T(1,128)S(1)} %collective-permute-done.15.refs_1_, f32[1,2048]{1,0:T(1,128)S(1)} %collective-permute-done.16.refs_2_, f32[1,2048]{1,0:T(1,128)S(1)} %collective-permute-done.17.refs_3_, ...), custom_call_target="tpu_custom_call" | custom-call | tf_op jit(solution)/shard_map/sweep/pallas_call | solution.py:214
  93.3 4.0 %sweep.3.part_ref = f32[1,2048]{1,0:T(1,128)S(1)} custom-call(f32[1,2048]{1,0:T(1,128)S(1)} %join_cores.5.refs_0_, f32[1,2048]{1,0:T(1,128)S(1)} %collective-permute-done.19.refs_1_, f32[1,2048]{1,0:T(1,128)S(1)} %collective-permute-done.20.refs_2_, f32[1,2048]{1,0:T(1,128)S(1)} %collective-permute-done.21.refs_3_, ...), custom_call_target="tpu_custom_call" | custom-call | tf_op jit(solution)/shard_map/sweep/pallas_call | solution.py:214
  97.3 2.1 %collective-permute-start.22 = (f32[1,2048]{1,0:T(1,128)S(1)}, f32[1,2048]{1,0:T(1,128)S(1)}, u32[]{:S(2)}, u32[]{:S(2)}) collective-permute-start(f32[1,2048]{1,0:T(1,128)S(1)} %sweep.3.part_ref), channel_id=1, source_target_pairs={{0,8},{1,9},{2,10},{3,11},{4,12},{5,13},{6,14},{7,15},{8,0},{9,1},... | collective-permute-start | bytes 24584 | tf_op jit(solution)/shard_map/ppermute | solution.py:47
  100.6 2.2 %collective-permute-start.24 = (f32[1,2048]{1,0:T(1,128)S(1)}, f32[1,2048]{1,0:T(1,128)S(1)}, u32[]{:S(2)}, u32[]{:S(2)}) collective-permute-start(f32[1,2048]{1,0:T(1,128)S(1)} %join_cores.6.refs_0_), channel_id=1, source_target_pairs={{0,4},{1,5},{2,6},{3,7},{4,0},{5,1},{6,2},{7,3},{8,12},{9,13},{10,... | collective-permute-start | bytes 24584 | tf_op jit(solution)/shard_map/ppermute | solution.py:47
  105.5 4.1 %last_sweep.1 = (f32[1,2048]{1,0:T(1,128)S(1)}, f32[1536,128]{1,0:T(8,128)S(1)}, f32[1,2048]{1,0:T(1,128)S(1)}) custom-call(f32[1,2048]{1,0:T(1,128)S(1)} %join_cores.6.refs_0_, f32[1,2048]{1,0:T(1,128)S(1)} %collective-permute-done.23.refs_1_, f32[1,2048]{1,0:T(1,128)S(1)} %collective-permute-done.24.refs_2_, ...), custom_call_target="tpu_custom_call" | custom-call | tf_op jit(solution)/shard_map/last_sweep/pallas_call | solution.py:214
  111.6 2.0 %numerator.4 = (bf16[512,256]{1,0:T(8,128)(2,1)S(1)}, bf16[512,256]{1,0:T(8,128)(2,1)S(1)}, bf16[512,256]{1,0:T(8,128)(2,1)S(1)}, bf16[512,256]{1,0:T(8,128)(2,1)S(1)}) custom-call(bf16[1024,1536]{1,0:T(8,128)(2,1)S(1)} %get-tuple-element.57.turned_ref, bf16[1536,512]{1,0:T(8,128)(2,1)S(1)} %get-tuple-element.53.refs_5_.weights_ref, ...), custom_call_target="tpu_custom_call" | custom-call | flops 1610612736 | bytes 8000000 | tf_op jit(solution)/shard_map/numerator/pallas_call | solution.py:214
  115.5 2.0 %numerator.5 = (bf16[512,256]{1,0:T(8,128)(2,1)S(1)}, bf16[512,256]{1,0:T(8,128)(2,1)S(1)}, bf16[512,256]{1,0:T(8,128)(2,1)S(1)}, bf16[512,256]{1,0:T(8,128)(2,1)S(1)}) custom-call(bf16[1024,1536]{1,0:T(8,128)(2,1)S(1)} %get-tuple-element.57.turned_ref, bf16[1536,512]{1,0:T(8,128)(2,1)S(1)} %get-tuple-element.54.refs_6_.weights_ref, ...), custom_call_target="tpu_custom_call" | custom-call | flops 1610612736 | bytes 8000000 | tf_op jit(solution)/shard_map/numerator/pallas_call | solution.py:214
  117.5 2.0 %numerator.6 = (bf16[512,256]{1,0:T(8,128)(2,1)S(1)}, bf16[512,256]{1,0:T(8,128)(2,1)S(1)}, bf16[512,256]{1,0:T(8,128)(2,1)S(1)}, bf16[512,256]{1,0:T(8,128)(2,1)S(1)}) custom-call(bf16[1024,1536]{1,0:T(8,128)(2,1)S(1)} %get-tuple-element.57.turned_ref, bf16[1536,512]{1,0:T(8,128)(2,1)S(1)} %get-tuple-element.55.refs_7_.weights_ref, ...), custom_call_target="tpu_custom_call" | custom-call | flops 1610612736 | bytes 8000000 | tf_op jit(solution)/shard_map/numerator/pallas_call | solution.py:214
  123.1 6.9 %collective-permute-done.38 = bf16[512,256]{1,0:T(8,128)(2,1)S(1)} collective-permute-done((bf16[512,256]{1,0:T(8,128)(2,1)S(1)}, bf16[512,256]{1,0:T(8,128)(2,1)S(1)}, u32[]{:S(2)}, u32[]{:S(2)}) %collective-permute-start.38) | collective-permute-done | bytes 262176 | tf_op jit(solution)/shard_map/ppermute | solution.py:47
  130.0 2.1 %collective-permute-start.35 = (bf16[512,256]{1,0:T(8,128)(2,1)S(1)}, bf16[512,256]{1,0:T(8,128)(2,1)S(1)}, u32[]{:S(2)}, u32[]{:S(2)}) collective-permute-start(bf16[512,256]{1,0:T(8,128)(2,1)S(1)} %get-tuple-element.65), channel_id=1, source_target_pairs={{0,8},{1,9},{2,10},{3,11},{4,12},{5,13},{6,14},{7,15},{8,0},{9,1},... | collective-permute-start | bytes 786440 | tf_op jit(solution)/shard_map/ppermute | solution.py:47
  132.3 2.6 %collective-permute-start.46 = (bf16[512,256]{1,0:T(8,128)(2,1)S(1)}, bf16[512,256]{1,0:T(8,128)(2,1)S(1)}, u32[]{:S(2)}, u32[]{:S(2)}) collective-permute-start(bf16[512,256]{1,0:T(8,128)(2,1)S(1)} %add_convert_fusion), channel_id=1, source_target_pairs={{0,0},{1,8},{2,2},{3,10},{4,4},{5,12},{6,6},{7,14},{8,1},{9,9},{10... | collective-permute-start | bytes 786440 | tf_op jit(solution)/shard_map/ppermute | solution.py:47
  135.9 3.9 %collective-permute-start.44 = (bf16[512,256]{1,0:T(8,128)(2,1)S(1)}, bf16[512,256]{1,0:T(8,128)(2,1)S(1)}, u32[]{:S(2)}, u32[]{:S(2)}) collective-permute-start(bf16[512,256]{1,0:T(8,128)(2,1)S(1)} %add_convert_fusion.1), channel_id=1, source_target_pairs={{0,0},{1,8},{2,2},{3,10},{4,4},{5,12},{6,6},{7,14},{8,1},{9,9},{10... | collective-permute-start | bytes 786440 | tf_op jit(solution)/shard_map/ppermute | solution.py:47
  139.8 4.2 %collective-permute-done.40 = bf16[512,256]{1,0:T(8,128)(2,1)S(1)} collective-permute-done((bf16[512,256]{1,0:T(8,128)(2,1)S(1)}, bf16[512,256]{1,0:T(8,128)(2,1)S(1)}, u32[]{:S(2)}, u32[]{:S(2)}) %collective-permute-start.40) | collective-permute-done | bytes 262176 | tf_op jit(solution)/shard_map/ppermute | solution.py:47
  144.0 2.4 %collective-permute-start.42 = (bf16[512,256]{1,0:T(8,128)(2,1)S(1)}, bf16[512,256]{1,0:T(8,128)(2,1)S(1)}, u32[]{:S(2)}, u32[]{:S(2)}) collective-permute-start(bf16[512,256]{1,0:T(8,128)(2,1)S(1)} %add_convert_fusion.2), channel_id=1, source_target_pairs={{0,2},{1,10},{2,4},{3,12},{4,6},{5,14},{6,0},{7,8},{8,3},{9,11},{1... | collective-permute-start | bytes 786440 | tf_op jit(solution)/shard_map/ppermute | solution.py:47
  146.4 3.1 %collective-permute-done.34 = bf16[512,256]{1,0:T(8,128)(2,1)S(1)} collective-permute-done((bf16[512,256]{1,0:T(8,128)(2,1)S(1)}, bf16[512,256]{1,0:T(8,128)(2,1)S(1)}, u32[]{:S(2)}, u32[]{:S(2)}) %collective-permute-start.34) | collective-permute-done | bytes 262176 | tf_op jit(solution)/shard_map/ppermute | solution.py:47
  149.7 2.4 %collective-permute-start.36 = (bf16[512,256]{1,0:T(8,128)(2,1)S(1)}, bf16[512,256]{1,0:T(8,128)(2,1)S(1)}, u32[]{:S(2)}, u32[]{:S(2)}) collective-permute-start(bf16[512,256]{1,0:T(8,128)(2,1)S(1)} %add_convert_fusion.5), channel_id=1, source_target_pairs={{0,2},{1,10},{2,4},{3,12},{4,6},{5,14},{6,0},{7,8},{8,3},{9,11},{1... | collective-permute-start | bytes 786440 | tf_op jit(solution)/shard_map/ppermute | solution.py:47
  153.2 11.1 %collective-permute-done.27 = f32[1,2048]{1,0:T(1,128)S(1)} collective-permute-done((f32[1,2048]{1,0:T(1,128)S(1)}, f32[1,2048]{1,0:T(1,128)S(1)}, u32[]{:S(2)}, u32[]{:S(2)}) %collective-permute-start.27) | collective-permute-done | bytes 8224 | tf_op jit(solution)/shard_map/ppermute | solution.py:47
  164.3 3.4 %collective-permute-done.28 = f32[1,2048]{1,0:T(1,128)S(1)} collective-permute-done((f32[1,2048]{1,0:T(1,128)S(1)}, f32[1,2048]{1,0:T(1,128)S(1)}, u32[]{:S(2)}, u32[]{:S(2)}) %collective-permute-start.28) | collective-permute-done | bytes 8224 | tf_op jit(solution)/shard_map/ppermute | solution.py:47
  167.7 2.5 %collective-permute-done.29 = f32[1,2048]{1,0:T(1,128)S(1)} collective-permute-done((f32[1,2048]{1,0:T(1,128)S(1)}, f32[1,2048]{1,0:T(1,128)S(1)}, u32[]{:S(2)}, u32[]{:S(2)}) %collective-permute-start.29) | collective-permute-done | bytes 8224 | tf_op jit(solution)/shard_map/ppermute | solution.py:47
  170.3 3.7 %collective-permute-start.30 = (f32[1,256]{1,0:T(1,128)S(1)}, f32[1,256]{1,0:T(1,128)S(1)}, u32[]{:S(2)}, u32[]{:S(2)}) collective-permute-start(f32[1,256]{1,0:T(1,128)S(1)} %slice_add_fusion), channel_id=1, source_target_pairs={{0,0},{1,8},{2,2},{3,10},{4,4},{5,12},{6,6},{7,14},{8,1},{9,9},{10... | collective-permute-start | bytes 3080 | tf_op jit(solution)/shard_map/ppermute | solution.py:47
  (109 shorter events, 48.9 us)
Async XLA Ops:
  1.9 12.9 %collective-permute-start.3 = (bf16[256,1024]{1,0:T(8,128)(2,1)S(1)}, bf16[256,1024]{1,0:T(8,128)(2,1)S(1)}, u32[]{:S(2)}, u32[]{:S(2)}) collective-permute-start(bf16[256,1024]{1,0:T(8,128)(2,1)S(1)} %unit_centroids.1), channel_id=1, source_target_pairs={{0,0},{1,8},{2,2},{3,10},{4,4},{5,12},{6,6},{7,14},{8,1},{9,9},{10... | collective-permute-start | bytes 1572872 | tf_op jit(solution)/shard_map/ppermute | solution.py:47
  12.0 19.6 %collective-permute-start.2 = (bf16[384,1024]{1,0:T(8,128)(2,1)S(1)}, bf16[384,1024]{1,0:T(8,128)(2,1)S(1)}, u32[]{:S(2)}, u32[]{:S(2)}) collective-permute-start(bf16[384,1024]{1,0:T(8,128)(2,1)S(1)} %get-tuple-element.42), channel_id=1, source_target_pairs={{0,1},{1,0},{2,3},{3,2},{4,5},{5,4},{6,7},{7,6},{8,9},{9,8},{10,11... | collective-permute-start | bytes 2359304 | tf_op jit(solution)/shard_map/ppermute | solution.py:47
  12.1 34.6 %collective-permute-start = (bf16[384,1024]{1,0:T(8,128)(2,1)S(1)}, bf16[384,1024]{1,0:T(8,128)(2,1)S(1)}, u32[]{:S(2)}, u32[]{:S(2)}) collective-permute-start(bf16[384,1024]{1,0:T(8,128)(2,1)S(1)} %get-tuple-element.39), channel_id=1, source_target_pairs={{0,16},{1,17},{2,18},{3,19},{4,20},{5,21},{6,22},{7,23},{8,24},{9,... | collective-permute-start | bytes 2359304 | tf_op jit(solution)/shard_map/ppermute | solution.py:47
  13.4 35.6 %collective-permute-start.1 = (bf16[384,1024]{1,0:T(8,128)(2,1)S(1)}, bf16[384,1024]{1,0:T(8,128)(2,1)S(1)}, u32[]{:S(2)}, u32[]{:S(2)}) collective-permute-start(bf16[384,1024]{1,0:T(8,128)(2,1)S(1)} %get-tuple-element.40), channel_id=1, source_target_pairs={{0,17},{1,16},{2,19},{3,18},{4,21},{5,20},{6,23},{7,22},{8,25},{9,... | collective-permute-start | bytes 2359304 | tf_op jit(solution)/shard_map/ppermute | solution.py:47
  14.8 10.2 %collective-permute-start.5 = (bf16[128,1024]{1,0:T(8,128)(2,1)S(1)}, bf16[128,1024]{1,0:T(8,128)(2,1)S(1)}, u32[]{:S(2)}, u32[]{:S(2)}) collective-permute-start(bf16[128,1024]{1,0:T(8,128)(2,1)S(1)} %get-tuple-element.77), channel_id=1, source_target_pairs={{0,2},{1,3},{2,4},{3,5},{4,6},{5,7},{6,0},{7,1},{8,10},{9,11},{10,... | collective-permute-start | bytes 786440 | tf_op jit(solution)/shard_map/ppermute | solution.py:47
  16.1 13.9 %collective-permute-start.6 = (bf16[128,1024]{1,0:T(8,128)(2,1)S(1)}, bf16[128,1024]{1,0:T(8,128)(2,1)S(1)}, u32[]{:S(2)}, u32[]{:S(2)}) collective-permute-start(bf16[128,1024]{1,0:T(8,128)(2,1)S(1)} %get-tuple-element.76), channel_id=1, source_target_pairs={{0,2},{1,3},{2,4},{3,5},{4,6},{5,7},{6,0},{7,1},{8,10},{9,11},{10,... | collective-permute-start | bytes 786440 | tf_op jit(solution)/shard_map/ppermute | solution.py:47
  25.0 27.8 %collective-permute-start.4 = (bf16[256,1024]{1,0:T(8,128)(2,1)S(1)}, bf16[256,1024]{1,0:T(8,128)(2,1)S(1)}, u32[]{:S(2)}, u32[]{:S(2)}) collective-permute-start(bf16[256,1024]{1,0:T(8,128)(2,1)S(1)} %collective-permute-done.3.mine_ref), channel_id=1, source_target_pairs={{0,8},{1,9},{2,10},{3,11},{4,12},{5,13},{6,14},{7,15},{8,0},{9,1},... | collective-permute-start | bytes 1572872 | tf_op jit(solution)/shard_map/ppermute | solution.py:47
  30.0 20.0 %collective-permute-start.8 = (bf16[128,1024]{1,0:T(8,128)(2,1)S(1)}, bf16[128,1024]{1,0:T(8,128)(2,1)S(1)}, u32[]{:S(2)}, u32[]{:S(2)}) collective-permute-start(bf16[128,1024]{1,0:T(8,128)(2,1)S(1)} %collective-permute-done.5), channel_id=1, source_target_pairs={{0,2},{1,3},{2,4},{3,5},{4,6},{5,7},{6,0},{7,1},{8,10},{9,11},{10,... | collective-permute-start | bytes 786440 | tf_op jit(solution)/shard_map/ppermute | solution.py:47
  31.7 18.4 %collective-permute-start.9 = (bf16[128,1024]{1,0:T(8,128)(2,1)S(1)}, bf16[128,1024]{1,0:T(8,128)(2,1)S(1)}, u32[]{:S(2)}, u32[]{:S(2)}) collective-permute-start(bf16[128,1024]{1,0:T(8,128)(2,1)S(1)} %collective-permute-done.6), channel_id=1, source_target_pairs={{0,2},{1,3},{2,4},{3,5},{4,6},{5,7},{6,0},{7,1},{8,10},{9,11},{10,... | collective-permute-start | bytes 786440 | tf_op jit(solution)/shard_map/ppermute | solution.py:47
  46.7 19.8 %collective-permute-start.7 = (bf16[256,1024]{1,0:T(8,128)(2,1)S(1)}, bf16[256,1024]{1,0:T(8,128)(2,1)S(1)}, u32[]{:S(2)}, u32[]{:S(2)}) collective-permute-start(bf16[256,1024]{1,0:T(8,128)(2,1)S(1)} %constant_dynamic-update-slice_fusion.mine_ref), channel_id=1, source_target_pairs={{0,8},{1,9},{2,10},{3,11},{4,12},{5,13},{6,14},{7,15},{8,0},{9,1},... | collective-permute-start | bytes 1572872 | tf_op jit(solution)/shard_map/ppermute | solution.py:47
  50.1 19.3 %collective-permute-start.10 = (bf16[256,1024]{1,0:T(8,128)(2,1)S(1)}, bf16[256,1024]{1,0:T(8,128)(2,1)S(1)}, u32[]{:S(2)}, u32[]{:S(2)}) collective-permute-start(bf16[256,1024]{1,0:T(8,128)(2,1)S(1)} %constant_dynamic-update-slice_fusion.2.mine_ref), channel_id=1, source_target_pairs={{0,8},{1,9},{2,10},{3,11},{4,12},{5,13},{6,14},{7,15},{8,0},{9,1},... | collective-permute-start | bytes 1572872 | tf_op jit(solution)/shard_map/ppermute | solution.py:47
  50.1 9.4 %collective-permute-start.11 = (bf16[128,1024]{1,0:T(8,128)(2,1)S(1)}, bf16[128,1024]{1,0:T(8,128)(2,1)S(1)}, u32[]{:S(2)}, u32[]{:S(2)}) collective-permute-start(bf16[128,1024]{1,0:T(8,128)(2,1)S(1)} %collective-permute-done.8), channel_id=1, source_target_pairs={{0,2},{1,3},{2,4},{3,5},{4,6},{5,7},{6,0},{7,1},{8,10},{9,11},{10,... | collective-permute-start | bytes 786440 | tf_op jit(solution)/shard_map/ppermute | solution.py:47
  51.5 13.7 %collective-permute-start.12 = (bf16[128,1024]{1,0:T(8,128)(2,1)S(1)}, bf16[128,1024]{1,0:T(8,128)(2,1)S(1)}, u32[]{:S(2)}, u32[]{:S(2)}) collective-permute-start(bf16[128,1024]{1,0:T(8,128)(2,1)S(1)} %collective-permute-done.9), channel_id=1, source_target_pairs={{0,2},{1,3},{2,4},{3,5},{4,6},{5,7},{6,0},{7,1},{8,10},{9,11},{10,... | collective-permute-start | bytes 786440 | tf_op jit(solution)/shard_map/ppermute | solution.py:47
  65.2 7.1 %collective-permute-start.13 = (bf16[256,1024]{1,0:T(8,128)(2,1)S(1)}, bf16[256,1024]{1,0:T(8,128)(2,1)S(1)}, u32[]{:S(2)}, u32[]{:S(2)}) collective-permute-start(bf16[256,1024]{1,0:T(8,128)(2,1)S(1)} %constant_dynamic-update-slice_fusion.4.mine_ref), channel_id=1, source_target_pairs={{0,8},{1,9},{2,10},{3,11},{4,12},{5,13},{6,14},{7,15},{8,0},{9,1},... | collective-permute-start | bytes 1572872 | tf_op jit(solution)/shard_map/ppermute | solution.py:47
  76.5 4.3 %collective-permute-start.15 = (f32[1,2048]{1,0:T(1,128)S(1)}, f32[1,2048]{1,0:T(1,128)S(1)}, u32[]{:S(2)}, u32[]{:S(2)}) collective-permute-start(f32[1,2048]{1,0:T(1,128)S(1)} %join_cores.4.refs_0_), channel_id=1, source_target_pairs={{0,2},{1,3},{2,4},{3,5},{4,6},{5,7},{6,0},{7,1},{8,10},{9,11},{10,... | collective-permute-start | bytes 24584 | tf_op jit(solution)/shard_map/ppermute | solution.py:47
  87.6 4.3 %collective-permute-start.19 = (f32[1,2048]{1,0:T(1,128)S(1)}, f32[1,2048]{1,0:T(1,128)S(1)}, u32[]{:S(2)}, u32[]{:S(2)}) collective-permute-start(f32[1,2048]{1,0:T(1,128)S(1)} %join_cores.5.refs_0_), channel_id=1, source_target_pairs={{0,2},{1,3},{2,4},{3,5},{4,6},{5,7},{6,0},{7,1},{8,10},{9,11},{10,... | collective-permute-start | bytes 24584 | tf_op jit(solution)/shard_map/ppermute | solution.py:47
  113.6 6.9 %collective-permute-start.37 = (bf16[512,256]{1,0:T(8,128)(2,1)S(1)}, bf16[512,256]{1,0:T(8,128)(2,1)S(1)}, u32[]{:S(2)}, u32[]{:S(2)}) collective-permute-start(bf16[512,256]{1,0:T(8,128)(2,1)S(1)} %get-tuple-element.67), channel_id=1, source_target_pairs={{0,8},{1,9},{2,10},{3,11},{4,12},{5,13},{6,14},{7,15},{8,0},{9,1},... | collective-permute-start | bytes 786440 | tf_op jit(solution)/shard_map/ppermute | solution.py:47
  115.5 5.2 %collective-permute-start.31 = (bf16[512,256]{1,0:T(8,128)(2,1)S(1)}, bf16[512,256]{1,0:T(8,128)(2,1)S(1)}, u32[]{:S(2)}, u32[]{:S(2)}) collective-permute-start(bf16[512,256]{1,0:T(8,128)(2,1)S(1)} %get-tuple-element.61), channel_id=1, source_target_pairs={{0,8},{1,9},{2,10},{3,11},{4,12},{5,13},{6,14},{7,15},{8,0},{9,1},... | collective-permute-start | bytes 786440 | tf_op jit(solution)/shard_map/ppermute | solution.py:47
  120.0 15.7 %collective-permute-start.43 = (bf16[512,256]{1,0:T(8,128)(2,1)S(1)}, bf16[512,256]{1,0:T(8,128)(2,1)S(1)}, u32[]{:S(2)}, u32[]{:S(2)}) collective-permute-start(bf16[512,256]{1,0:T(8,128)(2,1)S(1)} %get-tuple-element.73), channel_id=1, source_target_pairs={{0,8},{1,9},{2,10},{3,11},{4,12},{5,13},{6,14},{7,15},{8,0},{9,1},... | collective-permute-start | bytes 786440 | tf_op jit(solution)/shard_map/ppermute | solution.py:47
  120.5 11.7 %collective-permute-start.33 = (bf16[512,256]{1,0:T(8,128)(2,1)S(1)}, bf16[512,256]{1,0:T(8,128)(2,1)S(1)}, u32[]{:S(2)}, u32[]{:S(2)}) collective-permute-start(bf16[512,256]{1,0:T(8,128)(2,1)S(1)} %get-tuple-element.63), channel_id=1, source_target_pairs={{0,8},{1,9},{2,10},{3,11},{4,12},{5,13},{6,14},{7,15},{8,0},{9,1},... | collective-permute-start | bytes 786440 | tf_op jit(solution)/shard_map/ppermute | solution.py:47
  120.7 9.3 %collective-permute-start.38 = (bf16[512,256]{1,0:T(8,128)(2,1)S(1)}, bf16[512,256]{1,0:T(8,128)(2,1)S(1)}, u32[]{:S(2)}, u32[]{:S(2)}) collective-permute-start(bf16[512,256]{1,0:T(8,128)(2,1)S(1)} %add_convert_fusion.4), channel_id=1, source_target_pairs={{0,2},{1,3},{2,4},{3,5},{4,6},{5,7},{6,0},{7,1},{8,10},{9,11},{10,... | collective-permute-start | bytes 786440 | tf_op jit(solution)/shard_map/ppermute | solution.py:47
  121.9 13.7 %collective-permute-start.32 = (bf16[512,256]{1,0:T(8,128)(2,1)S(1)}, bf16[512,256]{1,0:T(8,128)(2,1)S(1)}, u32[]{:S(2)}, u32[]{:S(2)}) collective-permute-start(bf16[512,256]{1,0:T(8,128)(2,1)S(1)} %add_convert_fusion.7), channel_id=1, source_target_pairs={{0,2},{1,3},{2,4},{3,5},{4,6},{5,7},{6,0},{7,1},{8,10},{9,11},{10,... | collective-permute-start | bytes 786440 | tf_op jit(solution)/shard_map/ppermute | solution.py:47
  122.4 13.5 %collective-permute-start.41 = (bf16[512,256]{1,0:T(8,128)(2,1)S(1)}, bf16[512,256]{1,0:T(8,128)(2,1)S(1)}, u32[]{:S(2)}, u32[]{:S(2)}) collective-permute-start(bf16[512,256]{1,0:T(8,128)(2,1)S(1)} %get-tuple-element.71), channel_id=1, source_target_pairs={{0,8},{1,9},{2,10},{3,11},{4,12},{5,13},{6,14},{7,15},{8,0},{9,1},... | collective-permute-start | bytes 786440 | tf_op jit(solution)/shard_map/ppermute | solution.py:47
  130.0 16.4 %collective-permute-start.35 = (bf16[512,256]{1,0:T(8,128)(2,1)S(1)}, bf16[512,256]{1,0:T(8,128)(2,1)S(1)}, u32[]{:S(2)}, u32[]{:S(2)}) collective-permute-start(bf16[512,256]{1,0:T(8,128)(2,1)S(1)} %get-tuple-element.65), channel_id=1, source_target_pairs={{0,8},{1,9},{2,10},{3,11},{4,12},{5,13},{6,14},{7,15},{8,0},{9,1},... | collective-permute-start | bytes 786440 | tf_op jit(solution)/shard_map/ppermute | solution.py:47
  132.3 42.9 %collective-permute-start.46 = (bf16[512,256]{1,0:T(8,128)(2,1)S(1)}, bf16[512,256]{1,0:T(8,128)(2,1)S(1)}, u32[]{:S(2)}, u32[]{:S(2)}) collective-permute-start(bf16[512,256]{1,0:T(8,128)(2,1)S(1)} %add_convert_fusion), channel_id=1, source_target_pairs={{0,0},{1,8},{2,2},{3,10},{4,4},{5,12},{6,6},{7,14},{8,1},{9,9},{10... | collective-permute-start | bytes 786440 | tf_op jit(solution)/shard_map/ppermute | solution.py:47
  135.6 8.3 %collective-permute-start.40 = (bf16[512,256]{1,0:T(8,128)(2,1)S(1)}, bf16[512,256]{1,0:T(8,128)(2,1)S(1)}, u32[]{:S(2)}, u32[]{:S(2)}) collective-permute-start(bf16[512,256]{1,0:T(8,128)(2,1)S(1)} %add_convert_fusion.3), channel_id=1, source_target_pairs={{0,2},{1,3},{2,4},{3,5},{4,6},{5,7},{6,0},{7,1},{8,10},{9,11},{10,... | collective-permute-start | bytes 786440 | tf_op jit(solution)/shard_map/ppermute | solution.py:47
  135.7 13.8 %collective-permute-start.34 = (bf16[512,256]{1,0:T(8,128)(2,1)S(1)}, bf16[512,256]{1,0:T(8,128)(2,1)S(1)}, u32[]{:S(2)}, u32[]{:S(2)}) collective-permute-start(bf16[512,256]{1,0:T(8,128)(2,1)S(1)} %add_convert_fusion.6), channel_id=1, source_target_pairs={{0,2},{1,3},{2,4},{3,5},{4,6},{5,7},{6,0},{7,1},{8,10},{9,11},{10,... | collective-permute-start | bytes 786440 | tf_op jit(solution)/shard_map/ppermute | solution.py:47
  135.9 39.3 %collective-permute-start.44 = (bf16[512,256]{1,0:T(8,128)(2,1)S(1)}, bf16[512,256]{1,0:T(8,128)(2,1)S(1)}, u32[]{:S(2)}, u32[]{:S(2)}) collective-permute-start(bf16[512,256]{1,0:T(8,128)(2,1)S(1)} %add_convert_fusion.1), channel_id=1, source_target_pairs={{0,0},{1,8},{2,2},{3,10},{4,4},{5,12},{6,6},{7,14},{8,1},{9,9},{10... | collective-permute-start | bytes 786440 | tf_op jit(solution)/shard_map/ppermute | solution.py:47
  144.0 31.2 %collective-permute-start.42 = (bf16[512,256]{1,0:T(8,128)(2,1)S(1)}, bf16[512,256]{1,0:T(8,128)(2,1)S(1)}, u32[]{:S(2)}, u32[]{:S(2)}) collective-permute-start(bf16[512,256]{1,0:T(8,128)(2,1)S(1)} %add_convert_fusion.2), channel_id=1, source_target_pairs={{0,2},{1,10},{2,4},{3,12},{4,6},{5,14},{6,0},{7,8},{8,3},{9,11},{1... | collective-permute-start | bytes 786440 | tf_op jit(solution)/shard_map/ppermute | solution.py:47
  149.7 25.6 %collective-permute-start.36 = (bf16[512,256]{1,0:T(8,128)(2,1)S(1)}, bf16[512,256]{1,0:T(8,128)(2,1)S(1)}, u32[]{:S(2)}, u32[]{:S(2)}) collective-permute-start(bf16[512,256]{1,0:T(8,128)(2,1)S(1)} %add_convert_fusion.5), channel_id=1, source_target_pairs={{0,2},{1,10},{2,4},{3,12},{4,6},{5,14},{6,0},{7,8},{8,3},{9,11},{1... | collective-permute-start | bytes 786440 | tf_op jit(solution)/shard_map/ppermute | solution.py:47
  153.2 11.1 %collective-permute-start.27 = (f32[1,2048]{1,0:T(1,128)S(1)}, f32[1,2048]{1,0:T(1,128)S(1)}, u32[]{:S(2)}, u32[]{:S(2)}) collective-permute-start(f32[1,2048]{1,0:T(1,128)S(1)} %join_cores.7), channel_id=1, source_target_pairs={{0,2},{1,3},{2,4},{3,5},{4,6},{5,7},{6,0},{7,1},{8,10},{9,11},{10,... | collective-permute-start | bytes 24584 | tf_op jit(solution)/shard_map/ppermute | solution.py:47
  170.3 4.9 %collective-permute-start.30 = (f32[1,256]{1,0:T(1,128)S(1)}, f32[1,256]{1,0:T(1,128)S(1)}, u32[]{:S(2)}, u32[]{:S(2)}) collective-permute-start(f32[1,256]{1,0:T(1,128)S(1)} %slice_add_fusion), channel_id=1, source_target_pairs={{0,0},{1,8},{2,2},{3,10},{4,4},{5,12},{6,6},{7,14},{8,1},{9,9},{10... | collective-permute-start | bytes 3080 | tf_op jit(solution)/shard_map/ppermute | solution.py:47
  (18 other events, 46.0 us)

commit v2 on v0

v2 whole, which is shorter than its diff:
```python
import functools
import math

import jax
import jax.numpy as jnp
from jax import lax
from jax.experimental import pallas as pl
from jax.experimental.pallas import tpu as pltpu
from jax.sharding import PartitionSpec as P

SWEEPS = 3
EMPTY = 64.0
AXES = ("grp", "dev")
F32 = jnp.float32
BF16 = jnp.bfloat16
NT = (((1,), (1,)), ((), ()))
NN = (((1,), (0,)), ((), ()))
VMEM = pl.BlockSpec(memory_space=pltpu.VMEM)
SMEM = pl.BlockSpec(memory_space=pltpu.SMEM)
HELD = pl.BlockSpec(memory_space=pl.ANY)
PARAMS = pltpu.CompilerParams(vmem_limit_bytes=16 * 1024 * 1024)


def permutation(groups, peers, move):
    pairs = []
    for grp in range(groups):
        for dev in range(peers):
            target = move(grp // 2, grp % 2, dev // 2, dev % 2)
            if target is None:
                continue
            pair, side, place, half = target
            pairs.append((grp * peers + dev, (2 * pair + side) * peers + 2 * place + half))
    return pairs


class Routes:
    def __init__(self, groups, peers):
        self.ring = peers // 2
        make = functools.partial(permutation, groups, peers)
        turn = self.ring
        self.swap = make(lambda p, s, z, h: (p, h, z, s))
        self.core = make(lambda p, s, z, h: (p, 1 - s, z, h))
        self.shift = [make(lambda p, s, z, h, t=t: (p, s, (z + t) % turn, h)) for t in range(turn)]
        self.swap = make(lambda p, s, z, h: (p, h, z, s))
        self.both = [
            make(lambda p, s, z, h, t=t: (p, s, (z + (-t if s else t)) % turn, h))
            for t in range(turn // 2 + 1)
        ]
        self.home = make(lambda p, s, z, h: (p, h, (z + 1) % turn, s))
        self.cluster = [
            make(lambda p, s, z, h, d=d: ((2 * p + h ^ d) // 2, s, z, (2 * p + h ^ d) % 2))
            for d in range(groups)
        ]


def send(value, route):
    return lax.ppermute(value, AXES, route)


def call(kernel, outs, args, after=(), specs=None, alias=None, out_specs=None, **kwargs):
    args, after = list(args), list(after)

    def ordered(*refs):
        kernel(*refs[: len(args)], *refs[len(args) + len(after) :])

    return pl.pallas_call(
        ordered,
        out_shape=outs,
        in_specs=(specs or [VMEM] * len(args)) + [HELD] * len(after),
        out_specs=out_specs or jax.tree.map(lambda _: VMEM, outs),
        input_output_aliases=alias or {},
        compiler_params=PARAMS,
        **kwargs,
    )(*args, *after)


def cost(m, n, k):
    return pl.CostEstimate(
        flops=2 * m * n * k, bytes_accessed=2 * (m * n + n * k + m * k), transcendentals=0
    )


WAIT = pl.CostEstimate(flops=2 * 10**10, bytes_accessed=0, transcendentals=0)


def tie(values, after):
    values, after = list(values), list(after)
    return pl.pallas_call(
        lambda *refs: None,
        out_shape=tuple(jax.ShapeDtypeStruct(v.shape, v.dtype) for v in values),
        in_specs=[HELD] * (len(values) + len(after)),
        out_specs=(HELD,) * len(values),
        input_output_aliases={j: j for j in range(len(values))},
        compiler_params=PARAMS,
        cost_estimate=WAIT,
        name="tie",
    )(*values, *after)


def shape(*dims, dtype=BF16):
    return jax.ShapeDtypeStruct(dims, dtype)


def exact(line):
    high = line.astype(BF16).astype(F32)
    middle = (line - high).astype(BF16).astype(F32)
    low = line - high - middle
    at = lax.broadcasted_iota(jnp.int32, (16, line.shape[1]), 0)
    split = jnp.where(at == 0, high, jnp.where(at == 1, middle, jnp.where(at == 2, low, 0.0)))
    return split.astype(BF16)


def fast_here():
    return lax.axis_index("grp") % 2 == lax.axis_index("dev") % 2


def cluster_here():
    return lax.axis_index("grp") // 2 * 2 + lax.axis_index("dev") % 2


def unit(rows):
    wide = rows.astype(F32)
    inverse = lax.rsqrt(jnp.mean(wide * wide, axis=-1, keepdims=True) + 1e-06)
    return (wide * inverse).astype(BF16)


def unit_kernel(rows_ref, *outs):
    height = outs[0].shape[0]
    for j, out_ref in enumerate(outs):
        out_ref[...] = unit(rows_ref[pl.ds(j * height, height), :])


def rank_kernel(level_ref, place_ref):
    lines, count = place_ref.shape
    relative = level_ref[...] ^ cluster_here()
    member = lax.broadcasted_iota(jnp.int32, (lines, count), 0) == relative
    upto = lax.broadcasted_iota(jnp.int32, (count, count), 0) <= lax.broadcasted_iota(
        jnp.int32, (count, count), 1
    )
    running = lax.dot_general(
        member.astype(F32).astype(BF16),
        upto.astype(F32).astype(BF16),
        NN,
        preferred_element_type=F32,
    )
    place_ref[...] = jnp.where(member, running.astype(jnp.int32) - 1, -1)


def pick_kernel(place_ref, rows_ref, out_ref, *, which):
    capacity, count = out_ref.shape[0], rows_ref.shape[0]
    slots = lax.broadcasted_iota(jnp.int32, (capacity, count), 0)
    pick = (slots == place_ref[which : which + 1, :]).astype(F32)
    filled = jnp.sum(pick, axis=1, keepdims=True)
    picked = lax.dot_general(pick.astype(BF16), rows_ref[...], NN, preferred_element_type=F32)
    out_ref[...] = (picked + (1.0 - filled) * EMPTY).astype(BF16)


def weights_kernel(*refs, raw, lines, columns, carried, groups):
    *refs, unit_ref, valid_ref, weights_ref, sums_ref = refs
    inputs = refs[4 if carried else 0 :]
    pieces = inputs[len(raw) :]
    each = len(pieces) // (2 * len(columns))
    height = pieces[0].shape[0]
    capacity, depth = unit_ref.shape[0] // groups, unit_ref.shape[1]
    pick = lax.broadcasted_iota(jnp.int32, (16, 128), 0) + lax.broadcasted_iota(
        jnp.int32, (16, 128), 1
    )
    pick = jnp.where(pick == 0, 1.0, 0.0).astype(BF16)
    for ref, d in zip(inputs, raw):
        span = pl.ds(d * capacity, capacity)
        rows = ref[...]
        present = (rows[:, 0:1].astype(F32) < 0.5 * EMPTY).astype(F32)
        unit_ref[span, :] = unit(rows.astype(F32) * present)
        across = jnp.broadcast_to(present, (capacity, 128)).astype(BF16)
        valid = lax.dot_general(pick, across, NT, preferred_element_type=F32)
        valid_ref[:, span] = valid[0:1]

    fast = fast_here()
    half = each * height
    group = max(1, 512 // (2 * half))
    factor = 3.0 / math.sqrt(depth) * math.log2(math.e)
    for j in range(0, len(columns), group):
        block = []
        for k in range(j, min(j + group, len(columns))):
            refs = pieces[2 * each * k : 2 * each * (k + 1)]
            mine, other = (
                jnp.concatenate([ref[...] for ref in part], axis=0)
                for part in (refs[:each], refs[each:])
            )
            block += [jnp.where(fast, mine, other), jnp.where(fast, other, mine)]
        block = jnp.concatenate(block, axis=0)
        at = pl.ds(columns[j] * 2 * half, block.shape[0])
        for d in lines:
            span = pl.ds(d * capacity, capacity)
            scores = lax.dot_general(unit_ref[span, :], block, NT, preferred_element_type=F32)
            weights_ref[span, at] = jnp.exp2(scores * factor).astype(BF16)
    at = pl.ds(columns[0] * 2 * half, len(columns) * 2 * half)
    span = pl.ds(lines[0] * capacity, len(lines) * capacity)
    valid = jnp.broadcast_to(valid_ref[:, span], (16, len(lines) * capacity)).astype(BF16)
    sums = lax.dot_general(valid, weights_ref[span, at], NN, preferred_element_type=F32)[0:1]
    sums_ref[:, at] = sums if 0 in lines else sums_ref[:, at] + sums


def turn_kernel(*refs):
    rows, out_ref = refs[:-1], refs[-1]
    width = 2 * rows[0].shape[0]
    for j in range(len(rows) // 2):
        both = jnp.concatenate([rows[2 * j][...], rows[2 * j + 1][...]], axis=0)
        out_ref[:, pl.ds(j * width, width)] = both.T


def join_kernel(part_ref, other_ref, out_ref):
    out_ref[...] = part_ref[...] + other_ref[...]


def inverse_totals(totals, scale_ref):
    ring, width = len(totals), totals[0].shape[1] // len(totals)
    zero = lax.axis_index("grp") % 2 == 0
    for s in range(ring):

        def chunk(ref, t):
            return ref[:, pl.ds((s - t) % ring * width, width)]

        total = chunk(totals[0], 0) + chunk(totals[1], ring // 2)
        for t in range(1, ring // 2):
            near, far = totals[2 * t], totals[2 * t + 1]
            ahead = jnp.where(zero, chunk(near, t), chunk(far, t))
            behind = jnp.where(zero, chunk(far, -t), chunk(near, -t))
            total = total + (ahead + behind)
        scale_ref[:, pl.ds(s * width, width)] = 1.0 / total


def sweep_kernel(*refs, ring, last):
    valid_ref, weights_ref, *refs = refs
    totals = refs[:ring]
    if last:
        out_ref, rows_ref, scale_ref = refs[ring:]
    else:
        out_ref, scale_ref = refs[ring:]
    inverse_totals(totals, scale_ref)
    weights, valid = weights_ref[...], valid_ref[...]
    total = lax.dot_general(exact(scale_ref[...]), weights, NT, preferred_element_type=F32)
    total = jnp.sum(total, axis=0, keepdims=True)
    row_scale = valid / (total + 1.0 - valid)
    sums = lax.dot_general(exact(row_scale), weights, NN, preferred_element_type=F32)
    sums = jnp.sum(sums, axis=0, keepdims=True)
    if last:
        rows_ref[...] = row_scale
        out_ref[...] = sums * scale_ref[...]
    else:
        out_ref[...] = sums


def high_low(total, height):
    line = lax.broadcasted_iota(jnp.int32, (height, total.shape[1]), 0)
    high = total.astype(BF16).astype(F32)
    return jnp.where(line == 0, high, jnp.where(line == 1, total - high, 0.0)).astype(BF16)


def numerator_kernel(turned_ref, weights_ref, *refs, chunk, first, height, fresh):
    fast = fast_here()
    if fresh:
        rows_ref, scale_ref, mass_ref, scaled_ref, *outs = refs
        scaled = turned_ref[pl.ds(first, height), :].astype(F32) * rows_ref[...]
        scaled_ref[...] = scaled.astype(BF16)
    else:
        scale_ref, mass_ref, *outs = refs
        scaled_ref = turned_ref
    width = outs[0].shape[1]
    step = min(256, height)
    at = pl.ds(chunk * 2 * width, 2 * width)
    for i in range(height // step):
        part = lax.dot_general(
            scaled_ref[pl.ds(i * step, step), :],
            weights_ref[:, at],
            NN,
            preferred_element_type=F32,
        )
        part = (part * scale_ref[:, at]).astype(BF16)
        one, two = part[:, :width], part[:, width:]
        outs[0][pl.ds(i * step, step), :] = jnp.where(fast, one, two)
        outs[1][pl.ds(i * step, step), :] = jnp.where(fast, two, one)
    extra = outs[0].shape[0] - height
    if extra:
        masses = [mass_ref[:, pl.ds((2 * chunk + k) * width, width)] for k in range(2)]
        one, two = (high_low(mass, extra) for mass in masses)
        outs[0][pl.ds(height, extra), :] = jnp.where(fast, one, two)
        outs[1][pl.ds(height, extra), :] = jnp.where(fast, two, one)


def total_of(refs, height):
    total = refs[0][0:height, :].astype(F32)
    for ref in refs[1:]:
        total = total + ref[0:height, :].astype(F32)
    return total


def mass_of(refs, height):
    mass = 0.0
    for ref in refs:
        lines = ref[height : height + 16, :].astype(F32)
        mass = mass + (lines[0:1] + lines[1:2])
    return mass


def combine_kernel(*refs, height):
    out_ref = refs[-1]
    extra = out_ref.shape[0] - height
    out_ref[0:height, :] = total_of(refs[:-1], height).astype(BF16)
    if extra:
        out_ref[height : height + extra, :] = high_low(mass_of(refs[:-1], height), extra)


def finish_kernel(*refs, height):
    out_ref, mass_ref = refs[-2:]
    terms = refs[:-2]
    parts = len(terms) // 2
    mass = mass_of(terms[2 * parts - 2 :], height)
    mass_ref[...] = mass
    inverse = 1.0 / mass
    for j in range(parts):
        total = total_of(terms[2 * j : 2 * j + 2], height)
        out_ref[:, pl.ds(j * height, height)] = (total * inverse).T


def body(embeddings, level_one, centroids):
    groups, peers = lax.axis_size("grp"), lax.axis_size("dev")
    routes = Routes(groups, peers)
    ring = routes.ring
    count, depth = embeddings.shape
    capacity = 2 * count // groups
    slots = groups * capacity
    owned = centroids.shape[0]
    clusters = owned * peers
    parts = 2

    own = call(
        unit_kernel,
        (shape(owned // parts, depth),) * parts,
        [send(centroids, routes.swap)],
        name="unit_centroids",
        cost_estimate=WAIT,
    )
    mine = [own]
    for s in range(1, ring):
        mine.append([send(p, routes.shift[1]) for p in mine[-1]])
    other = [[send(p, routes.core) for p in m] for m in mine]

    place = call(
        rank_kernel,
        shape(-(-groups // 8) * 8, count, dtype=jnp.int32),
        [level_one.reshape(1, count)],
        name="rank_rows",
    )

    def pick(d, after=()):
        return call(
            functools.partial(pick_kernel, which=d),
            shape(capacity, depth),
            [place, embeddings],
            after=after,
            name="pick_rows",
        )

    arrived, packed = {}, ()
    for d in [*range(2, groups), 1, 0]:
        packed = (pick(d, packed),)
        arrived[d] = send(packed[0], routes.cluster[d]) if d else packed[0]

    state_shapes = (
        shape(slots, depth),
        shape(1, slots, dtype=F32),
        shape(slots, clusters),
        shape(1, clusters, dtype=F32),
    )

    def absorb(state, raw, lines, columns):
        pieces = [p for s in columns for part in (mine, other) for p in part[s]]
        rows = [arrived[d] for d in raw]
        return call(
            functools.partial(
                weights_kernel,
                raw=raw,
                lines=lines,
                columns=columns,
                carried=bool(state),
                groups=groups,
            ),
            state_shapes,
            [*state, *rows, *pieces],
            alias={j: j for j in range(len(state))},
            name="weights",
        )

    early = list(range(ring - 1))
    state = absorb((), [0], [0], early)
    rest = list(range(1, groups))
    waited = rest
    arrived.update(zip(waited, tie([arrived[d] for d in waited], ())))
    state = absorb(state, rest, rest, early)
    rows, valid, weights, part = absorb(state, [], [0, *rest], [ring - 1])
    turned = call(
        turn_kernel, shape(depth, slots), [arrived[d] for d in range(groups)], name="turn_rows"
    )

    def sweep(part, last):
        chip = call(
            join_kernel,
            shape(1, clusters, dtype=F32),
            [part, send(part, routes.core)],
            name="join_cores",
        )
        near = [send(chip, routes.both[t]) for t in range(1, ring // 2)]
        totals = [chip, send(chip, routes.shift[ring // 2])]
        for value in near:
            totals += [value, send(value, routes.core)]
        outs = (shape(1, clusters, dtype=F32),)
        if last:
            outs += (shape(1, slots, dtype=F32), shape(1, clusters, dtype=F32))
        return call(
            functools.partial(sweep_kernel, ring=ring, last=last),
            outs,
            [valid, weights, *totals],
            scratch_shapes=() if last else (pltpu.VMEM((1, clusters), F32),),
            name="last_sweep" if last else "sweep",
        )

    for _ in range(SWEEPS - 1):
        (part,) = sweep(part, last=False)
    mass_part, row_scale, column_scale = sweep(part, last=True)

    height = depth // parts
    tall = [height] * (parts - 1) + [height + 16]

    def numerator(s, j, after):
        fresh = scaled[j] is None
        args = [turned, weights, row_scale] if fresh else [scaled[j], weights]
        args = [*args, column_scale, mass_part]
        outs = (shape(tall[j], owned),) * 2
        if fresh:
            outs = (shape(height, slots), *outs)
        outs = call(
            functools.partial(
                numerator_kernel, chunk=s, first=j * height, height=height, fresh=fresh
            ),
            outs,
            args,
            after=after,
            name="numerator",
            cost_estimate=cost(height, 2 * owned, slots),
        )
        if fresh:
            scaled[j] = outs[0]
        return outs[-2], outs[-1]

    def combine(j, *terms):
        return call(
            functools.partial(combine_kernel, height=height),
            shape(tall[j], owned),
            terms,
            name="combine",
        )

    scaled = [None] * parts
    after, moving, kept = (), [()] * parts, []
    for s in [*range(1, ring), 0]:
        route = routes.swap if s == 0 else routes.home if s == ring - 1 else routes.shift[1]
        pairs = []
        for j in range(parts):
            kept_part, sent_part = numerator(s, j, after)
            pairs.append((kept_part, send(sent_part, routes.core)))
        if s == 0:
            kept = [send(combine(j, *pairs[j]), route) for j in range(parts)]
            continue
        added = [combine(j, *moving[j], *pairs[j]) for j in range(parts)]
        if s == 1:
            after = tuple(added)
        moving = [(send(a, route),) for a in added]

    updated, mass = call(
        functools.partial(finish_kernel, height=height),
        (shape(owned, depth, dtype=F32), shape(1, owned, dtype=F32)),
        [t for j in range(parts) for t in (moving[j][0], kept[j])],
        name="finish",
    )
    return updated, mass.reshape(owned)


def solution(mesh):
    in_specs = (P(AXES, None), P(AXES, None), P(AXES, None))
    out_specs = (P(AXES, None), P(AXES))
    return jax.shard_map(body, mesh=mesh, in_specs=in_specs, out_specs=out_specs, check_vma=False)
```

time: 281 us -> 144 us (0.51)
  blocking collectives: 60.5 us -> 0 us
  waiting for transfers between devices: 121 us -> 62.3 us
  starting transfers between devices: 8.24 us -> 47.1 us
  other arithmetic: 32 us -> 0 us
  Pallas kernels: 0 us -> 31.2 us
  matrix products: 24.3 us -> 0 us
  local copies, waits for them, and re-layouts: 19.1 us -> 2.09 us
  between operations: 14.2 us -> 1.01 us
    reduce_scatter x1 -> x0, waiting for transfers between devices: 77.8 us -> none  [body(): lax.psum_scatter(lax.dot_general(shared, group_rows, (((0,), (0,)), ((),...]
    ppermute x0 -> x46, waiting for transfers between devices: none -> 62.3 us  [send(): return lax.ppermute(value, AXES, route)]
    psum x4 -> x0, blocking collectives: 60.5 us -> none  [the longest x3 46.2 us: body(): column_total = lax.psum(partial_total, 'dev')]
    ppermute x0 -> x46, starting transfers between devices: none -> 47.1 us  [send(): return lax.ppermute(value, AXES, route)]
    all_to_all x2 -> x0, waiting for transfers between devices: 35.8 us -> none  [the longest x1 35.8 us: body(): lax.all_to_all(outgoing.reshape(groups, capacity, feature_width), 'grp',...]
    pallas_call x0 -> x34, Pallas kernels: none -> 31.2 us  [the longest x33 31.2 us: call(): pl.pallas_call(ordered, out_shape=outs, in_specs=(specs or [VMEM] * len(a...]
    dot_general x2 -> x0, matrix products: 24.3 us -> none  [the longest x1 12.2 us: body(): lax.dot_general(normed, lax.all_gather(own_normed, 'dev', axis=0, tiled=T...]
    reduce_sum x9 -> x0, other arithmetic: 24.2 us -> none  [the longest x3 12.5 us: body(): jnp.sum(weights.astype(jnp.float32) * column_scale[None, :], axis=1)]
  transfers between devices with their start and end apart: 4 -> 46, of which waited for: 3 -> 22; matrix products, arithmetic and copies ran while one was open for 10% -> 0% of each run, Pallas kernels for 0% -> 13%
where the time goes in v2:
time: 144 us
  waiting for transfers between devices  62.3 us (43%)
  starting transfers between devices  47.1 us (33%)
  Pallas kernels  31.2 us (22%)
  local copies, waits for them, and re-layouts  2.09 us (1%)
    ppermute x46, waiting for transfers between devices, send(): return lax.ppermute(value, AXES, route)  62.3 us
    ppermute x46, starting transfers between devices, send(): return lax.ppermute(value, AXES, route)  47.1 us
    pallas_call x33, Pallas kernels, call(): pl.pallas_call(ordered, out_shape=outs, in_specs=(specs or [VMEM] * len(a...  31.2 us
  transfers between devices with their start and end apart: 46, of which 22 were waited for; matrix products, arithmetic and copies ran while one was open for 0% of the time, Pallas kernels for 13%

profile of v2, /device:TPU:1, one launch (start us, length us, event | category | flops | bytes accessed | tf_op | source)
XLA Modules:
  0.0 143.8 jit_solution(15949438289294894973)
XLA Ops:
  0.6 4.5 %collective-permute-start.3 = (bf16[256,1024]{1,0:T(8,128)(2,1)}, bf16[256,1024]{1,0:T(8,128)(2,1)S(1)}, u32[]{:S(2)}, u32[]{:S(2)}) collective-permute-start(bf16[256,1024]{1,0:T(8,128)(2,1)} %param.5), channel_id=1, source_target_pairs={{0,0},{1,8},{2,2},{3,10},{4,4},{5,12},{6,6},{7,14},{8,1},{9,9},{10... | collective-permute-start | bytes 1572872 | tf_op jit(solution)/shard_map/ppermute | solution.py:57
  6.1 1.4 copy-done
  10.1 2.1 %collective-permute-done.3.refs_0_ = bf16[256,1024]{1,0:T(8,128)(2,1)S(1)} collective-permute-done((bf16[256,1024]{1,0:T(8,128)(2,1)}, bf16[256,1024]{1,0:T(8,128)(2,1)S(1)}, u32[]{:S(2)}, u32[]{:S(2)}) %collective-permute-start.3) | collective-permute-done | bytes 524320 | tf_op jit(solution)/shard_map/ppermute | solution.py:57
  12.4 1.3 collective-permute-start.6
  16.3 6.4 %collective-permute-done.6.refs_5_.refs_11_ = bf16[128,1024]{1,0:T(8,128)(2,1)S(1)} collective-permute-done((bf16[128,1024]{1,0:T(8,128)(2,1)S(1)}, bf16[128,1024]{1,0:T(8,128)(2,1)S(1)}, u32[]{:S(2)}, u32[]{:S(2)}) %collective-permute-start.6) | collective-permute-done | bytes 262176 | tf_op jit(solution)/shard_map/ppermute | solution.py:57
  22.7 4.0 %collective-permute-done.7.refs_6_.refs_12_ = bf16[128,1024]{1,0:T(8,128)(2,1)S(1)} collective-permute-done((bf16[128,1024]{1,0:T(8,128)(2,1)S(1)}, bf16[128,1024]{1,0:T(8,128)(2,1)S(1)}, u32[]{:S(2)}, u32[]{:S(2)}) %collective-permute-start.7) | collective-permute-done | bytes 262176 | tf_op jit(solution)/shard_map/ppermute | solution.py:57
  26.7 1.5 %collective-permute-done.5.refs_4_.refs_10_ = bf16[128,1024]{1,0:T(8,128)(2,1)S(1)} collective-permute-done((bf16[128,1024]{1,0:T(8,128)(2,1)S(1)}, bf16[128,1024]{1,0:T(8,128)(2,1)S(1)}, u32[]{:S(2)}, u32[]{:S(2)}) %collective-permute-start.5) | collective-permute-done | bytes 262176 | tf_op jit(solution)/shard_map/ppermute | solution.py:57
  28.2 1.5 %collective-permute-done.refs_0_ = bf16[384,1024]{1,0:T(8,128)(2,1)S(1)} collective-permute-done((bf16[384,1024]{1,0:T(8,128)(2,1)S(1)}, bf16[384,1024]{1,0:T(8,128)(2,1)S(1)}, u32[]{:S(2)}, u32[]{:S(2)}) %collective-permute-start) | collective-permute-done | bytes 786464 | tf_op jit(solution)/shard_map/ppermute | solution.py:57
  29.7 6.1 %collective-permute-done.10.refs_9_.refs_15_ = bf16[128,1024]{1,0:T(8,128)(2,1)S(1)} collective-permute-done((bf16[128,1024]{1,0:T(8,128)(2,1)S(1)}, bf16[128,1024]{1,0:T(8,128)(2,1)S(1)}, u32[]{:S(2)}, u32[]{:S(2)}) %collective-permute-start.10) | collective-permute-done | bytes 262176 | tf_op jit(solution)/shard_map/ppermute | solution.py:57
  35.8 5.6 %collective-permute-done.11.refs_10_.refs_16_ = bf16[128,1024]{1,0:T(8,128)(2,1)S(1)} collective-permute-done((bf16[128,1024]{1,0:T(8,128)(2,1)S(1)}, bf16[128,1024]{1,0:T(8,128)(2,1)S(1)}, u32[]{:S(2)}, u32[]{:S(2)}) %collective-permute-start.11) | collective-permute-done | bytes 262176 | tf_op jit(solution)/shard_map/ppermute | solution.py:57
  42.3 4.9 %collective-permute-done.2.refs_2_ = bf16[384,1024]{1,0:T(8,128)(2,1)S(1)} collective-permute-done((bf16[384,1024]{1,0:T(8,128)(2,1)S(1)}, bf16[384,1024]{1,0:T(8,128)(2,1)S(1)}, u32[]{:S(2)}, u32[]{:S(2)}) %collective-permute-start.2) | collective-permute-done | bytes 786464 | tf_op jit(solution)/shard_map/ppermute | solution.py:57
  47.8 4.4 %collective-permute-start.12 = (bf16[128,1024]{1,0:T(8,128)(2,1)S(1)}, bf16[128,1024]{1,0:T(8,128)(2,1)S(1)}, u32[]{:S(2)}, u32[]{:S(2)}) collective-permute-start(bf16[128,1024]{1,0:T(8,128)(2,1)S(1)} %collective-permute-done.10.refs_9_.refs_15_), channel_id=1, source_target_pairs={{0,8},{1,9},{2,10},{3,11},{4,12},{5,13},{6,14},{7,15},{8,0},{9,1},... | collective-permute-start | bytes 786440 | tf_op jit(solution)/shard_map/ppermute | solution.py:57
  52.7 1.3 collective-permute-start.17
  54.1 1.8 %weights.3 = (bf16[1536,1024]{1,0:T(8,128)(2,1)S(1)}, f32[1,1536]{1,0:T(1,128)S(1)}, bf16[1536,2048]{1,0:T(8,128)(2,1)S(1)}, f32[1,2048]{1,0:T(1,128)S(1)}) custom-call(bf16[384,1024]{1,0:T(8,128)(2,1)S(1)} %pick_rows.7.refs_0_, bf16[128,1024]{1,0:T(8,128)(2,1)S(1)} %get-tuple-element.44.refs_1_.refs_7_, ...), custom_call_target="tpu_custom_call" | custom-call | tf_op jit(solution)/shard_map/weights/pallas_call | solution.py:66
  55.9 5.1 %weights.4 = (bf16[1536,1024]{1,0:T(8,128)(2,1)S(1)}, f32[1,1536]{1,0:T(1,128)S(1)}, bf16[1536,2048]{1,0:T(8,128)(2,1)S(1)}, f32[1,2048]{1,0:T(1,128)S(1)}) custom-call(bf16[1536,1024]{1,0:T(8,128)(2,1)S(1)} %get-tuple-element.46.refs_0_, ...), custom_call_target="tpu_custom_call", output_to_operand_aliasing={{0}: (0, {}), {1}: (1, {}), {2}: (2, {}), {3}: (3, {})} | custom-call | tf_op jit(solution)/shard_map/weights/pallas_call | solution.py:66
  61.0 2.0 %weights.5 = (bf16[1536,1024]{1,0:T(8,128)(2,1)S(1)}, f32[1,1536]{1,0:T(1,128)S(1)}, bf16[1536,2048]{1,0:T(8,128)(2,1)S(1)}, f32[1,2048]{1,0:T(1,128)S(1)}) custom-call(bf16[1536,1024]{1,0:T(8,128)(2,1)S(1)} %get-tuple-element.50.refs_0_, ...), custom_call_target="tpu_custom_call", output_to_operand_aliasing={{0}: (0, {}), {1}: (1, {}), {2}: (2, {}), {3}: (3, {})} | custom-call | tf_op jit(solution)/shard_map/weights/pallas_call | solution.py:66
  64.3 1.6 %collective-permute-start.20 = (f32[1,2048]{1,0:T(1,128)S(1)}, f32[1,2048]{1,0:T(1,128)S(1)}, u32[]{:S(2)}, u32[]{:S(2)}) collective-permute-start(f32[1,2048]{1,0:T(1,128)S(1)} %join_cores.3.refs_2_), channel_id=1, source_target_pairs={{0,2},{1,3},{2,4},{3,5},{4,6},{5,7},{6,0},{7,1},{8,14},{9,15},{10,... | collective-permute-start | bytes 24584 | tf_op jit(solution)/shard_map/ppermute | solution.py:57
  66.8 3.1 %collective-permute-start.21 = (f32[1,2048]{1,0:T(1,128)S(1)}, f32[1,2048]{1,0:T(1,128)S(1)}, u32[]{:S(2)}, u32[]{:S(2)}) collective-permute-start(f32[1,2048]{1,0:T(1,128)S(1)} %collective-permute-done.20.refs_4_), channel_id=1, source_target_pairs={{0,8},{1,9},{2,10},{3,11},{4,12},{5,13},{6,14},{7,15},{8,0},{9,1},... | collective-permute-start | bytes 24584 | tf_op jit(solution)/shard_map/ppermute | solution.py:57
  70.7 2.6 %sweep.2.refs_0_ = f32[1,2048]{1,0:T(1,128)S(1)} custom-call(f32[1,1536]{1,0:T(1,128)S(1)} %get-tuple-element.55.refs_0_, bf16[1536,2048]{1,0:T(8,128)(2,1)S(1)} %get-tuple-element.54.refs_1_, f32[1,2048]{1,0:T(1,128)S(1)} %join_cores.3.refs_2_, f32[1,2048]{1,0:T(1,128)S(1)} %collective-permute-done.19.refs_3_, ...), custom_call_target="tpu_custom_call" | custom-call | tf_op jit(solution)/shard_map/sweep/pallas_call | solution.py:66
  74.5 1.5 %collective-permute-start.24 = (f32[1,2048]{1,0:T(1,128)S(1)}, f32[1,2048]{1,0:T(1,128)S(1)}, u32[]{:S(2)}, u32[]{:S(2)}) collective-permute-start(f32[1,2048]{1,0:T(1,128)S(1)} %join_cores.4.refs_2_), channel_id=1, source_target_pairs={{0,2},{1,3},{2,4},{3,5},{4,6},{5,7},{6,0},{7,1},{8,14},{9,15},{10,... | collective-permute-start | bytes 24584 | tf_op jit(solution)/shard_map/ppermute | solution.py:57
  77.0 3.3 %collective-permute-start.25 = (f32[1,2048]{1,0:T(1,128)S(1)}, f32[1,2048]{1,0:T(1,128)S(1)}, u32[]{:S(2)}, u32[]{:S(2)}) collective-permute-start(f32[1,2048]{1,0:T(1,128)S(1)} %collective-permute-done.24.refs_4_), channel_id=1, source_target_pairs={{0,8},{1,9},{2,10},{3,11},{4,12},{5,13},{6,14},{7,15},{8,0},{9,1},... | collective-permute-start | bytes 24584 | tf_op jit(solution)/shard_map/ppermute | solution.py:57
  81.1 2.6 %sweep.3.refs_0_ = f32[1,2048]{1,0:T(1,128)S(1)} custom-call(f32[1,1536]{1,0:T(1,128)S(1)} %get-tuple-element.55.refs_0_, bf16[1536,2048]{1,0:T(8,128)(2,1)S(1)} %get-tuple-element.54.refs_1_, f32[1,2048]{1,0:T(1,128)S(1)} %join_cores.4.refs_2_, f32[1,2048]{1,0:T(1,128)S(1)} %collective-permute-done.23.refs_3_, ...), custom_call_target="tpu_custom_call" | custom-call | tf_op jit(solution)/shard_map/sweep/pallas_call | solution.py:66
  85.0 1.5 %collective-permute-start.28 = (f32[1,2048]{1,0:T(1,128)S(1)}, f32[1,2048]{1,0:T(1,128)S(1)}, u32[]{:S(2)}, u32[]{:S(2)}) collective-permute-start(f32[1,2048]{1,0:T(1,128)S(1)} %join_cores.5.refs_2_), channel_id=1, source_target_pairs={{0,2},{1,3},{2,4},{3,5},{4,6},{5,7},{6,0},{7,1},{8,14},{9,15},{10,... | collective-permute-start | bytes 24584 | tf_op jit(solution)/shard_map/ppermute | solution.py:57
  87.5 3.3 %collective-permute-start.29 = (f32[1,2048]{1,0:T(1,128)S(1)}, f32[1,2048]{1,0:T(1,128)S(1)}, u32[]{:S(2)}, u32[]{:S(2)}) collective-permute-start(f32[1,2048]{1,0:T(1,128)S(1)} %collective-permute-done.28.refs_4_), channel_id=1, source_target_pairs={{0,8},{1,9},{2,10},{3,11},{4,12},{5,13},{6,14},{7,15},{8,0},{9,1},... | collective-permute-start | bytes 24584 | tf_op jit(solution)/shard_map/ppermute | solution.py:57
  91.6 2.6 %last_sweep.1 = (f32[1,2048]{1,0:T(1,128)S(1)}, f32[1,1536]{1,0:T(1,128)S(1)}, f32[1,2048]{1,0:T(1,128)S(1)}) custom-call(f32[1,1536]{1,0:T(1,128)S(1)} %get-tuple-element.55.refs_0_, bf16[1536,2048]{1,0:T(8,128)(2,1)S(1)} %get-tuple-element.54.refs_1_, f32[1,2048]{1,0:T(1,128)S(1)} %join_cores.5.refs_2_, f32[1,2048]{1,0:T(1,128)S(1)} %collective-permute-done.27.refs_3_, ...), custom_call_target="tpu_custom_call" | custom-call | tf_op jit(solution)/shard_map/last_sweep/pallas_call | solution.py:66
  105.4 8.2 %collective-permute-done.39.refs_0_ = bf16[528,256]{1,0:T(8,128)(2,1)S(1)} collective-permute-done((bf16[528,256]{1,0:T(8,128)(2,1)S(1)}, bf16[528,256]{1,0:T(8,128)(2,1)S(1)}, u32[]{:S(2)}, u32[]{:S(2)}) %collective-permute-start.39) | collective-permute-done | bytes 270368 | tf_op jit(solution)/shard_map/ppermute | solution.py:57
  116.2 4.2 %collective-permute-start.45 = (bf16[528,256]{1,0:T(8,128)(2,1)S(1)}, bf16[528,256]{1,0:T(8,128)(2,1)S(1)}, u32[]{:S(2)}, u32[]{:S(2)}) collective-permute-start(bf16[528,256]{1,0:T(8,128)(2,1)S(1)} %combine.15), channel_id=1, source_target_pairs={{0,0},{1,8},{2,2},{3,10},{4,4},{5,12},{6,6},{7,14},{8,1},{9,9},{10... | collective-permute-start | bytes 811016 | tf_op jit(solution)/shard_map/ppermute | solution.py:57
  120.4 2.1 %collective-permute-done.41.refs_0_ = bf16[528,256]{1,0:T(8,128)(2,1)S(1)} collective-permute-done((bf16[528,256]{1,0:T(8,128)(2,1)S(1)}, bf16[528,256]{1,0:T(8,128)(2,1)S(1)}, u32[]{:S(2)}, u32[]{:S(2)}) %collective-permute-start.41) | collective-permute-done | bytes 270368 | tf_op jit(solution)/shard_map/ppermute | solution.py:57
  122.6 3.0 %collective-permute-start.43 = (bf16[528,256]{1,0:T(8,128)(2,1)S(1)}, bf16[528,256]{1,0:T(8,128)(2,1)S(1)}, u32[]{:S(2)}, u32[]{:S(2)}) collective-permute-start(bf16[528,256]{1,0:T(8,128)(2,1)S(1)} %combine.14), channel_id=1, source_target_pairs={{0,2},{1,10},{2,4},{3,12},{4,6},{5,14},{6,0},{7,8},{8,3},{9,11},{1... | collective-permute-start | bytes 811016 | tf_op jit(solution)/shard_map/ppermute | solution.py:57
  125.7 4.3 %collective-permute-start.38 = (bf16[512,256]{1,0:T(8,128)(2,1)S(1)}, bf16[512,256]{1,0:T(8,128)(2,1)S(1)}, u32[]{:S(2)}, u32[]{:S(2)}) collective-permute-start(bf16[512,256]{1,0:T(8,128)(2,1)S(1)} %combine.12), channel_id=1, source_target_pairs={{0,0},{1,8},{2,2},{3,10},{4,4},{5,12},{6,6},{7,14},{8,1},{9,9},{10... | collective-permute-start | bytes 786440 | tf_op jit(solution)/shard_map/ppermute | solution.py:57
  131.2 4.6 %collective-permute-done.38.refs_1_ = bf16[512,256]{1,0:T(8,128)(2,1)S(1)} collective-permute-done((bf16[512,256]{1,0:T(8,128)(2,1)S(1)}, bf16[512,256]{1,0:T(8,128)(2,1)S(1)}, u32[]{:S(2)}, u32[]{:S(2)}) %collective-permute-start.38) | collective-permute-done | bytes 262176 | tf_op jit(solution)/shard_map/ppermute | solution.py:57
  135.8 6.6 %collective-permute-done.36.refs_0_ = bf16[512,256]{1,0:T(8,128)(2,1)S(1)} collective-permute-done((bf16[512,256]{1,0:T(8,128)(2,1)S(1)}, bf16[512,256]{1,0:T(8,128)(2,1)S(1)}, u32[]{:S(2)}, u32[]{:S(2)}) %collective-permute-start.36) | collective-permute-done | bytes 262176 | tf_op jit(solution)/shard_map/ppermute | solution.py:57
  (100 shorter events, 33.6 us)
Async XLA Ops:
  0.6 11.6 %collective-permute-start.3 = (bf16[256,1024]{1,0:T(8,128)(2,1)}, bf16[256,1024]{1,0:T(8,128)(2,1)S(1)}, u32[]{:S(2)}, u32[]{:S(2)}) collective-permute-start(bf16[256,1024]{1,0:T(8,128)(2,1)} %param.5), channel_id=1, source_target_pairs={{0,0},{1,8},{2,2},{3,10},{4,4},{5,12},{6,6},{7,14},{8,1},{9,9},{10... | collective-permute-start | bytes 1572872 | tf_op jit(solution)/shard_map/ppermute | solution.py:57
  10.0 19.7 %collective-permute-start = (bf16[384,1024]{1,0:T(8,128)(2,1)S(1)}, bf16[384,1024]{1,0:T(8,128)(2,1)S(1)}, u32[]{:S(2)}, u32[]{:S(2)}) collective-permute-start(bf16[384,1024]{1,0:T(8,128)(2,1)S(1)} %pick_rows.6.refs_2_), channel_id=1, source_target_pairs={{0,1},{1,0},{2,3},{3,2},{4,5},{5,4},{6,7},{7,6},{8,9},{9,8},{10,11... | collective-permute-start | bytes 2359304 | tf_op jit(solution)/shard_map/ppermute | solution.py:57
  12.4 10.3 %collective-permute-start.6 = (bf16[128,1024]{1,0:T(8,128)(2,1)S(1)}, bf16[128,1024]{1,0:T(8,128)(2,1)S(1)}, u32[]{:S(2)}, u32[]{:S(2)}) collective-permute-start(bf16[128,1024]{1,0:T(8,128)(2,1)S(1)} %get-tuple-element.44.refs_1_.refs_7_), channel_id=1, source_target_pairs={{0,2},{1,3},{2,4},{3,5},{4,6},{5,7},{6,0},{7,1},{8,10},{9,11},{10,... | collective-permute-start | bytes 786440 | tf_op jit(solution)/shard_map/ppermute | solution.py:57
  13.8 12.9 %collective-permute-start.7 = (bf16[128,1024]{1,0:T(8,128)(2,1)S(1)}, bf16[128,1024]{1,0:T(8,128)(2,1)S(1)}, u32[]{:S(2)}, u32[]{:S(2)}) collective-permute-start(bf16[128,1024]{1,0:T(8,128)(2,1)S(1)} %get-tuple-element.45.refs_2_.refs_8_), channel_id=1, source_target_pairs={{0,2},{1,3},{2,4},{3,5},{4,6},{5,7},{6,0},{7,1},{8,10},{9,11},{10,... | collective-permute-start | bytes 786440 | tf_op jit(solution)/shard_map/ppermute | solution.py:57
  15.0 32.2 %collective-permute-start.2 = (bf16[384,1024]{1,0:T(8,128)(2,1)S(1)}, bf16[384,1024]{1,0:T(8,128)(2,1)S(1)}, u32[]{:S(2)}, u32[]{:S(2)}) collective-permute-start(bf16[384,1024]{1,0:T(8,128)(2,1)S(1)} %pick_rows.5.refs_2_), channel_id=1, source_target_pairs={{0,17},{1,16},{2,19},{3,18},{4,21},{5,20},{6,23},{7,22},{8,25},{9,... | collective-permute-start | bytes 2359304 | tf_op jit(solution)/shard_map/ppermute | solution.py:57
  15.4 32.4 %collective-permute-start.1 = (bf16[384,1024]{1,0:T(8,128)(2,1)S(1)}, bf16[384,1024]{1,0:T(8,128)(2,1)S(1)}, u32[]{:S(2)}, u32[]{:S(2)}) collective-permute-start(bf16[384,1024]{1,0:T(8,128)(2,1)S(1)} %pick_rows.4.refs_2_), channel_id=1, source_target_pairs={{0,16},{1,17},{2,18},{3,19},{4,20},{5,21},{6,22},{7,23},{8,24},{9,... | collective-permute-start | bytes 2359304 | tf_op jit(solution)/shard_map/ppermute | solution.py:57
  26.7 9.2 %collective-permute-start.10 = (bf16[128,1024]{1,0:T(8,128)(2,1)S(1)}, bf16[128,1024]{1,0:T(8,128)(2,1)S(1)}, u32[]{:S(2)}, u32[]{:S(2)}) collective-permute-start(bf16[128,1024]{1,0:T(8,128)(2,1)S(1)} %collective-permute-done.6.refs_5_.refs_11_), channel_id=1, source_target_pairs={{0,2},{1,3},{2,4},{3,5},{4,6},{5,7},{6,0},{7,1},{8,10},{9,11},{10,... | collective-permute-start | bytes 786440 | tf_op jit(solution)/shard_map/ppermute | solution.py:57
  28.2 13.2 %collective-permute-start.11 = (bf16[128,1024]{1,0:T(8,128)(2,1)S(1)}, bf16[128,1024]{1,0:T(8,128)(2,1)S(1)}, u32[]{:S(2)}, u32[]{:S(2)}) collective-permute-start(bf16[128,1024]{1,0:T(8,128)(2,1)S(1)} %collective-permute-done.7.refs_6_.refs_12_), channel_id=1, source_target_pairs={{0,2},{1,3},{2,4},{3,5},{4,6},{5,7},{6,0},{7,1},{8,10},{9,11},{10,... | collective-permute-start | bytes 786440 | tf_op jit(solution)/shard_map/ppermute | solution.py:57
  29.7 22.5 %collective-permute-start.8 = (bf16[128,1024]{1,0:T(8,128)(2,1)S(1)}, bf16[128,1024]{1,0:T(8,128)(2,1)S(1)}, u32[]{:S(2)}, u32[]{:S(2)}) collective-permute-start(bf16[128,1024]{1,0:T(8,128)(2,1)S(1)} %collective-permute-done.6.refs_5_.refs_11_), channel_id=1, source_target_pairs={{0,8},{1,9},{2,10},{3,11},{4,12},{5,13},{6,14},{7,15},{8,0},{9,1},... | collective-permute-start | bytes 786440 | tf_op jit(solution)/shard_map/ppermute | solution.py:57
  35.8 16.4 %collective-permute-start.14 = (bf16[128,1024]{1,0:T(8,128)(2,1)S(1)}, bf16[128,1024]{1,0:T(8,128)(2,1)S(1)}, u32[]{:S(2)}, u32[]{:S(2)}) collective-permute-start(bf16[128,1024]{1,0:T(8,128)(2,1)S(1)} %collective-permute-done.10.refs_9_.refs_15_), channel_id=1, source_target_pairs={{0,2},{1,3},{2,4},{3,5},{4,6},{5,7},{6,0},{7,1},{8,10},{9,11},{10,... | collective-permute-start | bytes 786440 | tf_op jit(solution)/shard_map/ppermute | solution.py:57
  41.5 11.3 %collective-permute-start.15 = (bf16[128,1024]{1,0:T(8,128)(2,1)S(1)}, bf16[128,1024]{1,0:T(8,128)(2,1)S(1)}, u32[]{:S(2)}, u32[]{:S(2)}) collective-permute-start(bf16[128,1024]{1,0:T(8,128)(2,1)S(1)} %collective-permute-done.11.refs_10_.refs_16_), channel_id=1, source_target_pairs={{0,2},{1,3},{2,4},{3,5},{4,6},{5,7},{6,0},{7,1},{8,10},{9,11},{10,... | collective-permute-start | bytes 786440 | tf_op jit(solution)/shard_map/ppermute | solution.py:57
  47.2 6.8 %collective-permute-start.9 = (bf16[128,1024]{1,0:T(8,128)(2,1)S(1)}, bf16[128,1024]{1,0:T(8,128)(2,1)S(1)}, u32[]{:S(2)}, u32[]{:S(2)}) collective-permute-start(bf16[128,1024]{1,0:T(8,128)(2,1)S(1)} %collective-permute-done.7.refs_6_.refs_12_), channel_id=1, source_target_pairs={{0,8},{1,9},{2,10},{3,11},{4,12},{5,13},{6,14},{7,15},{8,0},{9,1},... | collective-permute-start | bytes 786440 | tf_op jit(solution)/shard_map/ppermute | solution.py:57
  47.8 6.3 %collective-permute-start.12 = (bf16[128,1024]{1,0:T(8,128)(2,1)S(1)}, bf16[128,1024]{1,0:T(8,128)(2,1)S(1)}, u32[]{:S(2)}, u32[]{:S(2)}) collective-permute-start(bf16[128,1024]{1,0:T(8,128)(2,1)S(1)} %collective-permute-done.10.refs_9_.refs_15_), channel_id=1, source_target_pairs={{0,8},{1,9},{2,10},{3,11},{4,12},{5,13},{6,14},{7,15},{8,0},{9,1},... | collective-permute-start | bytes 786440 | tf_op jit(solution)/shard_map/ppermute | solution.py:57
  52.2 8.8 %collective-permute-start.16 = (bf16[128,1024]{1,0:T(8,128)(2,1)S(1)}, bf16[128,1024]{1,0:T(8,128)(2,1)S(1)}, u32[]{:S(2)}, u32[]{:S(2)}) collective-permute-start(bf16[128,1024]{1,0:T(8,128)(2,1)S(1)} %collective-permute-done.14.refs_4_), channel_id=1, source_target_pairs={{0,8},{1,9},{2,10},{3,11},{4,12},{5,13},{6,14},{7,15},{8,0},{9,1},... | collective-permute-start | bytes 786440 | tf_op jit(solution)/shard_map/ppermute | solution.py:57
  52.7 8.3 %collective-permute-start.17 = (bf16[128,1024]{1,0:T(8,128)(2,1)S(1)}, bf16[128,1024]{1,0:T(8,128)(2,1)S(1)}, u32[]{:S(2)}, u32[]{:S(2)}) collective-permute-start(bf16[128,1024]{1,0:T(8,128)(2,1)S(1)} %collective-permute-done.15.refs_5_), channel_id=1, source_target_pairs={{0,8},{1,9},{2,10},{3,11},{4,12},{5,13},{6,14},{7,15},{8,0},{9,1},... | collective-permute-start | bytes 786440 | tf_op jit(solution)/shard_map/ppermute | solution.py:57
  76.0 4.3 %collective-permute-start.23 = (f32[1,2048]{1,0:T(1,128)S(1)}, f32[1,2048]{1,0:T(1,128)S(1)}, u32[]{:S(2)}, u32[]{:S(2)}) collective-permute-start(f32[1,2048]{1,0:T(1,128)S(1)} %join_cores.4.refs_2_), channel_id=1, source_target_pairs={{0,4},{1,5},{2,6},{3,7},{4,0},{5,1},{6,2},{7,3},{8,12},{9,13},{10,... | collective-permute-start | bytes 24584 | tf_op jit(solution)/shard_map/ppermute | solution.py:57
  86.4 5.2 %collective-permute-start.27 = (f32[1,2048]{1,0:T(1,128)S(1)}, f32[1,2048]{1,0:T(1,128)S(1)}, u32[]{:S(2)}, u32[]{:S(2)}) collective-permute-start(f32[1,2048]{1,0:T(1,128)S(1)} %join_cores.5.refs_2_), channel_id=1, source_target_pairs={{0,4},{1,5},{2,6},{3,7},{4,0},{5,1},{6,2},{7,3},{8,12},{9,13},{10,... | collective-permute-start | bytes 24584 | tf_op jit(solution)/shard_map/ppermute | solution.py:57
  87.5 4.2 %collective-permute-start.29 = (f32[1,2048]{1,0:T(1,128)S(1)}, f32[1,2048]{1,0:T(1,128)S(1)}, u32[]{:S(2)}, u32[]{:S(2)}) collective-permute-start(f32[1,2048]{1,0:T(1,128)S(1)} %collective-permute-done.28.refs_4_), channel_id=1, source_target_pairs={{0,8},{1,9},{2,10},{3,11},{4,12},{5,13},{6,14},{7,15},{8,0},{9,1},... | collective-permute-start | bytes 24584 | tf_op jit(solution)/shard_map/ppermute | solution.py:57
  98.2 16.5 %collective-permute-start.31 = (bf16[512,256]{1,0:T(8,128)(2,1)S(1)}, bf16[512,256]{1,0:T(8,128)(2,1)S(1)}, u32[]{:S(2)}, u32[]{:S(2)}) collective-permute-start(bf16[512,256]{1,0:T(8,128)(2,1)S(1)} %combine.8.refs_4_), channel_id=1, source_target_pairs={{0,2},{1,3},{2,4},{3,5},{4,6},{5,7},{6,0},{7,1},{8,10},{9,11},{10,... | collective-permute-start | bytes 786440 | tf_op jit(solution)/shard_map/ppermute | solution.py:57
  98.4 15.2 %collective-permute-start.39 = (bf16[528,256]{1,0:T(8,128)(2,1)S(1)}, bf16[528,256]{1,0:T(8,128)(2,1)S(1)}, u32[]{:S(2)}, u32[]{:S(2)}) collective-permute-start(bf16[528,256]{1,0:T(8,128)(2,1)S(1)} %combine.9.refs_5_), channel_id=1, source_target_pairs={{0,2},{1,3},{2,4},{3,5},{4,6},{5,7},{6,0},{7,1},{8,10},{9,11},{10,... | collective-permute-start | bytes 811016 | tf_op jit(solution)/shard_map/ppermute | solution.py:57
  99.9 5.4 %collective-permute-start.40 = (bf16[528,256]{1,0:T(8,128)(2,1)S(1)}, bf16[528,256]{1,0:T(8,128)(2,1)S(1)}, u32[]{:S(2)}, u32[]{:S(2)}) collective-permute-start(bf16[528,256]{1,0:T(8,128)(2,1)S(1)} %get-tuple-element.73), channel_id=1, source_target_pairs={{0,8},{1,9},{2,10},{3,11},{4,12},{5,13},{6,14},{7,15},{8,0},{9,1},... | collective-permute-start | bytes 811016 | tf_op jit(solution)/shard_map/ppermute | solution.py:57
  101.7 14.4 %collective-permute-start.44 = (bf16[528,256]{1,0:T(8,128)(2,1)S(1)}, bf16[528,256]{1,0:T(8,128)(2,1)S(1)}, u32[]{:S(2)}, u32[]{:S(2)}) collective-permute-start(bf16[528,256]{1,0:T(8,128)(2,1)S(1)} %get-tuple-element.77), channel_id=1, source_target_pairs={{0,8},{1,9},{2,10},{3,11},{4,12},{5,13},{6,14},{7,15},{8,0},{9,1},... | collective-permute-start | bytes 811016 | tf_op jit(solution)/shard_map/ppermute | solution.py:57
  102.7 13.1 %collective-permute-start.33 = (bf16[512,256]{1,0:T(8,128)(2,1)S(1)}, bf16[512,256]{1,0:T(8,128)(2,1)S(1)}, u32[]{:S(2)}, u32[]{:S(2)}) collective-permute-start(bf16[512,256]{1,0:T(8,128)(2,1)S(1)} %get-tuple-element.66), channel_id=1, source_target_pairs={{0,8},{1,9},{2,10},{3,11},{4,12},{5,13},{6,14},{7,15},{8,0},{9,1},... | collective-permute-start | bytes 786440 | tf_op jit(solution)/shard_map/ppermute | solution.py:57
  105.3 10.9 %collective-permute-start.42 = (bf16[528,256]{1,0:T(8,128)(2,1)S(1)}, bf16[528,256]{1,0:T(8,128)(2,1)S(1)}, u32[]{:S(2)}, u32[]{:S(2)}) collective-permute-start(bf16[528,256]{1,0:T(8,128)(2,1)S(1)} %get-tuple-element.75), channel_id=1, source_target_pairs={{0,8},{1,9},{2,10},{3,11},{4,12},{5,13},{6,14},{7,15},{8,0},{9,1},... | collective-permute-start | bytes 811016 | tf_op jit(solution)/shard_map/ppermute | solution.py:57
  113.7 8.8 %collective-permute-start.41 = (bf16[528,256]{1,0:T(8,128)(2,1)S(1)}, bf16[528,256]{1,0:T(8,128)(2,1)S(1)}, u32[]{:S(2)}, u32[]{:S(2)}) collective-permute-start(bf16[528,256]{1,0:T(8,128)(2,1)S(1)} %combine.13), channel_id=1, source_target_pairs={{0,2},{1,3},{2,4},{3,5},{4,6},{5,7},{6,0},{7,1},{8,10},{9,11},{10,... | collective-permute-start | bytes 811016 | tf_op jit(solution)/shard_map/ppermute | solution.py:57
  114.7 10.9 %collective-permute-start.37 = (bf16[512,256]{1,0:T(8,128)(2,1)S(1)}, bf16[512,256]{1,0:T(8,128)(2,1)S(1)}, u32[]{:S(2)}, u32[]{:S(2)}) collective-permute-start(bf16[512,256]{1,0:T(8,128)(2,1)S(1)} %get-tuple-element.70), channel_id=1, source_target_pairs={{0,8},{1,9},{2,10},{3,11},{4,12},{5,13},{6,14},{7,15},{8,0},{9,1},... | collective-permute-start | bytes 786440 | tf_op jit(solution)/shard_map/ppermute | solution.py:57
  115.9 14.1 %collective-permute-start.35 = (bf16[512,256]{1,0:T(8,128)(2,1)S(1)}, bf16[512,256]{1,0:T(8,128)(2,1)S(1)}, u32[]{:S(2)}, u32[]{:S(2)}) collective-permute-start(bf16[512,256]{1,0:T(8,128)(2,1)S(1)} %get-tuple-element.68), channel_id=1, source_target_pairs={{0,8},{1,9},{2,10},{3,11},{4,12},{5,13},{6,14},{7,15},{8,0},{9,1},... | collective-permute-start | bytes 786440 | tf_op jit(solution)/shard_map/ppermute | solution.py:57
  116.0 14.0 %collective-permute-start.34 = (bf16[512,256]{1,0:T(8,128)(2,1)S(1)}, bf16[512,256]{1,0:T(8,128)(2,1)S(1)}, u32[]{:S(2)}, u32[]{:S(2)}) collective-permute-start(bf16[512,256]{1,0:T(8,128)(2,1)S(1)} %combine.10), channel_id=1, source_target_pairs={{0,2},{1,3},{2,4},{3,5},{4,6},{5,7},{6,0},{7,1},{8,10},{9,11},{10,... | collective-permute-start | bytes 786440 | tf_op jit(solution)/shard_map/ppermute | solution.py:57
  116.2 19.6 %collective-permute-start.45 = (bf16[528,256]{1,0:T(8,128)(2,1)S(1)}, bf16[528,256]{1,0:T(8,128)(2,1)S(1)}, u32[]{:S(2)}, u32[]{:S(2)}) collective-permute-start(bf16[528,256]{1,0:T(8,128)(2,1)S(1)} %combine.15), channel_id=1, source_target_pairs={{0,0},{1,8},{2,2},{3,10},{4,4},{5,12},{6,6},{7,14},{8,1},{9,9},{10... | collective-permute-start | bytes 811016 | tf_op jit(solution)/shard_map/ppermute | solution.py:57
  122.6 19.9 %collective-permute-start.43 = (bf16[528,256]{1,0:T(8,128)(2,1)S(1)}, bf16[528,256]{1,0:T(8,128)(2,1)S(1)}, u32[]{:S(2)}, u32[]{:S(2)}) collective-permute-start(bf16[528,256]{1,0:T(8,128)(2,1)S(1)} %combine.14), channel_id=1, source_target_pairs={{0,2},{1,10},{2,4},{3,12},{4,6},{5,14},{6,0},{7,8},{8,3},{9,11},{1... | collective-permute-start | bytes 811016 | tf_op jit(solution)/shard_map/ppermute | solution.py:57
  125.7 10.1 %collective-permute-start.38 = (bf16[512,256]{1,0:T(8,128)(2,1)S(1)}, bf16[512,256]{1,0:T(8,128)(2,1)S(1)}, u32[]{:S(2)}, u32[]{:S(2)}) collective-permute-start(bf16[512,256]{1,0:T(8,128)(2,1)S(1)} %combine.12), channel_id=1, source_target_pairs={{0,0},{1,8},{2,2},{3,10},{4,4},{5,12},{6,6},{7,14},{8,1},{9,9},{10... | collective-permute-start | bytes 786440 | tf_op jit(solution)/shard_map/ppermute | solution.py:57
  130.1 12.3 %collective-permute-start.36 = (bf16[512,256]{1,0:T(8,128)(2,1)S(1)}, bf16[512,256]{1,0:T(8,128)(2,1)S(1)}, u32[]{:S(2)}, u32[]{:S(2)}) collective-permute-start(bf16[512,256]{1,0:T(8,128)(2,1)S(1)} %combine.11), channel_id=1, source_target_pairs={{0,2},{1,10},{2,4},{3,12},{4,6},{5,14},{6,0},{7,8},{8,3},{9,11},{1... | collective-permute-start | bytes 786440 | tf_op jit(solution)/shard_map/ppermute | solution.py:57
  (17 other events, 68.8 us)

commit v3 on v2

--- a/solution.py
+++ b/solution.py
@@ -57,6 +57,11 @@
     return lax.ppermute(value, AXES, route)
 
 
+BRIEF = pl.CostEstimate(flops=1, bytes_accessed=1, transcendentals=0)
+TURN = pl.CostEstimate(flops=6 * 10**9, bytes_accessed=1, transcendentals=0)
+WAIT = pl.CostEstimate(flops=2 * 10**10, bytes_accessed=0, transcendentals=0)
+
+
 def call(kernel, outs, args, after=(), specs=None, alias=None, out_specs=None, **kwargs):
     args, after = list(args), list(after)
 
@@ -80,10 +85,7 @@
     )
 
 
-WAIT = pl.CostEstimate(flops=2 * 10**10, bytes_accessed=0, transcendentals=0)
-
-
-def tie(values, after):
+def tie(values, after, hint=WAIT):
     values, after = list(values), list(after)
     return pl.pallas_call(
         lambda *refs: None,
@@ -92,7 +94,7 @@
         out_specs=(HELD,) * len(values),
         input_output_aliases={j: j for j in range(len(values))},
         compiler_params=PARAMS,
-        cost_estimate=WAIT,
+        cost_estimate=hint,
         name="tie",
     )(*values, *after)
 
@@ -267,7 +269,7 @@
         scale_ref, mass_ref, *outs = refs
         scaled_ref = turned_ref
     width = outs[0].shape[1]
-    step = min(256, height)
+    step = height if height <= 384 else height // 2
     at = pl.ds(chunk * 2 * width, 2 * width)
     for i in range(height // step):
         part = lax.dot_general(
@@ -311,16 +313,17 @@
         out_ref[height : height + extra, :] = high_low(mass_of(refs[:-1], height), extra)
 
 
-def finish_kernel(*refs, height):
+def finish_kernel(*refs, heights):
     out_ref, mass_ref = refs[-2:]
     terms = refs[:-2]
-    parts = len(terms) // 2
-    mass = mass_of(terms[2 * parts - 2 :], height)
+    mass = mass_of(terms[-2:], heights[-1])
     mass_ref[...] = mass
     inverse = 1.0 / mass
-    for j in range(parts):
+    start = 0
+    for j, height in enumerate(heights):
         total = total_of(terms[2 * j : 2 * j + 2], height)
-        out_ref[:, pl.ds(j * height, height)] = (total * inverse).T
+        out_ref[:, pl.ds(start, height)] = (total * inverse).T
+        start += height
 
 
 def body(embeddings, level_one, centroids):
@@ -429,8 +432,9 @@
         (part,) = sweep(part, last=False)
     mass_part, row_scale, column_scale = sweep(part, last=True)
 
-    height = depth // parts
-    tall = [height] * (parts - 1) + [height + 16]
+    heights = [depth * 4 // 8, depth - depth * 4 // 8]
+    starts = [0, heights[0]]
+    tall = [heights[0], heights[1] + 16]
 
     def numerator(s, j, after):
         fresh = scaled[j] is None
@@ -438,47 +442,68 @@
         args = [*args, column_scale, mass_part]
         outs = (shape(tall[j], owned),) * 2
         if fresh:
-            outs = (shape(height, slots), *outs)
+            outs = (shape(heights[j], slots), *outs)
         outs = call(
             functools.partial(
-                numerator_kernel, chunk=s, first=j * height, height=height, fresh=fresh
+                numerator_kernel, chunk=s, first=starts[j], height=heights[j], fresh=fresh
             ),
             outs,
             args,
             after=after,
             name="numerator",
-            cost_estimate=cost(height, 2 * owned, slots),
+            cost_estimate=cost(heights[j], 2 * owned, slots),
         )
         if fresh:
             scaled[j] = outs[0]
         return outs[-2], outs[-1]
 
-    def combine(j, *terms):
+    def combine(j, terms, after=()):
         return call(
-            functools.partial(combine_kernel, height=height),
+            functools.partial(combine_kernel, height=heights[j]),
             shape(tall[j], owned),
             terms,
+            after=after,
             name="combine",
+            cost_estimate=BRIEF if j else TURN,
         )
 
     scaled = [None] * parts
-    after, moving, kept = (), [()] * parts, []
-    for s in [*range(1, ring), 0]:
-        route = routes.swap if s == 0 else routes.home if s == ring - 1 else routes.shift[1]
-        pairs = []
+    first, *others = [*range(1, ring), 0]
+    pairs, moving, kept = {}, [()] * parts, [()] * parts
+
+    def sums_of(s, after):
         for j in range(parts):
             kept_part, sent_part = numerator(s, j, after)
-            pairs.append((kept_part, send(sent_part, routes.core)))
-        if s == 0:
-            kept = [send(combine(j, *pairs[j]), route) for j in range(parts)]
-            continue
-        added = [combine(j, *moving[j], *pairs[j]) for j in range(parts)]
-        if s == 1:
-            after = tuple(added)
-        moving = [(send(a, route),) for a in added]
-
+            pairs[s, j] = (kept_part, send(sent_part, routes.core))
+            if s == first:
+                after = (kept_part,)
+
+    def step(s, after):
+        route = routes.home if s == ring - 1 else routes.shift[1]
+        made = []
+        for j in range(parts):
+            added = combine(j, (*moving[j], *pairs[s, j]), after)
+            moving[j] = (send(added, route),)
+            made.append(added)
+            if s != first:
+                after = (added,)
+        return tuple(made)
+
+    sums_of(first, ())
+    after = step(first, ())
+    for s in others:
+        sums_of(s, after)
+    after = tuple(pairs[s, j][0] for s in others for j in range(parts))
+    for s in others[:-1]:
+        after = step(s, after)
+        if s == others[0]:
+            for j in range(parts):
+                kept[j] = send(combine(j, pairs[0, j], after), routes.swap)
+
+    (arrived_first,) = tie(moving[0], (), TURN)
+    moving[0] = (arrived_first,)
     updated, mass = call(
-        functools.partial(finish_kernel, height=height),
+        functools.partial(finish_kernel, heights=heights),
         (shape(owned, depth, dtype=F32), shape(1, owned, dtype=F32)),
         [t for j in range(parts) for t in (moving[j][0], kept[j])],
         name="finish",

time: 144 us -> 139 us (0.965)
  waiting for transfers between devices: 62.3 us -> 59.6 us
  starting transfers between devices: 47.1 us -> 44.8 us
    ppermute x46, waiting for transfers between devices: 62.3 us -> 59.6 us  [send(): return lax.ppermute(value, AXES, route)]
    ppermute x46, starting transfers between devices: 47.1 us -> 44.8 us  [send(): return lax.ppermute(value, AXES, route)]
  transfers between devices with their start and end apart: 46 -> 46, of which waited for: 22 -> 24; matrix products, arithmetic and copies ran while one was open for 0% -> 0% of each run, Pallas kernels for 13% -> 14%
where the time goes in v3:
time: 139 us
  waiting for transfers between devices  59.6 us (43%)
  starting transfers between devices  44.8 us (32%)
  Pallas kernels  31.2 us (22%)
  local copies, waits for them, and re-layouts  2.09 us (2%)
    ppermute x46, waiting for transfers between devices, send(): return lax.ppermute(value, AXES, route)  59.6 us
    ppermute x46, starting transfers between devices, send(): return lax.ppermute(value, AXES, route)  44.8 us
    pallas_call x33, Pallas kernels, call(): pl.pallas_call(ordered, out_shape=outs, in_specs=(specs or [VMEM] * len(a...  31.2 us
  transfers between devices with their start and end apart: 46, of which 24 were waited for; matrix products, arithmetic and copies ran while one was open for 0% of the time, Pallas kernels for 14%

profile of v3, /device:TPU:1, one launch (start us, length us, event | category | flops | bytes accessed | tf_op | source)
XLA Modules:
  0.0 138.6 jit_solution(1878443748167678245)
XLA Ops:
  0.6 4.5 %collective-permute-start.3 = (bf16[256,1024]{1,0:T(8,128)(2,1)}, bf16[256,1024]{1,0:T(8,128)(2,1)S(1)}, u32[]{:S(2)}, u32[]{:S(2)}) collective-permute-start(bf16[256,1024]{1,0:T(8,128)(2,1)} %param.5), channel_id=1, source_target_pairs={{0,0},{1,8},{2,2},{3,10},{4,4},{5,12},{6,6},{7,14},{8,1},{9,9},{10... | collective-permute-start | bytes 1572872 | tf_op jit(solution)/shard_map/ppermute | solution.py:57
  6.1 1.4 %copy-done = bf16[768,1024]{1,0:T(8,128)(2,1)S(1)} copy-done((bf16[768,1024]{1,0:T(8,128)(2,1)S(1)}, bf16[768,1024]{1,0:T(8,128)(2,1)}, u32[]{:S(2)}) %copy-start) | copy-done | bytes 1572888
  10.1 2.1 %collective-permute-done.3.refs_0_ = bf16[256,1024]{1,0:T(8,128)(2,1)S(1)} collective-permute-done((bf16[256,1024]{1,0:T(8,128)(2,1)}, bf16[256,1024]{1,0:T(8,128)(2,1)S(1)}, u32[]{:S(2)}, u32[]{:S(2)}) %collective-permute-start.3) | collective-permute-done | bytes 524320 | tf_op jit(solution)/shard_map/ppermute | solution.py:57
  12.4 1.3 collective-permute-start.6
  16.3 6.4 %collective-permute-done.6.refs_5_.refs_11_ = bf16[128,1024]{1,0:T(8,128)(2,1)S(1)} collective-permute-done((bf16[128,1024]{1,0:T(8,128)(2,1)S(1)}, bf16[128,1024]{1,0:T(8,128)(2,1)S(1)}, u32[]{:S(2)}, u32[]{:S(2)}) %collective-permute-start.6) | collective-permute-done | bytes 262176 | tf_op jit(solution)/shard_map/ppermute | solution.py:57
  22.7 4.0 %collective-permute-done.7.refs_6_.refs_12_ = bf16[128,1024]{1,0:T(8,128)(2,1)S(1)} collective-permute-done((bf16[128,1024]{1,0:T(8,128)(2,1)S(1)}, bf16[128,1024]{1,0:T(8,128)(2,1)S(1)}, u32[]{:S(2)}, u32[]{:S(2)}) %collective-permute-start.7) | collective-permute-done | bytes 262176 | tf_op jit(solution)/shard_map/ppermute | solution.py:57
  26.7 1.5 %collective-permute-done.5.refs_4_.refs_10_ = bf16[128,1024]{1,0:T(8,128)(2,1)S(1)} collective-permute-done((bf16[128,1024]{1,0:T(8,128)(2,1)S(1)}, bf16[128,1024]{1,0:T(8,128)(2,1)S(1)}, u32[]{:S(2)}, u32[]{:S(2)}) %collective-permute-start.5) | collective-permute-done | bytes 262176 | tf_op jit(solution)/shard_map/ppermute | solution.py:57
  28.2 1.5 %collective-permute-done.refs_0_ = bf16[384,1024]{1,0:T(8,128)(2,1)S(1)} collective-permute-done((bf16[384,1024]{1,0:T(8,128)(2,1)S(1)}, bf16[384,1024]{1,0:T(8,128)(2,1)S(1)}, u32[]{:S(2)}, u32[]{:S(2)}) %collective-permute-start) | collective-permute-done | bytes 786464 | tf_op jit(solution)/shard_map/ppermute | solution.py:57
  29.7 6.1 %collective-permute-done.10.refs_9_.refs_15_ = bf16[128,1024]{1,0:T(8,128)(2,1)S(1)} collective-permute-done((bf16[128,1024]{1,0:T(8,128)(2,1)S(1)}, bf16[128,1024]{1,0:T(8,128)(2,1)S(1)}, u32[]{:S(2)}, u32[]{:S(2)}) %collective-permute-start.10) | collective-permute-done | bytes 262176 | tf_op jit(solution)/shard_map/ppermute | solution.py:57
  35.8 5.6 %collective-permute-done.11.refs_10_.refs_16_ = bf16[128,1024]{1,0:T(8,128)(2,1)S(1)} collective-permute-done((bf16[128,1024]{1,0:T(8,128)(2,1)S(1)}, bf16[128,1024]{1,0:T(8,128)(2,1)S(1)}, u32[]{:S(2)}, u32[]{:S(2)}) %collective-permute-start.11) | collective-permute-done | bytes 262176 | tf_op jit(solution)/shard_map/ppermute | solution.py:57
  42.3 4.9 %collective-permute-done.2.refs_2_ = bf16[384,1024]{1,0:T(8,128)(2,1)S(1)} collective-permute-done((bf16[384,1024]{1,0:T(8,128)(2,1)S(1)}, bf16[384,1024]{1,0:T(8,128)(2,1)S(1)}, u32[]{:S(2)}, u32[]{:S(2)}) %collective-permute-start.2) | collective-permute-done | bytes 786464 | tf_op jit(solution)/shard_map/ppermute | solution.py:57
  47.8 4.4 %collective-permute-start.12 = (bf16[128,1024]{1,0:T(8,128)(2,1)S(1)}, bf16[128,1024]{1,0:T(8,128)(2,1)S(1)}, u32[]{:S(2)}, u32[]{:S(2)}) collective-permute-start(bf16[128,1024]{1,0:T(8,128)(2,1)S(1)} %collective-permute-done.10.refs_9_.refs_15_), channel_id=1, source_target_pairs={{0,8},{1,9},{2,10},{3,11},{4,12},{5,13},{6,14},{7,15},{8,0},{9,1},... | collective-permute-start | bytes 786440 | tf_op jit(solution)/shard_map/ppermute | solution.py:57
  52.7 1.3 collective-permute-start.17
  54.1 1.8 %weights.3 = (bf16[1536,1024]{1,0:T(8,128)(2,1)S(1)}, f32[1,1536]{1,0:T(1,128)S(1)}, bf16[1536,2048]{1,0:T(8,128)(2,1)S(1)}, f32[1,2048]{1,0:T(1,128)S(1)}) custom-call(bf16[384,1024]{1,0:T(8,128)(2,1)S(1)} %pick_rows.7.refs_0_, bf16[128,1024]{1,0:T(8,128)(2,1)S(1)} %get-tuple-element.44.refs_1_.refs_7_, ...), custom_call_target="tpu_custom_call" | custom-call | tf_op jit(solution)/shard_map/weights/pallas_call | solution.py:71
  55.9 5.1 %weights.4 = (bf16[1536,1024]{1,0:T(8,128)(2,1)S(1)}, f32[1,1536]{1,0:T(1,128)S(1)}, bf16[1536,2048]{1,0:T(8,128)(2,1)S(1)}, f32[1,2048]{1,0:T(1,128)S(1)}) custom-call(bf16[1536,1024]{1,0:T(8,128)(2,1)S(1)} %get-tuple-element.46.refs_0_, ...), custom_call_target="tpu_custom_call", output_to_operand_aliasing={{0}: (0, {}), {1}: (1, {}), {2}: (2, {}), {3}: (3, {})} | custom-call | tf_op jit(solution)/shard_map/weights/pallas_call | solution.py:71
  61.0 2.0 %weights.5 = (bf16[1536,1024]{1,0:T(8,128)(2,1)S(1)}, f32[1,1536]{1,0:T(1,128)S(1)}, bf16[1536,2048]{1,0:T(8,128)(2,1)S(1)}, f32[1,2048]{1,0:T(1,128)S(1)}) custom-call(bf16[1536,1024]{1,0:T(8,128)(2,1)S(1)} %get-tuple-element.50.refs_0_, ...), custom_call_target="tpu_custom_call", output_to_operand_aliasing={{0}: (0, {}), {1}: (1, {}), {2}: (2, {}), {3}: (3, {})} | custom-call | tf_op jit(solution)/shard_map/weights/pallas_call | solution.py:71
  64.3 1.6 %collective-permute-start.20 = (f32[1,2048]{1,0:T(1,128)S(1)}, f32[1,2048]{1,0:T(1,128)S(1)}, u32[]{:S(2)}, u32[]{:S(2)}) collective-permute-start(f32[1,2048]{1,0:T(1,128)S(1)} %join_cores.3.refs_2_), channel_id=1, source_target_pairs={{0,2},{1,3},{2,4},{3,5},{4,6},{5,7},{6,0},{7,1},{8,14},{9,15},{10,... | collective-permute-start | bytes 24584 | tf_op jit(solution)/shard_map/ppermute | solution.py:57
  66.8 3.1 %collective-permute-start.21 = (f32[1,2048]{1,0:T(1,128)S(1)}, f32[1,2048]{1,0:T(1,128)S(1)}, u32[]{:S(2)}, u32[]{:S(2)}) collective-permute-start(f32[1,2048]{1,0:T(1,128)S(1)} %collective-permute-done.20.refs_4_), channel_id=1, source_target_pairs={{0,8},{1,9},{2,10},{3,11},{4,12},{5,13},{6,14},{7,15},{8,0},{9,1},... | collective-permute-start | bytes 24584 | tf_op jit(solution)/shard_map/ppermute | solution.py:57
  70.7 2.6 %sweep.2.refs_0_ = f32[1,2048]{1,0:T(1,128)S(1)} custom-call(f32[1,1536]{1,0:T(1,128)S(1)} %get-tuple-element.55.refs_0_, bf16[1536,2048]{1,0:T(8,128)(2,1)S(1)} %get-tuple-element.54.refs_1_, f32[1,2048]{1,0:T(1,128)S(1)} %join_cores.3.refs_2_, f32[1,2048]{1,0:T(1,128)S(1)} %collective-permute-done.19.refs_3_, ...), custom_call_target="tpu_custom_call" | custom-call | tf_op jit(solution)/shard_map/sweep/pallas_call | solution.py:71
  74.5 1.5 %collective-permute-start.24 = (f32[1,2048]{1,0:T(1,128)S(1)}, f32[1,2048]{1,0:T(1,128)S(1)}, u32[]{:S(2)}, u32[]{:S(2)}) collective-permute-start(f32[1,2048]{1,0:T(1,128)S(1)} %join_cores.4.refs_2_), channel_id=1, source_target_pairs={{0,2},{1,3},{2,4},{3,5},{4,6},{5,7},{6,0},{7,1},{8,14},{9,15},{10,... | collective-permute-start | bytes 24584 | tf_op jit(solution)/shard_map/ppermute | solution.py:57
  77.0 3.3 %collective-permute-start.25 = (f32[1,2048]{1,0:T(1,128)S(1)}, f32[1,2048]{1,0:T(1,128)S(1)}, u32[]{:S(2)}, u32[]{:S(2)}) collective-permute-start(f32[1,2048]{1,0:T(1,128)S(1)} %collective-permute-done.24.refs_4_), channel_id=1, source_target_pairs={{0,8},{1,9},{2,10},{3,11},{4,12},{5,13},{6,14},{7,15},{8,0},{9,1},... | collective-permute-start | bytes 24584 | tf_op jit(solution)/shard_map/ppermute | solution.py:57
  81.1 2.6 %sweep.3.refs_0_ = f32[1,2048]{1,0:T(1,128)S(1)} custom-call(f32[1,1536]{1,0:T(1,128)S(1)} %get-tuple-element.55.refs_0_, bf16[1536,2048]{1,0:T(8,128)(2,1)S(1)} %get-tuple-element.54.refs_1_, f32[1,2048]{1,0:T(1,128)S(1)} %join_cores.4.refs_2_, f32[1,2048]{1,0:T(1,128)S(1)} %collective-permute-done.23.refs_3_, ...), custom_call_target="tpu_custom_call" | custom-call | tf_op jit(solution)/shard_map/sweep/pallas_call | solution.py:71
  85.0 1.5 %collective-permute-start.28 = (f32[1,2048]{1,0:T(1,128)S(1)}, f32[1,2048]{1,0:T(1,128)S(1)}, u32[]{:S(2)}, u32[]{:S(2)}) collective-permute-start(f32[1,2048]{1,0:T(1,128)S(1)} %join_cores.5.refs_2_), channel_id=1, source_target_pairs={{0,2},{1,3},{2,4},{3,5},{4,6},{5,7},{6,0},{7,1},{8,14},{9,15},{10,... | collective-permute-start | bytes 24584 | tf_op jit(solution)/shard_map/ppermute | solution.py:57
  87.5 3.3 %collective-permute-start.29 = (f32[1,2048]{1,0:T(1,128)S(1)}, f32[1,2048]{1,0:T(1,128)S(1)}, u32[]{:S(2)}, u32[]{:S(2)}) collective-permute-start(f32[1,2048]{1,0:T(1,128)S(1)} %collective-permute-done.28.refs_4_), channel_id=1, source_target_pairs={{0,8},{1,9},{2,10},{3,11},{4,12},{5,13},{6,14},{7,15},{8,0},{9,1},... | collective-permute-start | bytes 24584 | tf_op jit(solution)/shard_map/ppermute | solution.py:57
  91.6 2.6 %last_sweep.1 = (f32[1,2048]{1,0:T(1,128)S(1)}, f32[1,1536]{1,0:T(1,128)S(1)}, f32[1,2048]{1,0:T(1,128)S(1)}) custom-call(f32[1,1536]{1,0:T(1,128)S(1)} %get-tuple-element.55.refs_0_, bf16[1536,2048]{1,0:T(8,128)(2,1)S(1)} %get-tuple-element.54.refs_1_, f32[1,2048]{1,0:T(1,128)S(1)} %join_cores.5.refs_2_, f32[1,2048]{1,0:T(1,128)S(1)} %collective-permute-done.27.refs_3_, ...), custom_call_target="tpu_custom_call" | custom-call | tf_op jit(solution)/shard_map/last_sweep/pallas_call | solution.py:71
  105.1 1.5 %collective-permute-done.31.refs_0_ = bf16[512,256]{1,0:T(8,128)(2,1)S(1)} collective-permute-done((bf16[512,256]{1,0:T(8,128)(2,1)S(1)}, bf16[512,256]{1,0:T(8,128)(2,1)S(1)}, u32[]{:S(2)}, u32[]{:S(2)}) %collective-permute-start.31) | collective-permute-done | bytes 262176 | tf_op jit(solution)/shard_map/ppermute | solution.py:57
  106.6 1.8 %collective-permute-start.35 = (bf16[512,256]{1,0:T(8,128)(2,1)S(1)}, bf16[512,256]{1,0:T(8,128)(2,1)S(1)}, u32[]{:S(2)}, u32[]{:S(2)}) collective-permute-start(bf16[512,256]{1,0:T(8,128)(2,1)S(1)} %get-tuple-element.73), channel_id=1, source_target_pairs={{0,8},{1,9},{2,10},{3,11},{4,12},{5,13},{6,14},{7,15},{8,0},{9,1},... | collective-permute-start | bytes 786440 | tf_op jit(solution)/shard_map/ppermute | solution.py:57
  108.7 3.8 %collective-permute-done.36.refs_0_ = bf16[528,256]{1,0:T(8,128)(2,1)S(1)} collective-permute-done((bf16[528,256]{1,0:T(8,128)(2,1)S(1)}, bf16[528,256]{1,0:T(8,128)(2,1)S(1)}, u32[]{:S(2)}, u32[]{:S(2)}) %collective-permute-start.36) | collective-permute-done | bytes 270368 | tf_op jit(solution)/shard_map/ppermute | solution.py:57
  113.8 3.7 %collective-permute-start.45 = (bf16[528,256]{1,0:T(8,128)(2,1)S(1)}, bf16[528,256]{1,0:T(8,128)(2,1)S(1)}, u32[]{:S(2)}, u32[]{:S(2)}) collective-permute-start(bf16[528,256]{1,0:T(8,128)(2,1)S(1)} %combine.15), channel_id=1, source_target_pairs={{0,0},{1,8},{2,2},{3,10},{4,4},{5,12},{6,6},{7,14},{8,1},{9,9},{10... | collective-permute-start | bytes 811016 | tf_op jit(solution)/shard_map/ppermute | solution.py:57
  119.3 4.2 %collective-permute-start.40 = (bf16[512,256]{1,0:T(8,128)(2,1)S(1)}, bf16[512,256]{1,0:T(8,128)(2,1)S(1)}, u32[]{:S(2)}, u32[]{:S(2)}) collective-permute-start(bf16[512,256]{1,0:T(8,128)(2,1)S(1)} %combine.13), channel_id=1, source_target_pairs={{0,0},{1,8},{2,2},{3,10},{4,4},{5,12},{6,6},{7,14},{8,1},{9,9},{10... | collective-permute-start | bytes 786440 | tf_op jit(solution)/shard_map/ppermute | solution.py:57
  125.0 6.9 %collective-permute-done.38.refs_0_ = bf16[512,256]{1,0:T(8,128)(2,1)S(1)} collective-permute-done((bf16[512,256]{1,0:T(8,128)(2,1)S(1)}, bf16[512,256]{1,0:T(8,128)(2,1)S(1)}, u32[]{:S(2)}, u32[]{:S(2)}) %collective-permute-start.38) | collective-permute-done | bytes 262176 | tf_op jit(solution)/shard_map/ppermute | solution.py:57
  131.9 5.4 %collective-permute-done.43.refs_2_ = bf16[528,256]{1,0:T(8,128)(2,1)S(1)} collective-permute-done((bf16[528,256]{1,0:T(8,128)(2,1)S(1)}, bf16[528,256]{1,0:T(8,128)(2,1)S(1)}, u32[]{:S(2)}, u32[]{:S(2)}) %collective-permute-start.43) | collective-permute-done | bytes 270368 | tf_op jit(solution)/shard_map/ppermute | solution.py:57
  (101 shorter events, 34.2 us)
Async XLA Ops:
  0.6 11.6 %collective-permute-start.3 = (bf16[256,1024]{1,0:T(8,128)(2,1)}, bf16[256,1024]{1,0:T(8,128)(2,1)S(1)}, u32[]{:S(2)}, u32[]{:S(2)}) collective-permute-start(bf16[256,1024]{1,0:T(8,128)(2,1)} %param.5), channel_id=1, source_target_pairs={{0,0},{1,8},{2,2},{3,10},{4,4},{5,12},{6,6},{7,14},{8,1},{9,9},{10... | collective-permute-start | bytes 1572872 | tf_op jit(solution)/shard_map/ppermute | solution.py:57
  10.0 19.7 %collective-permute-start = (bf16[384,1024]{1,0:T(8,128)(2,1)S(1)}, bf16[384,1024]{1,0:T(8,128)(2,1)S(1)}, u32[]{:S(2)}, u32[]{:S(2)}) collective-permute-start(bf16[384,1024]{1,0:T(8,128)(2,1)S(1)} %pick_rows.6.refs_2_), channel_id=1, source_target_pairs={{0,1},{1,0},{2,3},{3,2},{4,5},{5,4},{6,7},{7,6},{8,9},{9,8},{10,11... | collective-permute-start | bytes 2359304 | tf_op jit(solution)/shard_map/ppermute | solution.py:57
  12.4 10.3 %collective-permute-start.6 = (bf16[128,1024]{1,0:T(8,128)(2,1)S(1)}, bf16[128,1024]{1,0:T(8,128)(2,1)S(1)}, u32[]{:S(2)}, u32[]{:S(2)}) collective-permute-start(bf16[128,1024]{1,0:T(8,128)(2,1)S(1)} %get-tuple-element.44.refs_1_.refs_7_), channel_id=1, source_target_pairs={{0,2},{1,3},{2,4},{3,5},{4,6},{5,7},{6,0},{7,1},{8,10},{9,11},{10,... | collective-permute-start | bytes 786440 | tf_op jit(solution)/shard_map/ppermute | solution.py:57
  13.8 12.9 %collective-permute-start.7 = (bf16[128,1024]{1,0:T(8,128)(2,1)S(1)}, bf16[128,1024]{1,0:T(8,128)(2,1)S(1)}, u32[]{:S(2)}, u32[]{:S(2)}) collective-permute-start(bf16[128,1024]{1,0:T(8,128)(2,1)S(1)} %get-tuple-element.45.refs_2_.refs_8_), channel_id=1, source_target_pairs={{0,2},{1,3},{2,4},{3,5},{4,6},{5,7},{6,0},{7,1},{8,10},{9,11},{10,... | collective-permute-start | bytes 786440 | tf_op jit(solution)/shard_map/ppermute | solution.py:57
  15.0 32.2 %collective-permute-start.2 = (bf16[384,1024]{1,0:T(8,128)(2,1)S(1)}, bf16[384,1024]{1,0:T(8,128)(2,1)S(1)}, u32[]{:S(2)}, u32[]{:S(2)}) collective-permute-start(bf16[384,1024]{1,0:T(8,128)(2,1)S(1)} %pick_rows.5.refs_2_), channel_id=1, source_target_pairs={{0,17},{1,16},{2,19},{3,18},{4,21},{5,20},{6,23},{7,22},{8,25},{9,... | collective-permute-start | bytes 2359304 | tf_op jit(solution)/shard_map/ppermute | solution.py:57
  15.4 32.4 %collective-permute-start.1 = (bf16[384,1024]{1,0:T(8,128)(2,1)S(1)}, bf16[384,1024]{1,0:T(8,128)(2,1)S(1)}, u32[]{:S(2)}, u32[]{:S(2)}) collective-permute-start(bf16[384,1024]{1,0:T(8,128)(2,1)S(1)} %pick_rows.4.refs_2_), channel_id=1, source_target_pairs={{0,16},{1,17},{2,18},{3,19},{4,20},{5,21},{6,22},{7,23},{8,24},{9,... | collective-permute-start | bytes 2359304 | tf_op jit(solution)/shard_map/ppermute | solution.py:57
  26.7 9.2 %collective-permute-start.10 = (bf16[128,1024]{1,0:T(8,128)(2,1)S(1)}, bf16[128,1024]{1,0:T(8,128)(2,1)S(1)}, u32[]{:S(2)}, u32[]{:S(2)}) collective-permute-start(bf16[128,1024]{1,0:T(8,128)(2,1)S(1)} %collective-permute-done.6.refs_5_.refs_11_), channel_id=1, source_target_pairs={{0,2},{1,3},{2,4},{3,5},{4,6},{5,7},{6,0},{7,1},{8,10},{9,11},{10,... | collective-permute-start | bytes 786440 | tf_op jit(solution)/shard_map/ppermute | solution.py:57
  28.2 13.2 %collective-permute-start.11 = (bf16[128,1024]{1,0:T(8,128)(2,1)S(1)}, bf16[128,1024]{1,0:T(8,128)(2,1)S(1)}, u32[]{:S(2)}, u32[]{:S(2)}) collective-permute-start(bf16[128,1024]{1,0:T(8,128)(2,1)S(1)} %collective-permute-done.7.refs_6_.refs_12_), channel_id=1, source_target_pairs={{0,2},{1,3},{2,4},{3,5},{4,6},{5,7},{6,0},{7,1},{8,10},{9,11},{10,... | collective-permute-start | bytes 786440 | tf_op jit(solution)/shard_map/ppermute | solution.py:57
  29.7 22.5 %collective-permute-start.8 = (bf16[128,1024]{1,0:T(8,128)(2,1)S(1)}, bf16[128,1024]{1,0:T(8,128)(2,1)S(1)}, u32[]{:S(2)}, u32[]{:S(2)}) collective-permute-start(bf16[128,1024]{1,0:T(8,128)(2,1)S(1)} %collective-permute-done.6.refs_5_.refs_11_), channel_id=1, source_target_pairs={{0,8},{1,9},{2,10},{3,11},{4,12},{5,13},{6,14},{7,15},{8,0},{9,1},... | collective-permute-start | bytes 786440 | tf_op jit(solution)/shard_map/ppermute | solution.py:57
  35.8 16.4 %collective-permute-start.14 = (bf16[128,1024]{1,0:T(8,128)(2,1)S(1)}, bf16[128,1024]{1,0:T(8,128)(2,1)S(1)}, u32[]{:S(2)}, u32[]{:S(2)}) collective-permute-start(bf16[128,1024]{1,0:T(8,128)(2,1)S(1)} %collective-permute-done.10.refs_9_.refs_15_), channel_id=1, source_target_pairs={{0,2},{1,3},{2,4},{3,5},{4,6},{5,7},{6,0},{7,1},{8,10},{9,11},{10,... | collective-permute-start | bytes 786440 | tf_op jit(solution)/shard_map/ppermute | solution.py:57
  41.5 11.3 %collective-permute-start.15 = (bf16[128,1024]{1,0:T(8,128)(2,1)S(1)}, bf16[128,1024]{1,0:T(8,128)(2,1)S(1)}, u32[]{:S(2)}, u32[]{:S(2)}) collective-permute-start(bf16[128,1024]{1,0:T(8,128)(2,1)S(1)} %collective-permute-done.11.refs_10_.refs_16_), channel_id=1, source_target_pairs={{0,2},{1,3},{2,4},{3,5},{4,6},{5,7},{6,0},{7,1},{8,10},{9,11},{10,... | collective-permute-start | bytes 786440 | tf_op jit(solution)/shard_map/ppermute | solution.py:57
  47.2 6.8 %collective-permute-start.9 = (bf16[128,1024]{1,0:T(8,128)(2,1)S(1)}, bf16[128,1024]{1,0:T(8,128)(2,1)S(1)}, u32[]{:S(2)}, u32[]{:S(2)}) collective-permute-start(bf16[128,1024]{1,0:T(8,128)(2,1)S(1)} %collective-permute-done.7.refs_6_.refs_12_), channel_id=1, source_target_pairs={{0,8},{1,9},{2,10},{3,11},{4,12},{5,13},{6,14},{7,15},{8,0},{9,1},... | collective-permute-start | bytes 786440 | tf_op jit(solution)/shard_map/ppermute | solution.py:57
  47.8 6.3 %collective-permute-start.12 = (bf16[128,1024]{1,0:T(8,128)(2,1)S(1)}, bf16[128,1024]{1,0:T(8,128)(2,1)S(1)}, u32[]{:S(2)}, u32[]{:S(2)}) collective-permute-start(bf16[128,1024]{1,0:T(8,128)(2,1)S(1)} %collective-permute-done.10.refs_9_.refs_15_), channel_id=1, source_target_pairs={{0,8},{1,9},{2,10},{3,11},{4,12},{5,13},{6,14},{7,15},{8,0},{9,1},... | collective-permute-start | bytes 786440 | tf_op jit(solution)/shard_map/ppermute | solution.py:57
  52.2 8.8 %collective-permute-start.16 = (bf16[128,1024]{1,0:T(8,128)(2,1)S(1)}, bf16[128,1024]{1,0:T(8,128)(2,1)S(1)}, u32[]{:S(2)}, u32[]{:S(2)}) collective-permute-start(bf16[128,1024]{1,0:T(8,128)(2,1)S(1)} %collective-permute-done.14.refs_4_), channel_id=1, source_target_pairs={{0,8},{1,9},{2,10},{3,11},{4,12},{5,13},{6,14},{7,15},{8,0},{9,1},... | collective-permute-start | bytes 786440 | tf_op jit(solution)/shard_map/ppermute | solution.py:57
  52.7 8.3 %collective-permute-start.17 = (bf16[128,1024]{1,0:T(8,128)(2,1)S(1)}, bf16[128,1024]{1,0:T(8,128)(2,1)S(1)}, u32[]{:S(2)}, u32[]{:S(2)}) collective-permute-start(bf16[128,1024]{1,0:T(8,128)(2,1)S(1)} %collective-permute-done.15.refs_5_), channel_id=1, source_target_pairs={{0,8},{1,9},{2,10},{3,11},{4,12},{5,13},{6,14},{7,15},{8,0},{9,1},... | collective-permute-start | bytes 786440 | tf_op jit(solution)/shard_map/ppermute | solution.py:57
  76.0 4.3 %collective-permute-start.23 = (f32[1,2048]{1,0:T(1,128)S(1)}, f32[1,2048]{1,0:T(1,128)S(1)}, u32[]{:S(2)}, u32[]{:S(2)}) collective-permute-start(f32[1,2048]{1,0:T(1,128)S(1)} %join_cores.4.refs_2_), channel_id=1, source_target_pairs={{0,4},{1,5},{2,6},{3,7},{4,0},{5,1},{6,2},{7,3},{8,12},{9,13},{10,... | collective-permute-start | bytes 24584 | tf_op jit(solution)/shard_map/ppermute | solution.py:57
  86.4 5.2 %collective-permute-start.27 = (f32[1,2048]{1,0:T(1,128)S(1)}, f32[1,2048]{1,0:T(1,128)S(1)}, u32[]{:S(2)}, u32[]{:S(2)}) collective-permute-start(f32[1,2048]{1,0:T(1,128)S(1)} %join_cores.5.refs_2_), channel_id=1, source_target_pairs={{0,4},{1,5},{2,6},{3,7},{4,0},{5,1},{6,2},{7,3},{8,12},{9,13},{10,... | collective-permute-start | bytes 24584 | tf_op jit(solution)/shard_map/ppermute | solution.py:57
  87.5 4.2 %collective-permute-start.29 = (f32[1,2048]{1,0:T(1,128)S(1)}, f32[1,2048]{1,0:T(1,128)S(1)}, u32[]{:S(2)}, u32[]{:S(2)}) collective-permute-start(f32[1,2048]{1,0:T(1,128)S(1)} %collective-permute-done.28.refs_4_), channel_id=1, source_target_pairs={{0,8},{1,9},{2,10},{3,11},{4,12},{5,13},{6,14},{7,15},{8,0},{9,1},... | collective-permute-start | bytes 24584 | tf_op jit(solution)/shard_map/ppermute | solution.py:57
  96.9 9.7 %collective-permute-start.31 = (bf16[512,256]{1,0:T(8,128)(2,1)S(1)}, bf16[512,256]{1,0:T(8,128)(2,1)S(1)}, u32[]{:S(2)}, u32[]{:S(2)}) collective-permute-start(bf16[512,256]{1,0:T(8,128)(2,1)S(1)} %combine.8.refs_4_), channel_id=1, source_target_pairs={{0,2},{1,3},{2,4},{3,5},{4,6},{5,7},{6,0},{7,1},{8,10},{9,11},{10,... | collective-permute-start | bytes 786440 | tf_op jit(solution)/shard_map/ppermute | solution.py:57
  100.2 8.2 %collective-permute-start.33 = (bf16[512,256]{1,0:T(8,128)(2,1)S(1)}, bf16[512,256]{1,0:T(8,128)(2,1)S(1)}, u32[]{:S(2)}, u32[]{:S(2)}) collective-permute-start(bf16[512,256]{1,0:T(8,128)(2,1)S(1)} %get-tuple-element.66), channel_id=1, source_target_pairs={{0,8},{1,9},{2,10},{3,11},{4,12},{5,13},{6,14},{7,15},{8,0},{9,1},... | collective-permute-start | bytes 786440 | tf_op jit(solution)/shard_map/ppermute | solution.py:57
  101.5 10.9 %collective-permute-start.36 = (bf16[528,256]{1,0:T(8,128)(2,1)S(1)}, bf16[528,256]{1,0:T(8,128)(2,1)S(1)}, u32[]{:S(2)}, u32[]{:S(2)}) collective-permute-start(bf16[528,256]{1,0:T(8,128)(2,1)S(1)} %combine.9.refs_5_), channel_id=1, source_target_pairs={{0,2},{1,3},{2,4},{3,5},{4,6},{5,7},{6,0},{7,1},{8,10},{9,11},{10,... | collective-permute-start | bytes 811016 | tf_op jit(solution)/shard_map/ppermute | solution.py:57
  101.6 7.0 %collective-permute-start.37 = (bf16[528,256]{1,0:T(8,128)(2,1)S(1)}, bf16[528,256]{1,0:T(8,128)(2,1)S(1)}, u32[]{:S(2)}, u32[]{:S(2)}) collective-permute-start(bf16[528,256]{1,0:T(8,128)(2,1)S(1)} %get-tuple-element.74), channel_id=1, source_target_pairs={{0,8},{1,9},{2,10},{3,11},{4,12},{5,13},{6,14},{7,15},{8,0},{9,1},... | collective-permute-start | bytes 811016 | tf_op jit(solution)/shard_map/ppermute | solution.py:57
  101.9 11.7 %collective-permute-start.44 = (bf16[528,256]{1,0:T(8,128)(2,1)S(1)}, bf16[528,256]{1,0:T(8,128)(2,1)S(1)}, u32[]{:S(2)}, u32[]{:S(2)}) collective-permute-start(bf16[528,256]{1,0:T(8,128)(2,1)S(1)} %get-tuple-element.77), channel_id=1, source_target_pairs={{0,8},{1,9},{2,10},{3,11},{4,12},{5,13},{6,14},{7,15},{8,0},{9,1},... | collective-permute-start | bytes 811016 | tf_op jit(solution)/shard_map/ppermute | solution.py:57
  106.6 7.2 %collective-permute-start.35 = (bf16[512,256]{1,0:T(8,128)(2,1)S(1)}, bf16[512,256]{1,0:T(8,128)(2,1)S(1)}, u32[]{:S(2)}, u32[]{:S(2)}) collective-permute-start(bf16[512,256]{1,0:T(8,128)(2,1)S(1)} %get-tuple-element.73), channel_id=1, source_target_pairs={{0,8},{1,9},{2,10},{3,11},{4,12},{5,13},{6,14},{7,15},{8,0},{9,1},... | collective-permute-start | bytes 786440 | tf_op jit(solution)/shard_map/ppermute | solution.py:57
  108.5 9.9 %collective-permute-start.34 = (bf16[512,256]{1,0:T(8,128)(2,1)S(1)}, bf16[512,256]{1,0:T(8,128)(2,1)S(1)}, u32[]{:S(2)}, u32[]{:S(2)}) collective-permute-start(bf16[512,256]{1,0:T(8,128)(2,1)S(1)} %combine.10.refs_3_.refs_2_), channel_id=1, source_target_pairs={{0,2},{1,3},{2,4},{3,5},{4,6},{5,7},{6,0},{7,1},{8,10},{9,11},{10,... | collective-permute-start | bytes 786440 | tf_op jit(solution)/shard_map/ppermute | solution.py:57
  108.6 14.9 %collective-permute-start.42 = (bf16[528,256]{1,0:T(8,128)(2,1)S(1)}, bf16[528,256]{1,0:T(8,128)(2,1)S(1)}, u32[]{:S(2)}, u32[]{:S(2)}) collective-permute-start(bf16[528,256]{1,0:T(8,128)(2,1)S(1)} %get-tuple-element.76), channel_id=1, source_target_pairs={{0,8},{1,9},{2,10},{3,11},{4,12},{5,13},{6,14},{7,15},{8,0},{9,1},... | collective-permute-start | bytes 811016 | tf_op jit(solution)/shard_map/ppermute | solution.py:57
  112.4 6.8 %collective-permute-start.39 = (bf16[512,256]{1,0:T(8,128)(2,1)S(1)}, bf16[512,256]{1,0:T(8,128)(2,1)S(1)}, u32[]{:S(2)}, u32[]{:S(2)}) collective-permute-start(bf16[512,256]{1,0:T(8,128)(2,1)S(1)} %get-tuple-element.75), channel_id=1, source_target_pairs={{0,8},{1,9},{2,10},{3,11},{4,12},{5,13},{6,14},{7,15},{8,0},{9,1},... | collective-permute-start | bytes 786440 | tf_op jit(solution)/shard_map/ppermute | solution.py:57
  113.7 10.6 %collective-permute-start.41 = (bf16[528,256]{1,0:T(8,128)(2,1)S(1)}, bf16[528,256]{1,0:T(8,128)(2,1)S(1)}, u32[]{:S(2)}, u32[]{:S(2)}) collective-permute-start(bf16[528,256]{1,0:T(8,128)(2,1)S(1)} %combine.11.refs_4_.refs_3_), channel_id=1, source_target_pairs={{0,2},{1,3},{2,4},{3,5},{4,6},{5,7},{6,0},{7,1},{8,10},{9,11},{10,... | collective-permute-start | bytes 811016 | tf_op jit(solution)/shard_map/ppermute | solution.py:57
  113.8 18.1 %collective-permute-start.45 = (bf16[528,256]{1,0:T(8,128)(2,1)S(1)}, bf16[528,256]{1,0:T(8,128)(2,1)S(1)}, u32[]{:S(2)}, u32[]{:S(2)}) collective-permute-start(bf16[528,256]{1,0:T(8,128)(2,1)S(1)} %combine.15), channel_id=1, source_target_pairs={{0,0},{1,8},{2,2},{3,10},{4,4},{5,12},{6,6},{7,14},{8,1},{9,9},{10... | collective-permute-start | bytes 811016 | tf_op jit(solution)/shard_map/ppermute | solution.py:57
  118.5 13.4 %collective-permute-start.38 = (bf16[512,256]{1,0:T(8,128)(2,1)S(1)}, bf16[512,256]{1,0:T(8,128)(2,1)S(1)}, u32[]{:S(2)}, u32[]{:S(2)}) collective-permute-start(bf16[512,256]{1,0:T(8,128)(2,1)S(1)} %combine.12.refs_3_), channel_id=1, source_target_pairs={{0,2},{1,10},{2,4},{3,12},{4,6},{5,14},{6,0},{7,8},{8,3},{9,11},{1... | collective-permute-start | bytes 786440 | tf_op jit(solution)/shard_map/ppermute | solution.py:57
  119.3 12.6 %collective-permute-start.40 = (bf16[512,256]{1,0:T(8,128)(2,1)S(1)}, bf16[512,256]{1,0:T(8,128)(2,1)S(1)}, u32[]{:S(2)}, u32[]{:S(2)}) collective-permute-start(bf16[512,256]{1,0:T(8,128)(2,1)S(1)} %combine.13), channel_id=1, source_target_pairs={{0,0},{1,8},{2,2},{3,10},{4,4},{5,12},{6,6},{7,14},{8,1},{9,9},{10... | collective-permute-start | bytes 786440 | tf_op jit(solution)/shard_map/ppermute | solution.py:57
  124.3 13.0 %collective-permute-start.43 = (bf16[528,256]{1,0:T(8,128)(2,1)S(1)}, bf16[528,256]{1,0:T(8,128)(2,1)S(1)}, u32[]{:S(2)}, u32[]{:S(2)}) collective-permute-start(bf16[528,256]{1,0:T(8,128)(2,1)S(1)} %combine.14), channel_id=1, source_target_pairs={{0,2},{1,10},{2,4},{3,12},{4,6},{5,14},{6,0},{7,8},{8,3},{9,11},{1... | collective-permute-start | bytes 811016 | tf_op jit(solution)/shard_map/ppermute | solution.py:57
  (17 other events, 67.4 us)

commit v4 on v3

--- a/solution.py
+++ b/solution.py
@@ -59,6 +59,7 @@
 
 BRIEF = pl.CostEstimate(flops=1, bytes_accessed=1, transcendentals=0)
 TURN = pl.CostEstimate(flops=6 * 10**9, bytes_accessed=1, transcendentals=0)
+HALF = pl.CostEstimate(flops=4 * 10**9, bytes_accessed=1, transcendentals=0)
 WAIT = pl.CostEstimate(flops=2 * 10**10, bytes_accessed=0, transcendentals=0)
 
 
@@ -236,7 +237,7 @@
     valid_ref, weights_ref, *refs = refs
     totals = refs[:ring]
     if last:
-        out_ref, rows_ref, scale_ref = refs[ring:]
+        rows_ref, scale_ref = refs[ring:]
     else:
         out_ref, scale_ref = refs[ring:]
     inverse_totals(totals, scale_ref)
@@ -244,13 +245,19 @@
     total = lax.dot_general(exact(scale_ref[...]), weights, NT, preferred_element_type=F32)
     total = jnp.sum(total, axis=0, keepdims=True)
     row_scale = valid / (total + 1.0 - valid)
-    sums = lax.dot_general(exact(row_scale), weights, NN, preferred_element_type=F32)
-    sums = jnp.sum(sums, axis=0, keepdims=True)
     if last:
         rows_ref[...] = row_scale
-        out_ref[...] = sums * scale_ref[...]
     else:
-        out_ref[...] = sums
+        out_ref[...] = column_sums(row_scale, weights)
+
+
+def column_sums(row_scale, weights):
+    sums = lax.dot_general(exact(row_scale), weights, NN, preferred_element_type=F32)
+    return jnp.sum(sums, axis=0, keepdims=True)
+
+
+def mass_kernel(rows_ref, scale_ref, weights_ref, out_ref):
+    out_ref[...] = column_sums(rows_ref[...], weights_ref[...]) * scale_ref[...]
 
 
 def high_low(total, height):
@@ -259,15 +266,17 @@
     return jnp.where(line == 0, high, jnp.where(line == 1, total - high, 0.0)).astype(BF16)
 
 
-def numerator_kernel(turned_ref, weights_ref, *refs, chunk, first, height, fresh):
+def numerator_kernel(turned_ref, weights_ref, *refs, chunk, first, height, fresh, extra):
     fast = fast_here()
     if fresh:
-        rows_ref, scale_ref, mass_ref, scaled_ref, *outs = refs
+        rows_ref, scale_ref, *refs = refs
+        *refs, scaled_ref, one_ref, two_ref = refs
         scaled = turned_ref[pl.ds(first, height), :].astype(F32) * rows_ref[...]
         scaled_ref[...] = scaled.astype(BF16)
     else:
-        scale_ref, mass_ref, *outs = refs
+        scale_ref, *refs, one_ref, two_ref = refs
         scaled_ref = turned_ref
+    outs = (one_ref, two_ref)
     width = outs[0].shape[1]
     step = height if height <= 384 else height // 2
     at = pl.ds(chunk * 2 * width, 2 * width)
@@ -282,8 +291,8 @@
         one, two = part[:, :width], part[:, width:]
         outs[0][pl.ds(i * step, step), :] = jnp.where(fast, one, two)
         outs[1][pl.ds(i * step, step), :] = jnp.where(fast, two, one)
-    extra = outs[0].shape[0] - height
     if extra:
+        (mass_ref,) = refs
         masses = [mass_ref[:, pl.ds((2 * chunk + k) * width, width)] for k in range(2)]
         one, two = (high_low(mass, extra) for mass in masses)
         outs[0][pl.ds(height, extra), :] = jnp.where(fast, one, two)
@@ -337,17 +346,7 @@
     clusters = owned * peers
     parts = 2
 
-    own = call(
-        unit_kernel,
-        (shape(owned // parts, depth),) * parts,
-        [send(centroids, routes.swap)],
-        name="unit_centroids",
-        cost_estimate=WAIT,
-    )
-    mine = [own]
-    for s in range(1, ring):
-        mine.append([send(p, routes.shift[1]) for p in mine[-1]])
-    other = [[send(p, routes.core) for p in m] for m in mine]
+    swapped = send(centroids, routes.swap)
 
     place = call(
         rank_kernel,
@@ -365,10 +364,36 @@
             name="pick_rows",
         )
 
-    arrived, packed = {}, ()
-    for d in [*range(2, groups), 1, 0]:
-        packed = (pick(d, packed),)
-        arrived[d] = send(packed[0], routes.cluster[d]) if d else packed[0]
+    direct = list(range(groups // 2, 0, -1))
+    distant = list(range(groups // 2 + 1, groups))
+    packed = {}
+    for d in [*direct, *distant, 0]:
+        packed[d] = pick(d, tuple(packed.values())[-1:])
+    arrived = {d: send(packed[d], routes.cluster[d]) for d in direct}
+
+    own = call(
+        unit_kernel,
+        (shape(owned // parts, depth),) * parts,
+        [swapped],
+        after=[packed[0]],
+        name="unit_centroids",
+        cost_estimate=WAIT,
+    )
+    mine = [own]
+    for s in range(1, ring):
+        one, two = (send(p, routes.shift[1]) for p in mine[-1])
+        if s < ring - 1:
+            (one,) = tie([one], (), HALF)
+            (two,) = tie([two], (one,), BRIEF)
+        mine.append([one, two])
+    for s in range(ring - 2):
+        mine[s] = [tie([p], (q,), BRIEF)[0] for p, q in zip(mine[s], mine[s + 1])]
+    mine[-2] = [tie([mine[-2][0]], mine[-1][:1], BRIEF)[0], mine[-2][1]]
+    other = [[send(p, routes.core) for p in m] for m in mine[:-1]]
+
+    waiting = tie([packed[d] for d in distant], [arrived[d] for d in direct], BRIEF)
+    arrived |= {d: send(p, routes.cluster[d]) for d, p in zip(distant, waiting)}
+    arrived[0] = packed[0]
 
     state_shapes = (
         shape(slots, depth),
@@ -395,13 +420,17 @@
             name="weights",
         )
 
-    early = list(range(ring - 1))
-    state = absorb((), [0], [0], early)
-    rest = list(range(1, groups))
-    waited = rest
-    arrived.update(zip(waited, tie([arrived[d] for d in waited], ())))
-    state = absorb(state, rest, rest, early)
-    rows, valid, weights, part = absorb(state, [], [0, *rest], [ring - 1])
+    near, early = [0, *sorted(direct)], list(range(ring - 1))
+    state = absorb((), near, near, early[:-1])
+    state = absorb(state, [], near, early[-1:])
+    one, two = mine[-1]
+    (one,) = tie([one], state[1:2], HALF)
+    arrived.update(zip(distant, tie([arrived[d] for d in distant], (), BRIEF)))
+    state = absorb(state, distant, distant, early)
+    (two,) = tie([two], (one, state[1]), BRIEF)
+    mine[-1] = [one, two]
+    other.append([send(p, routes.core) for p in mine[-1]])
+    rows, valid, weights, part = absorb(state, [], list(range(groups)), [ring - 1])
     turned = call(
         turn_kernel, shape(depth, slots), [arrived[d] for d in range(groups)], name="turn_rows"
     )
@@ -419,7 +448,7 @@
             totals += [value, send(value, routes.core)]
         outs = (shape(1, clusters, dtype=F32),)
         if last:
-            outs += (shape(1, slots, dtype=F32), shape(1, clusters, dtype=F32))
+            outs = (shape(1, slots, dtype=F32), *outs)
         return call(
             functools.partial(sweep_kernel, ring=ring, last=last),
             outs,
@@ -430,22 +459,41 @@
 
     for _ in range(SWEEPS - 1):
         (part,) = sweep(part, last=False)
-    mass_part, row_scale, column_scale = sweep(part, last=True)
+    row_scale, column_scale = sweep(part, last=True)
 
     heights = [depth * 4 // 8, depth - depth * 4 // 8]
     starts = [0, heights[0]]
     tall = [heights[0], heights[1] + 16]
 
+    masses = []
+
     def numerator(s, j, after):
         fresh = scaled[j] is None
         args = [turned, weights, row_scale] if fresh else [scaled[j], weights]
-        args = [*args, column_scale, mass_part]
+        args = [*args, column_scale]
+        if tall[j] > heights[j]:
+            if not masses:
+                masses.append(
+                    call(
+                        mass_kernel,
+                        shape(1, clusters, dtype=F32),
+                        [row_scale, column_scale, weights],
+                        after=after,
+                        name="masses",
+                    )
+                )
+            args += masses
         outs = (shape(tall[j], owned),) * 2
         if fresh:
             outs = (shape(heights[j], slots), *outs)
         outs = call(
             functools.partial(
-                numerator_kernel, chunk=s, first=starts[j], height=heights[j], fresh=fresh
+                numerator_kernel,
+                chunk=s,
+                first=starts[j],
+                height=heights[j],
+                fresh=fresh,
+                extra=tall[j] - heights[j],
             ),
             outs,
             args,
@@ -480,14 +528,14 @@
 
     def step(s, after):
         route = routes.home if s == ring - 1 else routes.shift[1]
-        made = []
+        sent = []
         for j in range(parts):
             added = combine(j, (*moving[j], *pairs[s, j]), after)
             moving[j] = (send(added, route),)
-            made.append(added)
+            sent.append(added)
             if s != first:
                 after = (added,)
-        return tuple(made)
+        return tuple(sent)
 
     sums_of(first, ())
     after = step(first, ())

time: 139 us -> 136 us (0.978)
  waiting for transfers between devices: 59.6 us -> 52.8 us
  starting transfers between devices: 44.8 us -> 47.8 us
    ppermute x46, waiting for transfers between devices: 59.6 us -> 52.8 us  [send(): return lax.ppermute(value, AXES, route)]
    ppermute x46, starting transfers between devices: 44.8 us -> 47.8 us  [send(): return lax.ppermute(value, AXES, route)]
    pallas_call x33 -> x35, Pallas kernels: 31.2 us -> 31.5 us  [call(): pl.pallas_call(ordered, out_shape=outs, in_specs=(specs or [VMEM] * len(a...]
  transfers between devices with their start and end apart: 46 -> 46, of which waited for: 24 -> 25; matrix products, arithmetic and copies ran while one was open for 0% -> 0% of each run, Pallas kernels for 14% -> 15%
where the time goes in v4:
time: 136 us; the launch traced here: 135 us
  waiting for transfers between devices  52.8 us (39%)
  starting transfers between devices  47.8 us (35%)
  Pallas kernels  31.6 us (23%)
  local copies, waits for them, and re-layouts  2.09 us (2%)
    ppermute x46, waiting for transfers between devices, send(): return lax.ppermute(value, AXES, route)  52.8 us
    ppermute x46, starting transfers between devices, send(): return lax.ppermute(value, AXES, route)  47.8 us
    pallas_call x35, Pallas kernels, call(): pl.pallas_call(ordered, out_shape=outs, in_specs=(specs or [VMEM] * len(a...  31.5 us
  transfers between devices with their start and end apart: 46, of which 25 were waited for; matrix products, arithmetic and copies ran while one was open for 0% of the time, Pallas kernels for 15%

profile of v4, /device:TPU:1, one launch (start us, length us, event | category | flops | bytes accessed | tf_op | source)
XLA Modules:
  0.0 135.3 jit_solution(10622501600577609906)
XLA Ops:
  0.6 4.5 %collective-permute-start.3 = (bf16[256,1024]{1,0:T(8,128)(2,1)}, bf16[256,1024]{1,0:T(8,128)(2,1)S(1)}, u32[]{:S(2)}, u32[]{:S(2)}) collective-permute-start(bf16[256,1024]{1,0:T(8,128)(2,1)} %param.5), channel_id=1, source_target_pairs={{0,0},{1,8},{2,2},{3,10},{4,4},{5,12},{6,6},{7,14},{8,1},{9,9},{10... | collective-permute-start | bytes 1572872 | tf_op jit(solution)/shard_map/ppermute | solution.py:57
  6.1 1.4 %copy-done = bf16[768,1024]{1,0:T(8,128)(2,1)S(1)} copy-done((bf16[768,1024]{1,0:T(8,128)(2,1)S(1)}, bf16[768,1024]{1,0:T(8,128)(2,1)}, u32[]{:S(2)}) %copy-start) | copy-done | bytes 1572888
  12.4 1.3 collective-permute-start.4
  16.3 3.6 %collective-permute-done.4.refs_0_ = bf16[128,1024]{1,0:T(8,128)(2,1)S(1)} collective-permute-done((bf16[128,1024]{1,0:T(8,128)(2,1)S(1)}, bf16[128,1024]{1,0:T(8,128)(2,1)S(1)}, u32[]{:S(2)}, u32[]{:S(2)}) %collective-permute-start.4) | collective-permute-done | bytes 262176 | tf_op jit(solution)/shard_map/ppermute | solution.py:57
  19.9 3.4 %collective-permute-done.5.refs_0_ = bf16[128,1024]{1,0:T(8,128)(2,1)S(1)} collective-permute-done((bf16[128,1024]{1,0:T(8,128)(2,1)S(1)}, bf16[128,1024]{1,0:T(8,128)(2,1)S(1)}, u32[]{:S(2)}, u32[]{:S(2)}) %collective-permute-start.5) | collective-permute-done | bytes 262176 | tf_op jit(solution)/shard_map/ppermute | solution.py:57
  23.3 9.2 %collective-permute-done.refs_2_.refs_1_ = bf16[384,1024]{1,0:T(8,128)(2,1)S(1)} collective-permute-done((bf16[384,1024]{1,0:T(8,128)(2,1)S(1)}, bf16[384,1024]{1,0:T(8,128)(2,1)S(1)}, u32[]{:S(2)}, u32[]{:S(2)}) %collective-permute-start) | collective-permute-done | bytes 786464 | tf_op jit(solution)/shard_map/ppermute | solution.py:57
  32.5 2.1 %collective-permute-start.2 = (bf16[384,1024]{1,0:T(8,128)(2,1)S(1)}, bf16[384,1024]{1,0:T(8,128)(2,1)S(1)}, u32[]{:S(2)}, u32[]{:S(2)}) collective-permute-start(bf16[384,1024]{1,0:T(8,128)(2,1)S(1)} %tie.14), channel_id=1, source_target_pairs={{0,17},{1,16},{2,19},{3,18},{4,21},{5,20},{6,23},{7,22},{8,25},{9,... | collective-permute-start | bytes 2359304 | tf_op jit(solution)/shard_map/ppermute | solution.py:57
  35.9 2.1 %collective-permute-start.7 = (bf16[128,1024]{1,0:T(8,128)(2,1)S(1)}, bf16[128,1024]{1,0:T(8,128)(2,1)S(1)}, u32[]{:S(2)}, u32[]{:S(2)}) collective-permute-start(bf16[128,1024]{1,0:T(8,128)(2,1)S(1)} %tie.19.refs_4_.refs_6_), channel_id=1, source_target_pairs={{0,8},{1,9},{2,10},{3,11},{4,12},{5,13},{6,14},{7,15},{8,0},{9,1},... | collective-permute-start | bytes 786440 | tf_op jit(solution)/shard_map/ppermute | solution.py:57
  38.5 3.9 %collective-permute-done.12.refs_1_.refs_0_ = bf16[128,1024]{1,0:T(8,128)(2,1)S(1)} collective-permute-done((bf16[128,1024]{1,0:T(8,128)(2,1)S(1)}, bf16[128,1024]{1,0:T(8,128)(2,1)S(1)}, u32[]{:S(2)}, u32[]{:S(2)}) %collective-permute-start.12) | collective-permute-done | bytes 262176 | tf_op jit(solution)/shard_map/ppermute | solution.py:57
  42.4 2.7 %collective-permute-start.10 = (bf16[128,1024]{1,0:T(8,128)(2,1)S(1)}, bf16[128,1024]{1,0:T(8,128)(2,1)S(1)}, u32[]{:S(2)}, u32[]{:S(2)}) collective-permute-start(bf16[128,1024]{1,0:T(8,128)(2,1)S(1)} %tie.21.refs_7_.refs_9_), channel_id=1, source_target_pairs={{0,8},{1,9},{2,10},{3,11},{4,12},{5,13},{6,14},{7,15},{8,0},{9,1},... | collective-permute-start | bytes 786440 | tf_op jit(solution)/shard_map/ppermute | solution.py:57
  46.3 3.7 %weights.4 = (bf16[1536,1024]{1,0:T(8,128)(2,1)S(1)}, f32[1,1536]{1,0:T(1,128)S(1)}, bf16[1536,2048]{1,0:T(8,128)(2,1)S(1)}, f32[1,2048]{1,0:T(1,128)S(1)}) custom-call(bf16[384,1024]{1,0:T(8,128)(2,1)S(1)} %pick_rows.7.refs_0_.refs_1_, bf16[384,1024]{1,0:T(8,128)(2,1)S(1)} %collective-permute-done.refs_2_.refs_1_, ...), custom_call_target="tpu_custom_call" | custom-call | tf_op jit(solution)/shard_map/weights/pallas_call | solution.py:72
  51.2 1.6 %weights.5 = (bf16[1536,1024]{1,0:T(8,128)(2,1)S(1)}, f32[1,1536]{1,0:T(1,128)S(1)}, bf16[1536,2048]{1,0:T(8,128)(2,1)S(1)}, f32[1,2048]{1,0:T(1,128)S(1)}) custom-call(bf16[1536,1024]{1,0:T(8,128)(2,1)S(1)} %get-tuple-element.43.refs_0_, ...), custom_call_target="tpu_custom_call", output_to_operand_aliasing={{0}: (0, {}), {1}: (1, {}), {2}: (2, {}), {3}: (3, {})} | custom-call | tf_op jit(solution)/shard_map/weights/pallas_call | solution.py:72
  52.8 1.8 %weights.6 = (bf16[1536,1024]{1,0:T(8,128)(2,1)S(1)}, f32[1,1536]{1,0:T(1,128)S(1)}, bf16[1536,2048]{1,0:T(8,128)(2,1)S(1)}, f32[1,2048]{1,0:T(1,128)S(1)}) custom-call(bf16[1536,1024]{1,0:T(8,128)(2,1)S(1)} %get-tuple-element.47.refs_0_, ...), custom_call_target="tpu_custom_call", output_to_operand_aliasing={{0}: (0, {}), {1}: (1, {}), {2}: (2, {}), {3}: (3, {})} | custom-call | tf_op jit(solution)/shard_map/weights/pallas_call | solution.py:72
  55.3 1.5 %collective-permute-start.17 = (bf16[128,1024]{1,0:T(8,128)(2,1)S(1)}, bf16[128,1024]{1,0:T(8,128)(2,1)S(1)}, u32[]{:S(2)}, u32[]{:S(2)}) collective-permute-start(bf16[128,1024]{1,0:T(8,128)(2,1)S(1)} %tie.26.refs_5_), channel_id=1, source_target_pairs={{0,8},{1,9},{2,10},{3,11},{4,12},{5,13},{6,14},{7,15},{8,0},{9,1},... | collective-permute-start | bytes 786440 | tf_op jit(solution)/shard_map/ppermute | solution.py:57
  58.4 2.0 %weights.7 = (bf16[1536,1024]{1,0:T(8,128)(2,1)S(1)}, f32[1,1536]{1,0:T(1,128)S(1)}, bf16[1536,2048]{1,0:T(8,128)(2,1)S(1)}, f32[1,2048]{1,0:T(1,128)S(1)}) custom-call(bf16[1536,1024]{1,0:T(8,128)(2,1)S(1)} %get-tuple-element.51.refs_0_, ...), custom_call_target="tpu_custom_call", output_to_operand_aliasing={{0}: (0, {}), {1}: (1, {}), {2}: (2, {}), {3}: (3, {})} | custom-call | tf_op jit(solution)/shard_map/weights/pallas_call | solution.py:72
  61.6 2.3 %collective-permute-start.20 = (f32[1,2048]{1,0:T(1,128)S(1)}, f32[1,2048]{1,0:T(1,128)S(1)}, u32[]{:S(2)}, u32[]{:S(2)}) collective-permute-start(f32[1,2048]{1,0:T(1,128)S(1)} %join_cores.3.refs_2_), channel_id=1, source_target_pairs={{0,2},{1,3},{2,4},{3,5},{4,6},{5,7},{6,0},{7,1},{8,14},{9,15},{10,... | collective-permute-start | bytes 24584 | tf_op jit(solution)/shard_map/ppermute | solution.py:57
  64.7 2.7 %collective-permute-start.21 = (f32[1,2048]{1,0:T(1,128)S(1)}, f32[1,2048]{1,0:T(1,128)S(1)}, u32[]{:S(2)}, u32[]{:S(2)}) collective-permute-start(f32[1,2048]{1,0:T(1,128)S(1)} %collective-permute-done.20.refs_4_), channel_id=1, source_target_pairs={{0,8},{1,9},{2,10},{3,11},{4,12},{5,13},{6,14},{7,15},{8,0},{9,1},... | collective-permute-start | bytes 24584 | tf_op jit(solution)/shard_map/ppermute | solution.py:57
  68.2 2.6 %sweep.2.refs_0_ = f32[1,2048]{1,0:T(1,128)S(1)} custom-call(f32[1,1536]{1,0:T(1,128)S(1)} %get-tuple-element.56.refs_0_, bf16[1536,2048]{1,0:T(8,128)(2,1)S(1)} %get-tuple-element.55.refs_1_.refs_2_, f32[1,2048]{1,0:T(1,128)S(1)} %join_cores.3.refs_2_, f32[1,2048]{1,0:T(1,128)S(1)} %collective-permute-done.19.refs_3_, ...), custom_call_target="tpu_custom_call" | custom-call | tf_op jit(solution)/shard_map/sweep/pallas_call | solution.py:72
  72.1 1.5 %collective-permute-start.24 = (f32[1,2048]{1,0:T(1,128)S(1)}, f32[1,2048]{1,0:T(1,128)S(1)}, u32[]{:S(2)}, u32[]{:S(2)}) collective-permute-start(f32[1,2048]{1,0:T(1,128)S(1)} %join_cores.4.refs_2_), channel_id=1, source_target_pairs={{0,2},{1,3},{2,4},{3,5},{4,6},{5,7},{6,0},{7,1},{8,14},{9,15},{10,... | collective-permute-start | bytes 24584 | tf_op jit(solution)/shard_map/ppermute | solution.py:57
  74.6 3.3 %collective-permute-start.25 = (f32[1,2048]{1,0:T(1,128)S(1)}, f32[1,2048]{1,0:T(1,128)S(1)}, u32[]{:S(2)}, u32[]{:S(2)}) collective-permute-start(f32[1,2048]{1,0:T(1,128)S(1)} %collective-permute-done.24.refs_4_), channel_id=1, source_target_pairs={{0,8},{1,9},{2,10},{3,11},{4,12},{5,13},{6,14},{7,15},{8,0},{9,1},... | collective-permute-start | bytes 24584 | tf_op jit(solution)/shard_map/ppermute | solution.py:57
  78.7 2.6 %sweep.3.refs_0_ = f32[1,2048]{1,0:T(1,128)S(1)} custom-call(f32[1,1536]{1,0:T(1,128)S(1)} %get-tuple-element.56.refs_0_, bf16[1536,2048]{1,0:T(8,128)(2,1)S(1)} %get-tuple-element.55.refs_1_.refs_2_, f32[1,2048]{1,0:T(1,128)S(1)} %join_cores.4.refs_2_, f32[1,2048]{1,0:T(1,128)S(1)} %collective-permute-done.23.refs_3_, ...), custom_call_target="tpu_custom_call" | custom-call | tf_op jit(solution)/shard_map/sweep/pallas_call | solution.py:72
  82.5 1.5 %collective-permute-start.28 = (f32[1,2048]{1,0:T(1,128)S(1)}, f32[1,2048]{1,0:T(1,128)S(1)}, u32[]{:S(2)}, u32[]{:S(2)}) collective-permute-start(f32[1,2048]{1,0:T(1,128)S(1)} %join_cores.5.refs_2_), channel_id=1, source_target_pairs={{0,2},{1,3},{2,4},{3,5},{4,6},{5,7},{6,0},{7,1},{8,14},{9,15},{10,... | collective-permute-start | bytes 24584 | tf_op jit(solution)/shard_map/ppermute | solution.py:57
  85.0 3.3 %collective-permute-start.29 = (f32[1,2048]{1,0:T(1,128)S(1)}, f32[1,2048]{1,0:T(1,128)S(1)}, u32[]{:S(2)}, u32[]{:S(2)}) collective-permute-start(f32[1,2048]{1,0:T(1,128)S(1)} %collective-permute-done.28.refs_4_), channel_id=1, source_target_pairs={{0,8},{1,9},{2,10},{3,11},{4,12},{5,13},{6,14},{7,15},{8,0},{9,1},... | collective-permute-start | bytes 24584 | tf_op jit(solution)/shard_map/ppermute | solution.py:57
  89.2 1.8 %last_sweep.1 = (f32[1,1536]{1,0:T(1,128)S(1)}, f32[1,2048]{1,0:T(1,128)S(1)}) custom-call(f32[1,1536]{1,0:T(1,128)S(1)} %get-tuple-element.56.refs_0_, bf16[1536,2048]{1,0:T(8,128)(2,1)S(1)} %get-tuple-element.55.refs_1_.refs_2_, f32[1,2048]{1,0:T(1,128)S(1)} %join_cores.5.refs_2_, f32[1,2048]{1,0:T(1,128)S(1)} %collective-permute-done.27.refs_3_, ...), custom_call_target="tpu_custom_call" | custom-call | tf_op jit(solution)/shard_map/last_sweep/pallas_call | solution.py:72
  104.1 1.8 %collective-permute-start.35 = (bf16[512,256]{1,0:T(8,128)(2,1)S(1)}, bf16[512,256]{1,0:T(8,128)(2,1)S(1)}, u32[]{:S(2)}, u32[]{:S(2)}) collective-permute-start(bf16[512,256]{1,0:T(8,128)(2,1)S(1)} %get-tuple-element.73), channel_id=1, source_target_pairs={{0,8},{1,9},{2,10},{3,11},{4,12},{5,13},{6,14},{7,15},{8,0},{9,1},... | collective-permute-start | bytes 786440 | tf_op jit(solution)/shard_map/ppermute | solution.py:57
  106.1 3.7 %collective-permute-done.36.refs_0_ = bf16[528,256]{1,0:T(8,128)(2,1)S(1)} collective-permute-done((bf16[528,256]{1,0:T(8,128)(2,1)S(1)}, bf16[528,256]{1,0:T(8,128)(2,1)S(1)}, u32[]{:S(2)}, u32[]{:S(2)}) %collective-permute-start.36) | collective-permute-done | bytes 270368 | tf_op jit(solution)/shard_map/ppermute | solution.py:57
  111.2 2.9 %collective-permute-start.45 = (bf16[528,256]{1,0:T(8,128)(2,1)S(1)}, bf16[528,256]{1,0:T(8,128)(2,1)S(1)}, u32[]{:S(2)}, u32[]{:S(2)}) collective-permute-start(bf16[528,256]{1,0:T(8,128)(2,1)S(1)} %combine.15), channel_id=1, source_target_pairs={{0,0},{1,8},{2,2},{3,10},{4,4},{5,12},{6,6},{7,14},{8,1},{9,9},{10... | collective-permute-start | bytes 811016 | tf_op jit(solution)/shard_map/ppermute | solution.py:57
  114.2 1.6 %collective-permute-done.34.refs_0_ = bf16[512,256]{1,0:T(8,128)(2,1)S(1)} collective-permute-done((bf16[512,256]{1,0:T(8,128)(2,1)S(1)}, bf16[512,256]{1,0:T(8,128)(2,1)S(1)}, u32[]{:S(2)}, u32[]{:S(2)}) %collective-permute-start.34) | collective-permute-done | bytes 262176 | tf_op jit(solution)/shard_map/ppermute | solution.py:57
  116.1 4.1 %collective-permute-start.40 = (bf16[512,256]{1,0:T(8,128)(2,1)S(1)}, bf16[512,256]{1,0:T(8,128)(2,1)S(1)}, u32[]{:S(2)}, u32[]{:S(2)}) collective-permute-start(bf16[512,256]{1,0:T(8,128)(2,1)S(1)} %combine.13), channel_id=1, source_target_pairs={{0,0},{1,8},{2,2},{3,10},{4,4},{5,12},{6,6},{7,14},{8,1},{9,9},{10... | collective-permute-start | bytes 786440 | tf_op jit(solution)/shard_map/ppermute | solution.py:57
  120.2 1.5 %collective-permute-done.41.refs_0_ = bf16[528,256]{1,0:T(8,128)(2,1)S(1)} collective-permute-done((bf16[528,256]{1,0:T(8,128)(2,1)S(1)}, bf16[528,256]{1,0:T(8,128)(2,1)S(1)}, u32[]{:S(2)}, u32[]{:S(2)}) %collective-permute-start.41) | collective-permute-done | bytes 270368 | tf_op jit(solution)/shard_map/ppermute | solution.py:57
  121.8 6.7 %collective-permute-done.38.refs_0_ = bf16[512,256]{1,0:T(8,128)(2,1)S(1)} collective-permute-done((bf16[512,256]{1,0:T(8,128)(2,1)S(1)}, bf16[512,256]{1,0:T(8,128)(2,1)S(1)}, u32[]{:S(2)}, u32[]{:S(2)}) %collective-permute-start.38) | collective-permute-done | bytes 262176 | tf_op jit(solution)/shard_map/ppermute | solution.py:57
  128.5 5.4 %collective-permute-done.43.refs_2_ = bf16[528,256]{1,0:T(8,128)(2,1)S(1)} collective-permute-done((bf16[528,256]{1,0:T(8,128)(2,1)S(1)}, bf16[528,256]{1,0:T(8,128)(2,1)S(1)}, u32[]{:S(2)}, u32[]{:S(2)}) %collective-permute-start.43) | collective-permute-done | bytes 270368 | tf_op jit(solution)/shard_map/ppermute | solution.py:57
  (113 shorter events, 40.1 us)
Async XLA Ops:
  0.6 11.6 %collective-permute-start.3 = (bf16[256,1024]{1,0:T(8,128)(2,1)}, bf16[256,1024]{1,0:T(8,128)(2,1)S(1)}, u32[]{:S(2)}, u32[]{:S(2)}) collective-permute-start(bf16[256,1024]{1,0:T(8,128)(2,1)} %param.5), channel_id=1, source_target_pairs={{0,0},{1,8},{2,2},{3,10},{4,4},{5,12},{6,6},{7,14},{8,1},{9,9},{10... | collective-permute-start | bytes 1572872 | tf_op jit(solution)/shard_map/ppermute | solution.py:57
  12.4 7.5 %collective-permute-start.4 = (bf16[128,1024]{1,0:T(8,128)(2,1)S(1)}, bf16[128,1024]{1,0:T(8,128)(2,1)S(1)}, u32[]{:S(2)}, u32[]{:S(2)}) collective-permute-start(bf16[128,1024]{1,0:T(8,128)(2,1)S(1)} %get-tuple-element.41.refs_0_), channel_id=1, source_target_pairs={{0,2},{1,3},{2,4},{3,5},{4,6},{5,7},{6,0},{7,1},{8,10},{9,11},{10,... | collective-permute-start | bytes 786440 | tf_op jit(solution)/shard_map/ppermute | solution.py:57
  13.8 18.7 %collective-permute-start = (bf16[384,1024]{1,0:T(8,128)(2,1)S(1)}, bf16[384,1024]{1,0:T(8,128)(2,1)S(1)}, u32[]{:S(2)}, u32[]{:S(2)}) collective-permute-start(bf16[384,1024]{1,0:T(8,128)(2,1)S(1)} %pick_rows.5.refs_2_), channel_id=1, source_target_pairs={{0,1},{1,0},{2,3},{3,2},{4,5},{5,4},{6,7},{7,6},{8,9},{9,8},{10,11... | collective-permute-start | bytes 2359304 | tf_op jit(solution)/shard_map/ppermute | solution.py:57
  13.8 18.7 %collective-permute-start.1 = (bf16[384,1024]{1,0:T(8,128)(2,1)S(1)}, bf16[384,1024]{1,0:T(8,128)(2,1)S(1)}, u32[]{:S(2)}, u32[]{:S(2)}) collective-permute-start(bf16[384,1024]{1,0:T(8,128)(2,1)S(1)} %pick_rows.4.refs_2_), channel_id=1, source_target_pairs={{0,16},{1,17},{2,18},{3,19},{4,20},{5,21},{6,22},{7,23},{8,24},{9,... | collective-permute-start | bytes 2359304 | tf_op jit(solution)/shard_map/ppermute | solution.py:57
  15.0 8.3 %collective-permute-start.5 = (bf16[128,1024]{1,0:T(8,128)(2,1)S(1)}, bf16[128,1024]{1,0:T(8,128)(2,1)S(1)}, u32[]{:S(2)}, u32[]{:S(2)}) collective-permute-start(bf16[128,1024]{1,0:T(8,128)(2,1)S(1)} %get-tuple-element.42.refs_0_), channel_id=1, source_target_pairs={{0,2},{1,3},{2,4},{3,5},{4,6},{5,7},{6,0},{7,1},{8,10},{9,11},{10,... | collective-permute-start | bytes 786440 | tf_op jit(solution)/shard_map/ppermute | solution.py:57
  19.9 14.7 %collective-permute-start.8 = (bf16[128,1024]{1,0:T(8,128)(2,1)S(1)}, bf16[128,1024]{1,0:T(8,128)(2,1)S(1)}, u32[]{:S(2)}, u32[]{:S(2)}) collective-permute-start(bf16[128,1024]{1,0:T(8,128)(2,1)S(1)} %tie.16.refs_1_.refs_0_), channel_id=1, source_target_pairs={{0,2},{1,3},{2,4},{3,5},{4,6},{5,7},{6,0},{7,1},{8,10},{9,11},{10,... | collective-permute-start | bytes 786440 | tf_op jit(solution)/shard_map/ppermute | solution.py:57
  23.3 14.7 %collective-permute-start.9 = (bf16[128,1024]{1,0:T(8,128)(2,1)S(1)}, bf16[128,1024]{1,0:T(8,128)(2,1)S(1)}, u32[]{:S(2)}, u32[]{:S(2)}) collective-permute-start(bf16[128,1024]{1,0:T(8,128)(2,1)S(1)} %tie.18.refs_1_.refs_0_), channel_id=1, source_target_pairs={{0,2},{1,3},{2,4},{3,5},{4,6},{5,7},{6,0},{7,1},{8,10},{9,11},{10,... | collective-permute-start | bytes 786440 | tf_op jit(solution)/shard_map/ppermute | solution.py:57
  32.5 18.7 %collective-permute-start.2 = (bf16[384,1024]{1,0:T(8,128)(2,1)S(1)}, bf16[384,1024]{1,0:T(8,128)(2,1)S(1)}, u32[]{:S(2)}, u32[]{:S(2)}) collective-permute-start(bf16[384,1024]{1,0:T(8,128)(2,1)S(1)} %tie.14), channel_id=1, source_target_pairs={{0,17},{1,16},{2,19},{3,18},{4,21},{5,20},{6,23},{7,22},{8,25},{9,... | collective-permute-start | bytes 2359304 | tf_op jit(solution)/shard_map/ppermute | solution.py:57
  34.6 7.8 %collective-permute-start.12 = (bf16[128,1024]{1,0:T(8,128)(2,1)S(1)}, bf16[128,1024]{1,0:T(8,128)(2,1)S(1)}, u32[]{:S(2)}, u32[]{:S(2)}) collective-permute-start(bf16[128,1024]{1,0:T(8,128)(2,1)S(1)} %tie.20.refs_1_.refs_0_), channel_id=1, source_target_pairs={{0,2},{1,3},{2,4},{3,5},{4,6},{5,7},{6,0},{7,1},{8,10},{9,11},{10,... | collective-permute-start | bytes 786440 | tf_op jit(solution)/shard_map/ppermute | solution.py:57
  35.9 9.2 %collective-permute-start.7 = (bf16[128,1024]{1,0:T(8,128)(2,1)S(1)}, bf16[128,1024]{1,0:T(8,128)(2,1)S(1)}, u32[]{:S(2)}, u32[]{:S(2)}) collective-permute-start(bf16[128,1024]{1,0:T(8,128)(2,1)S(1)} %tie.19.refs_4_.refs_6_), channel_id=1, source_target_pairs={{0,8},{1,9},{2,10},{3,11},{4,12},{5,13},{6,14},{7,15},{8,0},{9,1},... | collective-permute-start | bytes 786440 | tf_op jit(solution)/shard_map/ppermute | solution.py:57
  38.0 7.2 %collective-permute-start.6 = (bf16[128,1024]{1,0:T(8,128)(2,1)S(1)}, bf16[128,1024]{1,0:T(8,128)(2,1)S(1)}, u32[]{:S(2)}, u32[]{:S(2)}) collective-permute-start(bf16[128,1024]{1,0:T(8,128)(2,1)S(1)} %tie.17.refs_3_.refs_5_), channel_id=1, source_target_pairs={{0,8},{1,9},{2,10},{3,11},{4,12},{5,13},{6,14},{7,15},{8,0},{9,1},... | collective-permute-start | bytes 786440 | tf_op jit(solution)/shard_map/ppermute | solution.py:57
  38.0 7.6 %collective-permute-start.11 = (bf16[128,1024]{1,0:T(8,128)(2,1)S(1)}, bf16[128,1024]{1,0:T(8,128)(2,1)S(1)}, u32[]{:S(2)}, u32[]{:S(2)}) collective-permute-start(bf16[128,1024]{1,0:T(8,128)(2,1)S(1)} %tie.23.refs_8_.refs_10_), channel_id=1, source_target_pairs={{0,8},{1,9},{2,10},{3,11},{4,12},{5,13},{6,14},{7,15},{8,0},{9,1},... | collective-permute-start | bytes 786440 | tf_op jit(solution)/shard_map/ppermute | solution.py:57
  45.1 6.1 %collective-permute-start.14 = (bf16[128,1024]{1,0:T(8,128)(2,1)S(1)}, bf16[128,1024]{1,0:T(8,128)(2,1)S(1)}, u32[]{:S(2)}, u32[]{:S(2)}) collective-permute-start(bf16[128,1024]{1,0:T(8,128)(2,1)S(1)} %tie.22.refs_1_.refs_5_.refs_14_), channel_id=1, source_target_pairs={{0,8},{1,9},{2,10},{3,11},{4,12},{5,13},{6,14},{7,15},{8,0},{9,1},... | collective-permute-start | bytes 786440 | tf_op jit(solution)/shard_map/ppermute | solution.py:57
  45.2 6.0 %collective-permute-start.13 = (bf16[128,1024]{1,0:T(8,128)(2,1)S(1)}, bf16[128,1024]{1,0:T(8,128)(2,1)S(1)}, u32[]{:S(2)}, u32[]{:S(2)}) collective-permute-start(bf16[128,1024]{1,0:T(8,128)(2,1)S(1)} %tie.24.refs_4_.refs_13_), channel_id=1, source_target_pairs={{0,8},{1,9},{2,10},{3,11},{4,12},{5,13},{6,14},{7,15},{8,0},{9,1},... | collective-permute-start | bytes 786440 | tf_op jit(solution)/shard_map/ppermute | solution.py:57
  45.6 9.7 %collective-permute-start.15 = (bf16[128,1024]{1,0:T(8,128)(2,1)S(1)}, bf16[128,1024]{1,0:T(8,128)(2,1)S(1)}, u32[]{:S(2)}, u32[]{:S(2)}) collective-permute-start(bf16[128,1024]{1,0:T(8,128)(2,1)S(1)} %tie.22.refs_1_.refs_5_.refs_14_), channel_id=1, source_target_pairs={{0,2},{1,3},{2,4},{3,5},{4,6},{5,7},{6,0},{7,1},{8,10},{9,11},{10,... | collective-permute-start | bytes 786440 | tf_op jit(solution)/shard_map/ppermute | solution.py:57
  73.5 4.3 %collective-permute-start.23 = (f32[1,2048]{1,0:T(1,128)S(1)}, f32[1,2048]{1,0:T(1,128)S(1)}, u32[]{:S(2)}, u32[]{:S(2)}) collective-permute-start(f32[1,2048]{1,0:T(1,128)S(1)} %join_cores.4.refs_2_), channel_id=1, source_target_pairs={{0,4},{1,5},{2,6},{3,7},{4,0},{5,1},{6,2},{7,3},{8,12},{9,13},{10,... | collective-permute-start | bytes 24584 | tf_op jit(solution)/shard_map/ppermute | solution.py:57
  84.0 5.2 %collective-permute-start.27 = (f32[1,2048]{1,0:T(1,128)S(1)}, f32[1,2048]{1,0:T(1,128)S(1)}, u32[]{:S(2)}, u32[]{:S(2)}) collective-permute-start(f32[1,2048]{1,0:T(1,128)S(1)} %join_cores.5.refs_2_), channel_id=1, source_target_pairs={{0,4},{1,5},{2,6},{3,7},{4,0},{5,1},{6,2},{7,3},{8,12},{9,13},{10,... | collective-permute-start | bytes 24584 | tf_op jit(solution)/shard_map/ppermute | solution.py:57
  85.0 4.2 %collective-permute-start.29 = (f32[1,2048]{1,0:T(1,128)S(1)}, f32[1,2048]{1,0:T(1,128)S(1)}, u32[]{:S(2)}, u32[]{:S(2)}) collective-permute-start(f32[1,2048]{1,0:T(1,128)S(1)} %collective-permute-done.28.refs_4_), channel_id=1, source_target_pairs={{0,8},{1,9},{2,10},{3,11},{4,12},{5,13},{6,14},{7,15},{8,0},{9,1},... | collective-permute-start | bytes 24584 | tf_op jit(solution)/shard_map/ppermute | solution.py:57
  94.6 9.5 %collective-permute-start.31 = (bf16[512,256]{1,0:T(8,128)(2,1)S(1)}, bf16[512,256]{1,0:T(8,128)(2,1)S(1)}, u32[]{:S(2)}, u32[]{:S(2)}) collective-permute-start(bf16[512,256]{1,0:T(8,128)(2,1)S(1)} %combine.8.refs_3_.refs_4_), channel_id=1, source_target_pairs={{0,2},{1,3},{2,4},{3,5},{4,6},{5,7},{6,0},{7,1},{8,10},{9,11},{10,... | collective-permute-start | bytes 786440 | tf_op jit(solution)/shard_map/ppermute | solution.py:57
  97.9 8.0 %collective-permute-start.33 = (bf16[512,256]{1,0:T(8,128)(2,1)S(1)}, bf16[512,256]{1,0:T(8,128)(2,1)S(1)}, u32[]{:S(2)}, u32[]{:S(2)}) collective-permute-start(bf16[512,256]{1,0:T(8,128)(2,1)S(1)} %get-tuple-element.66), channel_id=1, source_target_pairs={{0,8},{1,9},{2,10},{3,11},{4,12},{5,13},{6,14},{7,15},{8,0},{9,1},... | collective-permute-start | bytes 786440 | tf_op jit(solution)/shard_map/ppermute | solution.py:57
  99.2 10.7 %collective-permute-start.36 = (bf16[528,256]{1,0:T(8,128)(2,1)S(1)}, bf16[528,256]{1,0:T(8,128)(2,1)S(1)}, u32[]{:S(2)}, u32[]{:S(2)}) collective-permute-start(bf16[528,256]{1,0:T(8,128)(2,1)S(1)} %combine.9.refs_4_.refs_5_), channel_id=1, source_target_pairs={{0,2},{1,3},{2,4},{3,5},{4,6},{5,7},{6,0},{7,1},{8,10},{9,11},{10,... | collective-permute-start | bytes 811016 | tf_op jit(solution)/shard_map/ppermute | solution.py:57
  99.5 6.6 %collective-permute-start.37 = (bf16[528,256]{1,0:T(8,128)(2,1)S(1)}, bf16[528,256]{1,0:T(8,128)(2,1)S(1)}, u32[]{:S(2)}, u32[]{:S(2)}) collective-permute-start(bf16[528,256]{1,0:T(8,128)(2,1)S(1)} %get-tuple-element.74), channel_id=1, source_target_pairs={{0,8},{1,9},{2,10},{3,11},{4,12},{5,13},{6,14},{7,15},{8,0},{9,1},... | collective-permute-start | bytes 811016 | tf_op jit(solution)/shard_map/ppermute | solution.py:57
  99.8 11.2 %collective-permute-start.44 = (bf16[528,256]{1,0:T(8,128)(2,1)S(1)}, bf16[528,256]{1,0:T(8,128)(2,1)S(1)}, u32[]{:S(2)}, u32[]{:S(2)}) collective-permute-start(bf16[528,256]{1,0:T(8,128)(2,1)S(1)} %get-tuple-element.77), channel_id=1, source_target_pairs={{0,8},{1,9},{2,10},{3,11},{4,12},{5,13},{6,14},{7,15},{8,0},{9,1},... | collective-permute-start | bytes 811016 | tf_op jit(solution)/shard_map/ppermute | solution.py:57
  104.1 7.2 %collective-permute-start.35 = (bf16[512,256]{1,0:T(8,128)(2,1)S(1)}, bf16[512,256]{1,0:T(8,128)(2,1)S(1)}, u32[]{:S(2)}, u32[]{:S(2)}) collective-permute-start(bf16[512,256]{1,0:T(8,128)(2,1)S(1)} %get-tuple-element.73), channel_id=1, source_target_pairs={{0,8},{1,9},{2,10},{3,11},{4,12},{5,13},{6,14},{7,15},{8,0},{9,1},... | collective-permute-start | bytes 786440 | tf_op jit(solution)/shard_map/ppermute | solution.py:57
  106.0 9.8 %collective-permute-start.34 = (bf16[512,256]{1,0:T(8,128)(2,1)S(1)}, bf16[512,256]{1,0:T(8,128)(2,1)S(1)}, u32[]{:S(2)}, u32[]{:S(2)}) collective-permute-start(bf16[512,256]{1,0:T(8,128)(2,1)S(1)} %combine.10.refs_3_.refs_2_), channel_id=1, source_target_pairs={{0,2},{1,3},{2,4},{3,5},{4,6},{5,7},{6,0},{7,1},{8,10},{9,11},{10,... | collective-permute-start | bytes 786440 | tf_op jit(solution)/shard_map/ppermute | solution.py:57
  106.1 14.1 %collective-permute-start.42 = (bf16[528,256]{1,0:T(8,128)(2,1)S(1)}, bf16[528,256]{1,0:T(8,128)(2,1)S(1)}, u32[]{:S(2)}, u32[]{:S(2)}) collective-permute-start(bf16[528,256]{1,0:T(8,128)(2,1)S(1)} %get-tuple-element.76), channel_id=1, source_target_pairs={{0,8},{1,9},{2,10},{3,11},{4,12},{5,13},{6,14},{7,15},{8,0},{9,1},... | collective-permute-start | bytes 811016 | tf_op jit(solution)/shard_map/ppermute | solution.py:57
  109.9 6.1 %collective-permute-start.39 = (bf16[512,256]{1,0:T(8,128)(2,1)S(1)}, bf16[512,256]{1,0:T(8,128)(2,1)S(1)}, u32[]{:S(2)}, u32[]{:S(2)}) collective-permute-start(bf16[512,256]{1,0:T(8,128)(2,1)S(1)} %get-tuple-element.75), channel_id=1, source_target_pairs={{0,8},{1,9},{2,10},{3,11},{4,12},{5,13},{6,14},{7,15},{8,0},{9,1},... | collective-permute-start | bytes 786440 | tf_op jit(solution)/shard_map/ppermute | solution.py:57
  111.1 10.5 %collective-permute-start.41 = (bf16[528,256]{1,0:T(8,128)(2,1)S(1)}, bf16[528,256]{1,0:T(8,128)(2,1)S(1)}, u32[]{:S(2)}, u32[]{:S(2)}) collective-permute-start(bf16[528,256]{1,0:T(8,128)(2,1)S(1)} %combine.11.refs_4_.refs_3_), channel_id=1, source_target_pairs={{0,2},{1,3},{2,4},{3,5},{4,6},{5,7},{6,0},{7,1},{8,10},{9,11},{10,... | collective-permute-start | bytes 811016 | tf_op jit(solution)/shard_map/ppermute | solution.py:57
  111.2 17.3 %collective-permute-start.45 = (bf16[528,256]{1,0:T(8,128)(2,1)S(1)}, bf16[528,256]{1,0:T(8,128)(2,1)S(1)}, u32[]{:S(2)}, u32[]{:S(2)}) collective-permute-start(bf16[528,256]{1,0:T(8,128)(2,1)S(1)} %combine.15), channel_id=1, source_target_pairs={{0,0},{1,8},{2,2},{3,10},{4,4},{5,12},{6,6},{7,14},{8,1},{9,9},{10... | collective-permute-start | bytes 811016 | tf_op jit(solution)/shard_map/ppermute | solution.py:57
  115.9 12.6 %collective-permute-start.38 = (bf16[512,256]{1,0:T(8,128)(2,1)S(1)}, bf16[512,256]{1,0:T(8,128)(2,1)S(1)}, u32[]{:S(2)}, u32[]{:S(2)}) collective-permute-start(bf16[512,256]{1,0:T(8,128)(2,1)S(1)} %combine.12.refs_3_), channel_id=1, source_target_pairs={{0,2},{1,10},{2,4},{3,12},{4,6},{5,14},{6,0},{7,8},{8,3},{9,11},{1... | collective-permute-start | bytes 786440 | tf_op jit(solution)/shard_map/ppermute | solution.py:57
  116.1 12.5 %collective-permute-start.40 = (bf16[512,256]{1,0:T(8,128)(2,1)S(1)}, bf16[512,256]{1,0:T(8,128)(2,1)S(1)}, u32[]{:S(2)}, u32[]{:S(2)}) collective-permute-start(bf16[512,256]{1,0:T(8,128)(2,1)S(1)} %combine.13), channel_id=1, source_target_pairs={{0,0},{1,8},{2,2},{3,10},{4,4},{5,12},{6,6},{7,14},{8,1},{9,9},{10... | collective-permute-start | bytes 786440 | tf_op jit(solution)/shard_map/ppermute | solution.py:57
  121.7 12.2 %collective-permute-start.43 = (bf16[528,256]{1,0:T(8,128)(2,1)S(1)}, bf16[528,256]{1,0:T(8,128)(2,1)S(1)}, u32[]{:S(2)}, u32[]{:S(2)}) collective-permute-start(bf16[528,256]{1,0:T(8,128)(2,1)S(1)} %combine.14), channel_id=1, source_target_pairs={{0,2},{1,10},{2,4},{3,12},{4,6},{5,14},{6,0},{7,8},{8,3},{9,11},{1... | collective-permute-start | bytes 811016 | tf_op jit(solution)/shard_map/ppermute | solution.py:57
  (16 other events, 37.4 us)

commit v5 on v4

--- a/solution.py
+++ b/solution.py
@@ -128,9 +128,10 @@
 
 
 def unit_kernel(rows_ref, *outs):
-    height = outs[0].shape[0]
-    for j, out_ref in enumerate(outs):
-        out_ref[...] = unit(rows_ref[pl.ds(j * height, height), :])
+    start = 0
+    for out_ref in outs:
+        out_ref[...] = unit(rows_ref[pl.ds(start, out_ref.shape[0]), :])
+        start += out_ref.shape[0]
 
 
 def rank_kernel(level_ref, place_ref):
@@ -163,7 +164,7 @@
     inputs = refs[4 if carried else 0 :]
     pieces = inputs[len(raw) :]
     each = len(pieces) // (2 * len(columns))
-    height = pieces[0].shape[0]
+    height = sum(p.shape[0] for p in pieces[:each]) // each
     capacity, depth = unit_ref.shape[0] // groups, unit_ref.shape[1]
     pick = lax.broadcasted_iota(jnp.int32, (16, 128), 0) + lax.broadcasted_iota(
         jnp.int32, (16, 128), 1
@@ -346,6 +347,7 @@
     clusters = owned * peers
     parts = 2
 
+    small = max(16, owned * 6 // 256 * 16)
     swapped = send(centroids, routes.swap)
 
     place = call(
@@ -373,7 +375,7 @@
 
     own = call(
         unit_kernel,
-        (shape(owned // parts, depth),) * parts,
+        (shape(small, depth), shape(owned - small, depth)),
         [swapped],
         after=[packed[0]],
         name="unit_centroids",

time: 136 us -> 134 us (0.985)
  waiting for transfers between devices: 52.8 us -> 47.9 us
  starting transfers between devices: 47.8 us -> 51.1 us
    ppermute x46, waiting for transfers between devices: 52.8 us -> 47.9 us  [send(): return lax.ppermute(value, AXES, route)]
    ppermute x46, starting transfers between devices: 47.8 us -> 51.1 us  [send(): return lax.ppermute(value, AXES, route)]
  transfers between devices with their start and end apart: 46 -> 46, of which waited for: 25 -> 23; matrix products, arithmetic and copies ran while one was open for 0% -> 0% of each run, Pallas kernels for 15% -> 15%
where the time goes in v5:
time: 134 us
  starting transfers between devices  51.1 us (38%)
  waiting for transfers between devices  47.9 us (36%)
  Pallas kernels  31.6 us (24%)
  local copies, waits for them, and re-layouts  2.09 us (2%)
    ppermute x46, starting transfers between devices, send(): return lax.ppermute(value, AXES, route)  51.1 us
    ppermute x46, waiting for transfers between devices, send(): return lax.ppermute(value, AXES, route)  47.9 us
    pallas_call x35, Pallas kernels, call(): pl.pallas_call(ordered, out_shape=outs, in_specs=(specs or [VMEM] * len(a...  31.5 us
  transfers between devices with their start and end apart: 46, of which 23 were waited for; matrix products, arithmetic and copies ran while one was open for 0% of the time, Pallas kernels for 15%

profile of v5, /device:TPU:1, one launch (start us, length us, event | category | flops | bytes accessed | tf_op | source)
XLA Modules:
  0.0 133.7 jit_solution(659251534046075260)
XLA Ops:
  0.6 4.5 %collective-permute-start.3 = (bf16[256,1024]{1,0:T(8,128)(2,1)}, bf16[256,1024]{1,0:T(8,128)(2,1)S(1)}, u32[]{:S(2)}, u32[]{:S(2)}) collective-permute-start(bf16[256,1024]{1,0:T(8,128)(2,1)} %param.5), channel_id=1, source_target_pairs={{0,0},{1,8},{2,2},{3,10},{4,4},{5,12},{6,6},{7,14},{8,1},{9,9},{10... | collective-permute-start | bytes 1572872 | tf_op jit(solution)/shard_map/ppermute | solution.py:57
  16.3 2.5 %collective-permute-done.4.refs_0_ = bf16[96,1024]{1,0:T(8,128)(2,1)S(1)} collective-permute-done((bf16[96,1024]{1,0:T(8,128)(2,1)S(1)}, bf16[96,1024]{1,0:T(8,128)(2,1)S(1)}, u32[]{:S(2)}, u32[]{:S(2)}) %collective-permute-start.4) | collective-permute-done | bytes 196640 | tf_op jit(solution)/shard_map/ppermute | solution.py:57
  18.8 2.0 %collective-permute-start.6 = (bf16[96,1024]{1,0:T(8,128)(2,1)S(1)}, bf16[96,1024]{1,0:T(8,128)(2,1)S(1)}, u32[]{:S(2)}, u32[]{:S(2)}) collective-permute-start(bf16[96,1024]{1,0:T(8,128)(2,1)S(1)} %tie.17.refs_3_.refs_5_), channel_id=1, source_target_pairs={{0,8},{1,9},{2,10},{3,11},{4,12},{5,13},{6,14},{7,15},{8,0},{9,1},... | collective-permute-start | bytes 589832 | tf_op jit(solution)/shard_map/ppermute | solution.py:57
  20.8 2.5 %collective-permute-done.5.refs_0_ = bf16[160,1024]{1,0:T(8,128)(2,1)S(1)} collective-permute-done((bf16[160,1024]{1,0:T(8,128)(2,1)S(1)}, bf16[160,1024]{1,0:T(8,128)(2,1)S(1)}, u32[]{:S(2)}, u32[]{:S(2)}) %collective-permute-start.5) | collective-permute-done | bytes 327712 | tf_op jit(solution)/shard_map/ppermute | solution.py:57
  23.3 4.2 %collective-permute-done.8.refs_0_ = bf16[96,1024]{1,0:T(8,128)(2,1)S(1)} collective-permute-done((bf16[96,1024]{1,0:T(8,128)(2,1)S(1)}, bf16[96,1024]{1,0:T(8,128)(2,1)S(1)}, u32[]{:S(2)}, u32[]{:S(2)}) %collective-permute-start.8) | collective-permute-done | bytes 196640 | tf_op jit(solution)/shard_map/ppermute | solution.py:57
  27.6 4.9 %collective-permute-done.refs_2_.refs_1_ = bf16[384,1024]{1,0:T(8,128)(2,1)S(1)} collective-permute-done((bf16[384,1024]{1,0:T(8,128)(2,1)S(1)}, bf16[384,1024]{1,0:T(8,128)(2,1)S(1)}, u32[]{:S(2)}, u32[]{:S(2)}) %collective-permute-start) | collective-permute-done | bytes 786464 | tf_op jit(solution)/shard_map/ppermute | solution.py:57
  32.5 2.1 %collective-permute-start.2 = (bf16[384,1024]{1,0:T(8,128)(2,1)S(1)}, bf16[384,1024]{1,0:T(8,128)(2,1)S(1)}, u32[]{:S(2)}, u32[]{:S(2)}) collective-permute-start(bf16[384,1024]{1,0:T(8,128)(2,1)S(1)} %tie.14), channel_id=1, source_target_pairs={{0,17},{1,16},{2,19},{3,18},{4,21},{5,20},{6,23},{7,22},{8,25},{9,... | collective-permute-start | bytes 2359304 | tf_op jit(solution)/shard_map/ppermute | solution.py:57
  34.6 1.8 %collective-permute-start.10 = (bf16[96,1024]{1,0:T(8,128)(2,1)S(1)}, bf16[96,1024]{1,0:T(8,128)(2,1)S(1)}, u32[]{:S(2)}, u32[]{:S(2)}) collective-permute-start(bf16[96,1024]{1,0:T(8,128)(2,1)S(1)} %tie.21.refs_7_.refs_9_), channel_id=1, source_target_pairs={{0,8},{1,9},{2,10},{3,11},{4,12},{5,13},{6,14},{7,15},{8,0},{9,1},... | collective-permute-start | bytes 589832 | tf_op jit(solution)/shard_map/ppermute | solution.py:57
  36.4 3.8 %collective-permute-start.7 = (bf16[160,1024]{1,0:T(8,128)(2,1)S(1)}, bf16[160,1024]{1,0:T(8,128)(2,1)S(1)}, u32[]{:S(2)}, u32[]{:S(2)}) collective-permute-start(bf16[160,1024]{1,0:T(8,128)(2,1)S(1)} %tie.19.refs_4_.refs_6_), channel_id=1, source_target_pairs={{0,8},{1,9},{2,10},{3,11},{4,12},{5,13},{6,14},{7,15},{8,0},{9,1},... | collective-permute-start | bytes 983048 | tf_op jit(solution)/shard_map/ppermute | solution.py:57
  40.3 2.0 %collective-permute-start.14 = (bf16[160,1024]{1,0:T(8,128)(2,1)S(1)}, bf16[160,1024]{1,0:T(8,128)(2,1)S(1)}, u32[]{:S(2)}, u32[]{:S(2)}) collective-permute-start(bf16[160,1024]{1,0:T(8,128)(2,1)S(1)} %tie.22.refs_1_.refs_5_.refs_14_), channel_id=1, source_target_pairs={{0,8},{1,9},{2,10},{3,11},{4,12},{5,13},{6,14},{7,15},{8,0},{9,1},... | collective-permute-start | bytes 983048 | tf_op jit(solution)/shard_map/ppermute | solution.py:57
  42.5 3.8 %weights.4 = (bf16[1536,1024]{1,0:T(8,128)(2,1)S(1)}, f32[1,1536]{1,0:T(1,128)S(1)}, bf16[1536,2048]{1,0:T(8,128)(2,1)S(1)}, f32[1,2048]{1,0:T(1,128)S(1)}) custom-call(bf16[384,1024]{1,0:T(8,128)(2,1)S(1)} %pick_rows.7.refs_0_.refs_1_, bf16[384,1024]{1,0:T(8,128)(2,1)S(1)} %collective-permute-done.refs_2_.refs_1_, ...), custom_call_target="tpu_custom_call" | custom-call | tf_op jit(solution)/shard_map/weights/pallas_call | solution.py:72
  46.2 1.6 %weights.5 = (bf16[1536,1024]{1,0:T(8,128)(2,1)S(1)}, f32[1,1536]{1,0:T(1,128)S(1)}, bf16[1536,2048]{1,0:T(8,128)(2,1)S(1)}, f32[1,2048]{1,0:T(1,128)S(1)}) custom-call(bf16[1536,1024]{1,0:T(8,128)(2,1)S(1)} %get-tuple-element.43.refs_0_, ...), custom_call_target="tpu_custom_call", output_to_operand_aliasing={{0}: (0, {}), {1}: (1, {}), {2}: (2, {}), {3}: (3, {})} | custom-call | tf_op jit(solution)/shard_map/weights/pallas_call | solution.py:72
  47.8 3.0 %collective-permute-done.2.refs_0_ = bf16[384,1024]{1,0:T(8,128)(2,1)S(1)} collective-permute-done((bf16[384,1024]{1,0:T(8,128)(2,1)S(1)}, bf16[384,1024]{1,0:T(8,128)(2,1)S(1)}, u32[]{:S(2)}, u32[]{:S(2)}) %collective-permute-start.2) | collective-permute-done | bytes 786464 | tf_op jit(solution)/shard_map/ppermute | solution.py:57
  50.8 1.8 %weights.6 = (bf16[1536,1024]{1,0:T(8,128)(2,1)S(1)}, f32[1,1536]{1,0:T(1,128)S(1)}, bf16[1536,2048]{1,0:T(8,128)(2,1)S(1)}, f32[1,2048]{1,0:T(1,128)S(1)}) custom-call(bf16[1536,1024]{1,0:T(8,128)(2,1)S(1)} %get-tuple-element.47.refs_0_, ...), custom_call_target="tpu_custom_call", output_to_operand_aliasing={{0}: (0, {}), {1}: (1, {}), {2}: (2, {}), {3}: (3, {})} | custom-call | tf_op jit(solution)/shard_map/weights/pallas_call | solution.py:72
  53.1 2.2 %collective-permute-start.17 = (bf16[160,1024]{1,0:T(8,128)(2,1)S(1)}, bf16[160,1024]{1,0:T(8,128)(2,1)S(1)}, u32[]{:S(2)}, u32[]{:S(2)}) collective-permute-start(bf16[160,1024]{1,0:T(8,128)(2,1)S(1)} %tie.26.refs_5_), channel_id=1, source_target_pairs={{0,8},{1,9},{2,10},{3,11},{4,12},{5,13},{6,14},{7,15},{8,0},{9,1},... | collective-permute-start | bytes 983048 | tf_op jit(solution)/shard_map/ppermute | solution.py:57
  56.8 2.0 %weights.7 = (bf16[1536,1024]{1,0:T(8,128)(2,1)S(1)}, f32[1,1536]{1,0:T(1,128)S(1)}, bf16[1536,2048]{1,0:T(8,128)(2,1)S(1)}, f32[1,2048]{1,0:T(1,128)S(1)}) custom-call(bf16[1536,1024]{1,0:T(8,128)(2,1)S(1)} %get-tuple-element.51.refs_0_, ...), custom_call_target="tpu_custom_call", output_to_operand_aliasing={{0}: (0, {}), {1}: (1, {}), {2}: (2, {}), {3}: (3, {})} | custom-call | tf_op jit(solution)/shard_map/weights/pallas_call | solution.py:72
  60.0 2.3 %collective-permute-start.20 = (f32[1,2048]{1,0:T(1,128)S(1)}, f32[1,2048]{1,0:T(1,128)S(1)}, u32[]{:S(2)}, u32[]{:S(2)}) collective-permute-start(f32[1,2048]{1,0:T(1,128)S(1)} %join_cores.3.refs_2_), channel_id=1, source_target_pairs={{0,2},{1,3},{2,4},{3,5},{4,6},{5,7},{6,0},{7,1},{8,14},{9,15},{10,... | collective-permute-start | bytes 24584 | tf_op jit(solution)/shard_map/ppermute | solution.py:57
  63.1 2.7 %collective-permute-start.21 = (f32[1,2048]{1,0:T(1,128)S(1)}, f32[1,2048]{1,0:T(1,128)S(1)}, u32[]{:S(2)}, u32[]{:S(2)}) collective-permute-start(f32[1,2048]{1,0:T(1,128)S(1)} %collective-permute-done.20.refs_4_), channel_id=1, source_target_pairs={{0,8},{1,9},{2,10},{3,11},{4,12},{5,13},{6,14},{7,15},{8,0},{9,1},... | collective-permute-start | bytes 24584 | tf_op jit(solution)/shard_map/ppermute | solution.py:57
  66.7 2.6 %sweep.2.refs_0_ = f32[1,2048]{1,0:T(1,128)S(1)} custom-call(f32[1,1536]{1,0:T(1,128)S(1)} %get-tuple-element.56.refs_0_, bf16[1536,2048]{1,0:T(8,128)(2,1)S(1)} %get-tuple-element.55.refs_1_.refs_2_, f32[1,2048]{1,0:T(1,128)S(1)} %join_cores.3.refs_2_, f32[1,2048]{1,0:T(1,128)S(1)} %collective-permute-done.19.refs_3_, ...), custom_call_target="tpu_custom_call" | custom-call | tf_op jit(solution)/shard_map/sweep/pallas_call | solution.py:72
  70.5 1.5 %collective-permute-start.24 = (f32[1,2048]{1,0:T(1,128)S(1)}, f32[1,2048]{1,0:T(1,128)S(1)}, u32[]{:S(2)}, u32[]{:S(2)}) collective-permute-start(f32[1,2048]{1,0:T(1,128)S(1)} %join_cores.4.refs_2_), channel_id=1, source_target_pairs={{0,2},{1,3},{2,4},{3,5},{4,6},{5,7},{6,0},{7,1},{8,14},{9,15},{10,... | collective-permute-start | bytes 24584 | tf_op jit(solution)/shard_map/ppermute | solution.py:57
  73.0 3.3 %collective-permute-start.25 = (f32[1,2048]{1,0:T(1,128)S(1)}, f32[1,2048]{1,0:T(1,128)S(1)}, u32[]{:S(2)}, u32[]{:S(2)}) collective-permute-start(f32[1,2048]{1,0:T(1,128)S(1)} %collective-permute-done.24.refs_4_), channel_id=1, source_target_pairs={{0,8},{1,9},{2,10},{3,11},{4,12},{5,13},{6,14},{7,15},{8,0},{9,1},... | collective-permute-start | bytes 24584 | tf_op jit(solution)/shard_map/ppermute | solution.py:57
  77.1 2.6 %sweep.3.refs_0_ = f32[1,2048]{1,0:T(1,128)S(1)} custom-call(f32[1,1536]{1,0:T(1,128)S(1)} %get-tuple-element.56.refs_0_, bf16[1536,2048]{1,0:T(8,128)(2,1)S(1)} %get-tuple-element.55.refs_1_.refs_2_, f32[1,2048]{1,0:T(1,128)S(1)} %join_cores.4.refs_2_, f32[1,2048]{1,0:T(1,128)S(1)} %collective-permute-done.23.refs_3_, ...), custom_call_target="tpu_custom_call" | custom-call | tf_op jit(solution)/shard_map/sweep/pallas_call | solution.py:72
  83.4 3.3 %collective-permute-start.29 = (f32[1,2048]{1,0:T(1,128)S(1)}, f32[1,2048]{1,0:T(1,128)S(1)}, u32[]{:S(2)}, u32[]{:S(2)}) collective-permute-start(f32[1,2048]{1,0:T(1,128)S(1)} %collective-permute-done.28.refs_4_), channel_id=1, source_target_pairs={{0,8},{1,9},{2,10},{3,11},{4,12},{5,13},{6,14},{7,15},{8,0},{9,1},... | collective-permute-start | bytes 24584 | tf_op jit(solution)/shard_map/ppermute | solution.py:57
  87.6 1.8 %last_sweep.1 = (f32[1,1536]{1,0:T(1,128)S(1)}, f32[1,2048]{1,0:T(1,128)S(1)}) custom-call(f32[1,1536]{1,0:T(1,128)S(1)} %get-tuple-element.56.refs_0_, bf16[1536,2048]{1,0:T(8,128)(2,1)S(1)} %get-tuple-element.55.refs_1_.refs_2_, f32[1,2048]{1,0:T(1,128)S(1)} %join_cores.5.refs_2_, f32[1,2048]{1,0:T(1,128)S(1)} %collective-permute-done.27.refs_3_, ...), custom_call_target="tpu_custom_call" | custom-call | tf_op jit(solution)/shard_map/last_sweep/pallas_call | solution.py:72
  102.5 1.8 %collective-permute-start.35 = (bf16[512,256]{1,0:T(8,128)(2,1)S(1)}, bf16[512,256]{1,0:T(8,128)(2,1)S(1)}, u32[]{:S(2)}, u32[]{:S(2)}) collective-permute-start(bf16[512,256]{1,0:T(8,128)(2,1)S(1)} %get-tuple-element.73), channel_id=1, source_target_pairs={{0,8},{1,9},{2,10},{3,11},{4,12},{5,13},{6,14},{7,15},{8,0},{9,1},... | collective-permute-start | bytes 786440 | tf_op jit(solution)/shard_map/ppermute | solution.py:57
  104.6 3.7 %collective-permute-done.36.refs_0_ = bf16[528,256]{1,0:T(8,128)(2,1)S(1)} collective-permute-done((bf16[528,256]{1,0:T(8,128)(2,1)S(1)}, bf16[528,256]{1,0:T(8,128)(2,1)S(1)}, u32[]{:S(2)}, u32[]{:S(2)}) %collective-permute-start.36) | collective-permute-done | bytes 270368 | tf_op jit(solution)/shard_map/ppermute | solution.py:57
  109.7 2.9 %collective-permute-start.45 = (bf16[528,256]{1,0:T(8,128)(2,1)S(1)}, bf16[528,256]{1,0:T(8,128)(2,1)S(1)}, u32[]{:S(2)}, u32[]{:S(2)}) collective-permute-start(bf16[528,256]{1,0:T(8,128)(2,1)S(1)} %combine.15), channel_id=1, source_target_pairs={{0,0},{1,8},{2,2},{3,10},{4,4},{5,12},{6,6},{7,14},{8,1},{9,9},{10... | collective-permute-start | bytes 811016 | tf_op jit(solution)/shard_map/ppermute | solution.py:57
  112.6 1.6 %collective-permute-done.34.refs_0_ = bf16[512,256]{1,0:T(8,128)(2,1)S(1)} collective-permute-done((bf16[512,256]{1,0:T(8,128)(2,1)S(1)}, bf16[512,256]{1,0:T(8,128)(2,1)S(1)}, u32[]{:S(2)}, u32[]{:S(2)}) %collective-permute-start.34) | collective-permute-done | bytes 262176 | tf_op jit(solution)/shard_map/ppermute | solution.py:57
  114.5 4.0 %collective-permute-start.40 = (bf16[512,256]{1,0:T(8,128)(2,1)S(1)}, bf16[512,256]{1,0:T(8,128)(2,1)S(1)}, u32[]{:S(2)}, u32[]{:S(2)}) collective-permute-start(bf16[512,256]{1,0:T(8,128)(2,1)S(1)} %combine.13), channel_id=1, source_target_pairs={{0,0},{1,8},{2,2},{3,10},{4,4},{5,12},{6,6},{7,14},{8,1},{9,9},{10... | collective-permute-start | bytes 786440 | tf_op jit(solution)/shard_map/ppermute | solution.py:57
  118.6 1.5 %collective-permute-done.41.refs_0_ = bf16[528,256]{1,0:T(8,128)(2,1)S(1)} collective-permute-done((bf16[528,256]{1,0:T(8,128)(2,1)S(1)}, bf16[528,256]{1,0:T(8,128)(2,1)S(1)}, u32[]{:S(2)}, u32[]{:S(2)}) %collective-permute-start.41) | collective-permute-done | bytes 270368 | tf_op jit(solution)/shard_map/ppermute | solution.py:57
  120.2 6.7 %collective-permute-done.38.refs_0_ = bf16[512,256]{1,0:T(8,128)(2,1)S(1)} collective-permute-done((bf16[512,256]{1,0:T(8,128)(2,1)S(1)}, bf16[512,256]{1,0:T(8,128)(2,1)S(1)}, u32[]{:S(2)}, u32[]{:S(2)}) %collective-permute-start.38) | collective-permute-done | bytes 262176 | tf_op jit(solution)/shard_map/ppermute | solution.py:57
  126.9 5.4 %collective-permute-done.43.refs_2_ = bf16[528,256]{1,0:T(8,128)(2,1)S(1)} collective-permute-done((bf16[528,256]{1,0:T(8,128)(2,1)S(1)}, bf16[528,256]{1,0:T(8,128)(2,1)S(1)}, u32[]{:S(2)}, u32[]{:S(2)}) %collective-permute-start.43) | collective-permute-done | bytes 270368 | tf_op jit(solution)/shard_map/ppermute | solution.py:57
  (113 shorter events, 40.2 us)
Async XLA Ops:
  0.6 11.6 %collective-permute-start.3 = (bf16[256,1024]{1,0:T(8,128)(2,1)}, bf16[256,1024]{1,0:T(8,128)(2,1)S(1)}, u32[]{:S(2)}, u32[]{:S(2)}) collective-permute-start(bf16[256,1024]{1,0:T(8,128)(2,1)} %param.5), channel_id=1, source_target_pairs={{0,0},{1,8},{2,2},{3,10},{4,4},{5,12},{6,6},{7,14},{8,1},{9,9},{10... | collective-permute-start | bytes 1572872 | tf_op jit(solution)/shard_map/ppermute | solution.py:57
  12.4 6.4 %collective-permute-start.4 = (bf16[96,1024]{1,0:T(8,128)(2,1)S(1)}, bf16[96,1024]{1,0:T(8,128)(2,1)S(1)}, u32[]{:S(2)}, u32[]{:S(2)}) collective-permute-start(bf16[96,1024]{1,0:T(8,128)(2,1)S(1)} %get-tuple-element.41.refs_0_), channel_id=1, source_target_pairs={{0,2},{1,3},{2,4},{3,5},{4,6},{5,7},{6,0},{7,1},{8,10},{9,11},{10,... | collective-permute-start | bytes 589832 | tf_op jit(solution)/shard_map/ppermute | solution.py:57
  13.8 18.7 %collective-permute-start = (bf16[384,1024]{1,0:T(8,128)(2,1)S(1)}, bf16[384,1024]{1,0:T(8,128)(2,1)S(1)}, u32[]{:S(2)}, u32[]{:S(2)}) collective-permute-start(bf16[384,1024]{1,0:T(8,128)(2,1)S(1)} %pick_rows.5.refs_2_), channel_id=1, source_target_pairs={{0,1},{1,0},{2,3},{3,2},{4,5},{5,4},{6,7},{7,6},{8,9},{9,8},{10,11... | collective-permute-start | bytes 2359304 | tf_op jit(solution)/shard_map/ppermute | solution.py:57
  13.8 18.7 %collective-permute-start.1 = (bf16[384,1024]{1,0:T(8,128)(2,1)S(1)}, bf16[384,1024]{1,0:T(8,128)(2,1)S(1)}, u32[]{:S(2)}, u32[]{:S(2)}) collective-permute-start(bf16[384,1024]{1,0:T(8,128)(2,1)S(1)} %pick_rows.4.refs_2_), channel_id=1, source_target_pairs={{0,16},{1,17},{2,18},{3,19},{4,20},{5,21},{6,22},{7,23},{8,24},{9,... | collective-permute-start | bytes 2359304 | tf_op jit(solution)/shard_map/ppermute | solution.py:57
  15.0 8.3 %collective-permute-start.5 = (bf16[160,1024]{1,0:T(8,128)(2,1)S(1)}, bf16[160,1024]{1,0:T(8,128)(2,1)S(1)}, u32[]{:S(2)}, u32[]{:S(2)}) collective-permute-start(bf16[160,1024]{1,0:T(8,128)(2,1)S(1)} %get-tuple-element.42.refs_0_), channel_id=1, source_target_pairs={{0,2},{1,3},{2,4},{3,5},{4,6},{5,7},{6,0},{7,1},{8,10},{9,11},{10,... | collective-permute-start | bytes 983048 | tf_op jit(solution)/shard_map/ppermute | solution.py:57
  18.8 8.7 %collective-permute-start.8 = (bf16[96,1024]{1,0:T(8,128)(2,1)S(1)}, bf16[96,1024]{1,0:T(8,128)(2,1)S(1)}, u32[]{:S(2)}, u32[]{:S(2)}) collective-permute-start(bf16[96,1024]{1,0:T(8,128)(2,1)S(1)} %tie.16.refs_1_.refs_0_), channel_id=1, source_target_pairs={{0,2},{1,3},{2,4},{3,5},{4,6},{5,7},{6,0},{7,1},{8,10},{9,11},{10,... | collective-permute-start | bytes 589832 | tf_op jit(solution)/shard_map/ppermute | solution.py:57
  18.8 21.4 %collective-permute-start.6 = (bf16[96,1024]{1,0:T(8,128)(2,1)S(1)}, bf16[96,1024]{1,0:T(8,128)(2,1)S(1)}, u32[]{:S(2)}, u32[]{:S(2)}) collective-permute-start(bf16[96,1024]{1,0:T(8,128)(2,1)S(1)} %tie.17.refs_3_.refs_5_), channel_id=1, source_target_pairs={{0,8},{1,9},{2,10},{3,11},{4,12},{5,13},{6,14},{7,15},{8,0},{9,1},... | collective-permute-start | bytes 589832 | tf_op jit(solution)/shard_map/ppermute | solution.py:57
  23.3 13.1 %collective-permute-start.9 = (bf16[160,1024]{1,0:T(8,128)(2,1)S(1)}, bf16[160,1024]{1,0:T(8,128)(2,1)S(1)}, u32[]{:S(2)}, u32[]{:S(2)}) collective-permute-start(bf16[160,1024]{1,0:T(8,128)(2,1)S(1)} %tie.18.refs_1_.refs_0_), channel_id=1, source_target_pairs={{0,2},{1,3},{2,4},{3,5},{4,6},{5,7},{6,0},{7,1},{8,10},{9,11},{10,... | collective-permute-start | bytes 983048 | tf_op jit(solution)/shard_map/ppermute | solution.py:57
  27.6 12.8 %collective-permute-start.12 = (bf16[96,1024]{1,0:T(8,128)(2,1)S(1)}, bf16[96,1024]{1,0:T(8,128)(2,1)S(1)}, u32[]{:S(2)}, u32[]{:S(2)}) collective-permute-start(bf16[96,1024]{1,0:T(8,128)(2,1)S(1)} %tie.20.refs_1_.refs_0_), channel_id=1, source_target_pairs={{0,2},{1,3},{2,4},{3,5},{4,6},{5,7},{6,0},{7,1},{8,10},{9,11},{10,... | collective-permute-start | bytes 589832 | tf_op jit(solution)/shard_map/ppermute | solution.py:57
  32.5 18.3 %collective-permute-start.2 = (bf16[384,1024]{1,0:T(8,128)(2,1)S(1)}, bf16[384,1024]{1,0:T(8,128)(2,1)S(1)}, u32[]{:S(2)}, u32[]{:S(2)}) collective-permute-start(bf16[384,1024]{1,0:T(8,128)(2,1)S(1)} %tie.14), channel_id=1, source_target_pairs={{0,17},{1,16},{2,19},{3,18},{4,21},{5,20},{6,23},{7,22},{8,25},{9,... | collective-permute-start | bytes 2359304 | tf_op jit(solution)/shard_map/ppermute | solution.py:57
  34.6 7.8 %collective-permute-start.10 = (bf16[96,1024]{1,0:T(8,128)(2,1)S(1)}, bf16[96,1024]{1,0:T(8,128)(2,1)S(1)}, u32[]{:S(2)}, u32[]{:S(2)}) collective-permute-start(bf16[96,1024]{1,0:T(8,128)(2,1)S(1)} %tie.21.refs_7_.refs_9_), channel_id=1, source_target_pairs={{0,8},{1,9},{2,10},{3,11},{4,12},{5,13},{6,14},{7,15},{8,0},{9,1},... | collective-permute-start | bytes 589832 | tf_op jit(solution)/shard_map/ppermute | solution.py:57
  36.4 6.0 %collective-permute-start.7 = (bf16[160,1024]{1,0:T(8,128)(2,1)S(1)}, bf16[160,1024]{1,0:T(8,128)(2,1)S(1)}, u32[]{:S(2)}, u32[]{:S(2)}) collective-permute-start(bf16[160,1024]{1,0:T(8,128)(2,1)S(1)} %tie.19.refs_4_.refs_6_), channel_id=1, source_target_pairs={{0,8},{1,9},{2,10},{3,11},{4,12},{5,13},{6,14},{7,15},{8,0},{9,1},... | collective-permute-start | bytes 983048 | tf_op jit(solution)/shard_map/ppermute | solution.py:57
  40.3 5.9 %collective-permute-start.14 = (bf16[160,1024]{1,0:T(8,128)(2,1)S(1)}, bf16[160,1024]{1,0:T(8,128)(2,1)S(1)}, u32[]{:S(2)}, u32[]{:S(2)}) collective-permute-start(bf16[160,1024]{1,0:T(8,128)(2,1)S(1)} %tie.22.refs_1_.refs_5_.refs_14_), channel_id=1, source_target_pairs={{0,8},{1,9},{2,10},{3,11},{4,12},{5,13},{6,14},{7,15},{8,0},{9,1},... | collective-permute-start | bytes 983048 | tf_op jit(solution)/shard_map/ppermute | solution.py:57
  42.4 10.6 %collective-permute-start.15 = (bf16[160,1024]{1,0:T(8,128)(2,1)S(1)}, bf16[160,1024]{1,0:T(8,128)(2,1)S(1)}, u32[]{:S(2)}, u32[]{:S(2)}) collective-permute-start(bf16[160,1024]{1,0:T(8,128)(2,1)S(1)} %tie.22.refs_1_.refs_5_.refs_14_), channel_id=1, source_target_pairs={{0,2},{1,3},{2,4},{3,5},{4,6},{5,7},{6,0},{7,1},{8,10},{9,11},{10,... | collective-permute-start | bytes 983048 | tf_op jit(solution)/shard_map/ppermute | solution.py:57
  72.0 4.3 %collective-permute-start.23 = (f32[1,2048]{1,0:T(1,128)S(1)}, f32[1,2048]{1,0:T(1,128)S(1)}, u32[]{:S(2)}, u32[]{:S(2)}) collective-permute-start(f32[1,2048]{1,0:T(1,128)S(1)} %join_cores.4.refs_2_), channel_id=1, source_target_pairs={{0,4},{1,5},{2,6},{3,7},{4,0},{5,1},{6,2},{7,3},{8,12},{9,13},{10,... | collective-permute-start | bytes 24584 | tf_op jit(solution)/shard_map/ppermute | solution.py:57
  73.0 4.1 %collective-permute-start.25 = (f32[1,2048]{1,0:T(1,128)S(1)}, f32[1,2048]{1,0:T(1,128)S(1)}, u32[]{:S(2)}, u32[]{:S(2)}) collective-permute-start(f32[1,2048]{1,0:T(1,128)S(1)} %collective-permute-done.24.refs_4_), channel_id=1, source_target_pairs={{0,8},{1,9},{2,10},{3,11},{4,12},{5,13},{6,14},{7,15},{8,0},{9,1},... | collective-permute-start | bytes 24584 | tf_op jit(solution)/shard_map/ppermute | solution.py:57
  82.4 5.2 %collective-permute-start.27 = (f32[1,2048]{1,0:T(1,128)S(1)}, f32[1,2048]{1,0:T(1,128)S(1)}, u32[]{:S(2)}, u32[]{:S(2)}) collective-permute-start(f32[1,2048]{1,0:T(1,128)S(1)} %join_cores.5.refs_2_), channel_id=1, source_target_pairs={{0,4},{1,5},{2,6},{3,7},{4,0},{5,1},{6,2},{7,3},{8,12},{9,13},{10,... | collective-permute-start | bytes 24584 | tf_op jit(solution)/shard_map/ppermute | solution.py:57
  83.4 4.2 %collective-permute-start.29 = (f32[1,2048]{1,0:T(1,128)S(1)}, f32[1,2048]{1,0:T(1,128)S(1)}, u32[]{:S(2)}, u32[]{:S(2)}) collective-permute-start(f32[1,2048]{1,0:T(1,128)S(1)} %collective-permute-done.28.refs_4_), channel_id=1, source_target_pairs={{0,8},{1,9},{2,10},{3,11},{4,12},{5,13},{6,14},{7,15},{8,0},{9,1},... | collective-permute-start | bytes 24584 | tf_op jit(solution)/shard_map/ppermute | solution.py:57
  93.0 9.5 %collective-permute-start.31 = (bf16[512,256]{1,0:T(8,128)(2,1)S(1)}, bf16[512,256]{1,0:T(8,128)(2,1)S(1)}, u32[]{:S(2)}, u32[]{:S(2)}) collective-permute-start(bf16[512,256]{1,0:T(8,128)(2,1)S(1)} %combine.8.refs_3_.refs_4_), channel_id=1, source_target_pairs={{0,2},{1,3},{2,4},{3,5},{4,6},{5,7},{6,0},{7,1},{8,10},{9,11},{10,... | collective-permute-start | bytes 786440 | tf_op jit(solution)/shard_map/ppermute | solution.py:57
  96.3 8.0 %collective-permute-start.33 = (bf16[512,256]{1,0:T(8,128)(2,1)S(1)}, bf16[512,256]{1,0:T(8,128)(2,1)S(1)}, u32[]{:S(2)}, u32[]{:S(2)}) collective-permute-start(bf16[512,256]{1,0:T(8,128)(2,1)S(1)} %get-tuple-element.66), channel_id=1, source_target_pairs={{0,8},{1,9},{2,10},{3,11},{4,12},{5,13},{6,14},{7,15},{8,0},{9,1},... | collective-permute-start | bytes 786440 | tf_op jit(solution)/shard_map/ppermute | solution.py:57
  97.6 10.7 %collective-permute-start.36 = (bf16[528,256]{1,0:T(8,128)(2,1)S(1)}, bf16[528,256]{1,0:T(8,128)(2,1)S(1)}, u32[]{:S(2)}, u32[]{:S(2)}) collective-permute-start(bf16[528,256]{1,0:T(8,128)(2,1)S(1)} %combine.9.refs_4_.refs_5_), channel_id=1, source_target_pairs={{0,2},{1,3},{2,4},{3,5},{4,6},{5,7},{6,0},{7,1},{8,10},{9,11},{10,... | collective-permute-start | bytes 811016 | tf_op jit(solution)/shard_map/ppermute | solution.py:57
  97.9 6.6 %collective-permute-start.37 = (bf16[528,256]{1,0:T(8,128)(2,1)S(1)}, bf16[528,256]{1,0:T(8,128)(2,1)S(1)}, u32[]{:S(2)}, u32[]{:S(2)}) collective-permute-start(bf16[528,256]{1,0:T(8,128)(2,1)S(1)} %get-tuple-element.74), channel_id=1, source_target_pairs={{0,8},{1,9},{2,10},{3,11},{4,12},{5,13},{6,14},{7,15},{8,0},{9,1},... | collective-permute-start | bytes 811016 | tf_op jit(solution)/shard_map/ppermute | solution.py:57
  98.2 11.3 %collective-permute-start.44 = (bf16[528,256]{1,0:T(8,128)(2,1)S(1)}, bf16[528,256]{1,0:T(8,128)(2,1)S(1)}, u32[]{:S(2)}, u32[]{:S(2)}) collective-permute-start(bf16[528,256]{1,0:T(8,128)(2,1)S(1)} %get-tuple-element.77), channel_id=1, source_target_pairs={{0,8},{1,9},{2,10},{3,11},{4,12},{5,13},{6,14},{7,15},{8,0},{9,1},... | collective-permute-start | bytes 811016 | tf_op jit(solution)/shard_map/ppermute | solution.py:57
  102.5 7.2 %collective-permute-start.35 = (bf16[512,256]{1,0:T(8,128)(2,1)S(1)}, bf16[512,256]{1,0:T(8,128)(2,1)S(1)}, u32[]{:S(2)}, u32[]{:S(2)}) collective-permute-start(bf16[512,256]{1,0:T(8,128)(2,1)S(1)} %get-tuple-element.73), channel_id=1, source_target_pairs={{0,8},{1,9},{2,10},{3,11},{4,12},{5,13},{6,14},{7,15},{8,0},{9,1},... | collective-permute-start | bytes 786440 | tf_op jit(solution)/shard_map/ppermute | solution.py:57
  104.4 9.9 %collective-permute-start.34 = (bf16[512,256]{1,0:T(8,128)(2,1)S(1)}, bf16[512,256]{1,0:T(8,128)(2,1)S(1)}, u32[]{:S(2)}, u32[]{:S(2)}) collective-permute-start(bf16[512,256]{1,0:T(8,128)(2,1)S(1)} %combine.10.refs_3_.refs_2_), channel_id=1, source_target_pairs={{0,2},{1,3},{2,4},{3,5},{4,6},{5,7},{6,0},{7,1},{8,10},{9,11},{10,... | collective-permute-start | bytes 786440 | tf_op jit(solution)/shard_map/ppermute | solution.py:57
  104.5 14.1 %collective-permute-start.42 = (bf16[528,256]{1,0:T(8,128)(2,1)S(1)}, bf16[528,256]{1,0:T(8,128)(2,1)S(1)}, u32[]{:S(2)}, u32[]{:S(2)}) collective-permute-start(bf16[528,256]{1,0:T(8,128)(2,1)S(1)} %get-tuple-element.76), channel_id=1, source_target_pairs={{0,8},{1,9},{2,10},{3,11},{4,12},{5,13},{6,14},{7,15},{8,0},{9,1},... | collective-permute-start | bytes 811016 | tf_op jit(solution)/shard_map/ppermute | solution.py:57
  108.3 6.1 %collective-permute-start.39 = (bf16[512,256]{1,0:T(8,128)(2,1)S(1)}, bf16[512,256]{1,0:T(8,128)(2,1)S(1)}, u32[]{:S(2)}, u32[]{:S(2)}) collective-permute-start(bf16[512,256]{1,0:T(8,128)(2,1)S(1)} %get-tuple-element.75), channel_id=1, source_target_pairs={{0,8},{1,9},{2,10},{3,11},{4,12},{5,13},{6,14},{7,15},{8,0},{9,1},... | collective-permute-start | bytes 786440 | tf_op jit(solution)/shard_map/ppermute | solution.py:57
  109.5 10.5 %collective-permute-start.41 = (bf16[528,256]{1,0:T(8,128)(2,1)S(1)}, bf16[528,256]{1,0:T(8,128)(2,1)S(1)}, u32[]{:S(2)}, u32[]{:S(2)}) collective-permute-start(bf16[528,256]{1,0:T(8,128)(2,1)S(1)} %combine.11.refs_4_.refs_3_), channel_id=1, source_target_pairs={{0,2},{1,3},{2,4},{3,5},{4,6},{5,7},{6,0},{7,1},{8,10},{9,11},{10,... | collective-permute-start | bytes 811016 | tf_op jit(solution)/shard_map/ppermute | solution.py:57
  109.7 17.3 %collective-permute-start.45 = (bf16[528,256]{1,0:T(8,128)(2,1)S(1)}, bf16[528,256]{1,0:T(8,128)(2,1)S(1)}, u32[]{:S(2)}, u32[]{:S(2)}) collective-permute-start(bf16[528,256]{1,0:T(8,128)(2,1)S(1)} %combine.15), channel_id=1, source_target_pairs={{0,0},{1,8},{2,2},{3,10},{4,4},{5,12},{6,6},{7,14},{8,1},{9,9},{10... | collective-permute-start | bytes 811016 | tf_op jit(solution)/shard_map/ppermute | solution.py:57
  114.4 12.6 %collective-permute-start.38 = (bf16[512,256]{1,0:T(8,128)(2,1)S(1)}, bf16[512,256]{1,0:T(8,128)(2,1)S(1)}, u32[]{:S(2)}, u32[]{:S(2)}) collective-permute-start(bf16[512,256]{1,0:T(8,128)(2,1)S(1)} %combine.12.refs_3_), channel_id=1, source_target_pairs={{0,2},{1,10},{2,4},{3,12},{4,6},{5,14},{6,0},{7,8},{8,3},{9,11},{1... | collective-permute-start | bytes 786440 | tf_op jit(solution)/shard_map/ppermute | solution.py:57
  114.5 12.4 %collective-permute-start.40 = (bf16[512,256]{1,0:T(8,128)(2,1)S(1)}, bf16[512,256]{1,0:T(8,128)(2,1)S(1)}, u32[]{:S(2)}, u32[]{:S(2)}) collective-permute-start(bf16[512,256]{1,0:T(8,128)(2,1)S(1)} %combine.13), channel_id=1, source_target_pairs={{0,0},{1,8},{2,2},{3,10},{4,4},{5,12},{6,6},{7,14},{8,1},{9,9},{10... | collective-permute-start | bytes 786440 | tf_op jit(solution)/shard_map/ppermute | solution.py:57
  120.2 12.2 %collective-permute-start.43 = (bf16[528,256]{1,0:T(8,128)(2,1)S(1)}, bf16[528,256]{1,0:T(8,128)(2,1)S(1)}, u32[]{:S(2)}, u32[]{:S(2)}) collective-permute-start(bf16[528,256]{1,0:T(8,128)(2,1)S(1)} %combine.14), channel_id=1, source_target_pairs={{0,2},{1,10},{2,4},{3,12},{4,6},{5,14},{6,0},{7,8},{8,3},{9,11},{1... | collective-permute-start | bytes 811016 | tf_op jit(solution)/shard_map/ppermute | solution.py:57
  (16 other events, 36.5 us)

commit v6 on v5

--- a/solution.py
+++ b/solution.py
@@ -539,8 +539,12 @@
                 after = (added,)
         return tuple(sent)
 
-    sums_of(first, ())
-    after = step(first, ())
+    after = ()
+    for j in range(parts):
+        kept_part, sent_part = numerator(first, j, after)
+        pair = (kept_part, send(sent_part, routes.core))
+        after += (combine(j, pair),)
+        moving[j] = (send(after[-1], routes.home if ring == 2 else routes.shift[1]),)
     for s in others:
         sums_of(s, after)
     after = tuple(pairs[s, j][0] for s in others for j in range(parts))

time: 134 us -> 135 us (level)
  waiting for transfers between devices: 47.9 us -> 49.4 us
    ppermute x46, waiting for transfers between devices: 47.9 us -> 49.4 us  [send(): return lax.ppermute(value, AXES, route)]
  transfers between devices with their start and end apart: 46 -> 46, of which waited for: 23 -> 24; matrix products, arithmetic and copies ran while one was open for 0% -> 0% of each run, Pallas kernels for 15% -> 13%
where the time goes in v6:
time: 135 us
  starting transfers between devices  50.9 us (38%)
  waiting for transfers between devices  49.4 us (37%)
  Pallas kernels  31.6 us (23%)
  local copies, waits for them, and re-layouts  2.09 us (2%)
    ppermute x46, starting transfers between devices, send(): return lax.ppermute(value, AXES, route)  50.9 us
    ppermute x46, waiting for transfers between devices, send(): return lax.ppermute(value, AXES, route)  49.4 us
    pallas_call x35, Pallas kernels, call(): pl.pallas_call(ordered, out_shape=outs, in_specs=(specs or [VMEM] * len(a...  31.6 us
  transfers between devices with their start and end apart: 46, of which 24 were waited for; matrix products, arithmetic and copies ran while one was open for 0% of the time, Pallas kernels for 13%

profile of v6, /device:TPU:1, one launch (start us, length us, event | category | flops | bytes accessed | tf_op | source)
XLA Modules:
  0.0 135.0 jit_solution(1079808748428103217)
XLA Ops:
  0.6 4.5 %collective-permute-start.3 = (bf16[256,1024]{1,0:T(8,128)(2,1)}, bf16[256,1024]{1,0:T(8,128)(2,1)S(1)}, u32[]{:S(2)}, u32[]{:S(2)}) collective-permute-start(bf16[256,1024]{1,0:T(8,128)(2,1)} %param.5), channel_id=1, source_target_pairs={{0,0},{1,8},{2,2},{3,10},{4,4},{5,12},{6,6},{7,14},{8,1},{9,9},{10... | collective-permute-start | bytes 1572872 | tf_op jit(solution)/shard_map/ppermute | solution.py:57
  16.3 2.5 %collective-permute-done.4.refs_0_ = bf16[96,1024]{1,0:T(8,128)(2,1)S(1)} collective-permute-done((bf16[96,1024]{1,0:T(8,128)(2,1)S(1)}, bf16[96,1024]{1,0:T(8,128)(2,1)S(1)}, u32[]{:S(2)}, u32[]{:S(2)}) %collective-permute-start.4) | collective-permute-done | bytes 196640 | tf_op jit(solution)/shard_map/ppermute | solution.py:57
  18.8 2.0 %collective-permute-start.6 = (bf16[96,1024]{1,0:T(8,128)(2,1)S(1)}, bf16[96,1024]{1,0:T(8,128)(2,1)S(1)}, u32[]{:S(2)}, u32[]{:S(2)}) collective-permute-start(bf16[96,1024]{1,0:T(8,128)(2,1)S(1)} %tie.17.refs_3_.refs_5_), channel_id=1, source_target_pairs={{0,8},{1,9},{2,10},{3,11},{4,12},{5,13},{6,14},{7,15},{8,0},{9,1},... | collective-permute-start | bytes 589832 | tf_op jit(solution)/shard_map/ppermute | solution.py:57
  20.8 2.5 %collective-permute-done.5.refs_0_ = bf16[160,1024]{1,0:T(8,128)(2,1)S(1)} collective-permute-done((bf16[160,1024]{1,0:T(8,128)(2,1)S(1)}, bf16[160,1024]{1,0:T(8,128)(2,1)S(1)}, u32[]{:S(2)}, u32[]{:S(2)}) %collective-permute-start.5) | collective-permute-done | bytes 327712 | tf_op jit(solution)/shard_map/ppermute | solution.py:57
  23.3 4.2 %collective-permute-done.8.refs_0_ = bf16[96,1024]{1,0:T(8,128)(2,1)S(1)} collective-permute-done((bf16[96,1024]{1,0:T(8,128)(2,1)S(1)}, bf16[96,1024]{1,0:T(8,128)(2,1)S(1)}, u32[]{:S(2)}, u32[]{:S(2)}) %collective-permute-start.8) | collective-permute-done | bytes 196640 | tf_op jit(solution)/shard_map/ppermute | solution.py:57
  27.6 4.9 %collective-permute-done.refs_2_.refs_1_ = bf16[384,1024]{1,0:T(8,128)(2,1)S(1)} collective-permute-done((bf16[384,1024]{1,0:T(8,128)(2,1)S(1)}, bf16[384,1024]{1,0:T(8,128)(2,1)S(1)}, u32[]{:S(2)}, u32[]{:S(2)}) %collective-permute-start) | collective-permute-done | bytes 786464 | tf_op jit(solution)/shard_map/ppermute | solution.py:57
  32.5 2.1 %collective-permute-start.2 = (bf16[384,1024]{1,0:T(8,128)(2,1)S(1)}, bf16[384,1024]{1,0:T(8,128)(2,1)S(1)}, u32[]{:S(2)}, u32[]{:S(2)}) collective-permute-start(bf16[384,1024]{1,0:T(8,128)(2,1)S(1)} %tie.14), channel_id=1, source_target_pairs={{0,17},{1,16},{2,19},{3,18},{4,21},{5,20},{6,23},{7,22},{8,25},{9,... | collective-permute-start | bytes 2359304 | tf_op jit(solution)/shard_map/ppermute | solution.py:57
  34.6 1.8 %collective-permute-start.10 = (bf16[96,1024]{1,0:T(8,128)(2,1)S(1)}, bf16[96,1024]{1,0:T(8,128)(2,1)S(1)}, u32[]{:S(2)}, u32[]{:S(2)}) collective-permute-start(bf16[96,1024]{1,0:T(8,128)(2,1)S(1)} %tie.21.refs_7_.refs_9_), channel_id=1, source_target_pairs={{0,8},{1,9},{2,10},{3,11},{4,12},{5,13},{6,14},{7,15},{8,0},{9,1},... | collective-permute-start | bytes 589832 | tf_op jit(solution)/shard_map/ppermute | solution.py:57
  36.4 3.8 %collective-permute-start.7 = (bf16[160,1024]{1,0:T(8,128)(2,1)S(1)}, bf16[160,1024]{1,0:T(8,128)(2,1)S(1)}, u32[]{:S(2)}, u32[]{:S(2)}) collective-permute-start(bf16[160,1024]{1,0:T(8,128)(2,1)S(1)} %tie.19.refs_4_.refs_6_), channel_id=1, source_target_pairs={{0,8},{1,9},{2,10},{3,11},{4,12},{5,13},{6,14},{7,15},{8,0},{9,1},... | collective-permute-start | bytes 983048 | tf_op jit(solution)/shard_map/ppermute | solution.py:57
  40.3 2.0 %collective-permute-start.14 = (bf16[160,1024]{1,0:T(8,128)(2,1)S(1)}, bf16[160,1024]{1,0:T(8,128)(2,1)S(1)}, u32[]{:S(2)}, u32[]{:S(2)}) collective-permute-start(bf16[160,1024]{1,0:T(8,128)(2,1)S(1)} %tie.22.refs_1_.refs_5_.refs_14_), channel_id=1, source_target_pairs={{0,8},{1,9},{2,10},{3,11},{4,12},{5,13},{6,14},{7,15},{8,0},{9,1},... | collective-permute-start | bytes 983048 | tf_op jit(solution)/shard_map/ppermute | solution.py:57
  42.5 3.8 %weights.4 = (bf16[1536,1024]{1,0:T(8,128)(2,1)S(1)}, f32[1,1536]{1,0:T(1,128)S(1)}, bf16[1536,2048]{1,0:T(8,128)(2,1)S(1)}, f32[1,2048]{1,0:T(1,128)S(1)}) custom-call(bf16[384,1024]{1,0:T(8,128)(2,1)S(1)} %pick_rows.7.refs_0_.refs_1_, bf16[384,1024]{1,0:T(8,128)(2,1)S(1)} %collective-permute-done.refs_2_.refs_1_, ...), custom_call_target="tpu_custom_call" | custom-call | tf_op jit(solution)/shard_map/weights/pallas_call | solution.py:72
  46.2 1.6 %weights.5 = (bf16[1536,1024]{1,0:T(8,128)(2,1)S(1)}, f32[1,1536]{1,0:T(1,128)S(1)}, bf16[1536,2048]{1,0:T(8,128)(2,1)S(1)}, f32[1,2048]{1,0:T(1,128)S(1)}) custom-call(bf16[1536,1024]{1,0:T(8,128)(2,1)S(1)} %get-tuple-element.43.refs_0_, ...), custom_call_target="tpu_custom_call", output_to_operand_aliasing={{0}: (0, {}), {1}: (1, {}), {2}: (2, {}), {3}: (3, {})} | custom-call | tf_op jit(solution)/shard_map/weights/pallas_call | solution.py:72
  47.8 3.0 %collective-permute-done.2.refs_0_ = bf16[384,1024]{1,0:T(8,128)(2,1)S(1)} collective-permute-done((bf16[384,1024]{1,0:T(8,128)(2,1)S(1)}, bf16[384,1024]{1,0:T(8,128)(2,1)S(1)}, u32[]{:S(2)}, u32[]{:S(2)}) %collective-permute-start.2) | collective-permute-done | bytes 786464 | tf_op jit(solution)/shard_map/ppermute | solution.py:57
  50.8 1.8 %weights.6 = (bf16[1536,1024]{1,0:T(8,128)(2,1)S(1)}, f32[1,1536]{1,0:T(1,128)S(1)}, bf16[1536,2048]{1,0:T(8,128)(2,1)S(1)}, f32[1,2048]{1,0:T(1,128)S(1)}) custom-call(bf16[1536,1024]{1,0:T(8,128)(2,1)S(1)} %get-tuple-element.47.refs_0_, ...), custom_call_target="tpu_custom_call", output_to_operand_aliasing={{0}: (0, {}), {1}: (1, {}), {2}: (2, {}), {3}: (3, {})} | custom-call | tf_op jit(solution)/shard_map/weights/pallas_call | solution.py:72
  53.1 2.2 %collective-permute-start.17 = (bf16[160,1024]{1,0:T(8,128)(2,1)S(1)}, bf16[160,1024]{1,0:T(8,128)(2,1)S(1)}, u32[]{:S(2)}, u32[]{:S(2)}) collective-permute-start(bf16[160,1024]{1,0:T(8,128)(2,1)S(1)} %tie.26.refs_5_), channel_id=1, source_target_pairs={{0,8},{1,9},{2,10},{3,11},{4,12},{5,13},{6,14},{7,15},{8,0},{9,1},... | collective-permute-start | bytes 983048 | tf_op jit(solution)/shard_map/ppermute | solution.py:57
  56.8 2.0 %weights.7 = (bf16[1536,1024]{1,0:T(8,128)(2,1)S(1)}, f32[1,1536]{1,0:T(1,128)S(1)}, bf16[1536,2048]{1,0:T(8,128)(2,1)S(1)}, f32[1,2048]{1,0:T(1,128)S(1)}) custom-call(bf16[1536,1024]{1,0:T(8,128)(2,1)S(1)} %get-tuple-element.51.refs_0_, ...), custom_call_target="tpu_custom_call", output_to_operand_aliasing={{0}: (0, {}), {1}: (1, {}), {2}: (2, {}), {3}: (3, {})} | custom-call | tf_op jit(solution)/shard_map/weights/pallas_call | solution.py:72
  60.0 2.3 %collective-permute-start.20 = (f32[1,2048]{1,0:T(1,128)S(1)}, f32[1,2048]{1,0:T(1,128)S(1)}, u32[]{:S(2)}, u32[]{:S(2)}) collective-permute-start(f32[1,2048]{1,0:T(1,128)S(1)} %join_cores.3.refs_2_), channel_id=1, source_target_pairs={{0,2},{1,3},{2,4},{3,5},{4,6},{5,7},{6,0},{7,1},{8,14},{9,15},{10,... | collective-permute-start | bytes 24584 | tf_op jit(solution)/shard_map/ppermute | solution.py:57
  63.1 2.7 %collective-permute-start.21 = (f32[1,2048]{1,0:T(1,128)S(1)}, f32[1,2048]{1,0:T(1,128)S(1)}, u32[]{:S(2)}, u32[]{:S(2)}) collective-permute-start(f32[1,2048]{1,0:T(1,128)S(1)} %collective-permute-done.20.refs_4_), channel_id=1, source_target_pairs={{0,8},{1,9},{2,10},{3,11},{4,12},{5,13},{6,14},{7,15},{8,0},{9,1},... | collective-permute-start | bytes 24584 | tf_op jit(solution)/shard_map/ppermute | solution.py:57
  66.7 2.6 %sweep.2.refs_0_ = f32[1,2048]{1,0:T(1,128)S(1)} custom-call(f32[1,1536]{1,0:T(1,128)S(1)} %get-tuple-element.56.refs_0_, bf16[1536,2048]{1,0:T(8,128)(2,1)S(1)} %get-tuple-element.55.refs_1_.refs_2_, f32[1,2048]{1,0:T(1,128)S(1)} %join_cores.3.refs_2_, f32[1,2048]{1,0:T(1,128)S(1)} %collective-permute-done.19.refs_3_, ...), custom_call_target="tpu_custom_call" | custom-call | tf_op jit(solution)/shard_map/sweep/pallas_call | solution.py:72
  70.5 1.5 %collective-permute-start.24 = (f32[1,2048]{1,0:T(1,128)S(1)}, f32[1,2048]{1,0:T(1,128)S(1)}, u32[]{:S(2)}, u32[]{:S(2)}) collective-permute-start(f32[1,2048]{1,0:T(1,128)S(1)} %join_cores.4.refs_2_), channel_id=1, source_target_pairs={{0,2},{1,3},{2,4},{3,5},{4,6},{5,7},{6,0},{7,1},{8,14},{9,15},{10,... | collective-permute-start | bytes 24584 | tf_op jit(solution)/shard_map/ppermute | solution.py:57
  73.0 3.3 %collective-permute-start.25 = (f32[1,2048]{1,0:T(1,128)S(1)}, f32[1,2048]{1,0:T(1,128)S(1)}, u32[]{:S(2)}, u32[]{:S(2)}) collective-permute-start(f32[1,2048]{1,0:T(1,128)S(1)} %collective-permute-done.24.refs_4_), channel_id=1, source_target_pairs={{0,8},{1,9},{2,10},{3,11},{4,12},{5,13},{6,14},{7,15},{8,0},{9,1},... | collective-permute-start | bytes 24584 | tf_op jit(solution)/shard_map/ppermute | solution.py:57
  77.1 2.6 %sweep.3.refs_0_ = f32[1,2048]{1,0:T(1,128)S(1)} custom-call(f32[1,1536]{1,0:T(1,128)S(1)} %get-tuple-element.56.refs_0_, bf16[1536,2048]{1,0:T(8,128)(2,1)S(1)} %get-tuple-element.55.refs_1_.refs_2_, f32[1,2048]{1,0:T(1,128)S(1)} %join_cores.4.refs_2_, f32[1,2048]{1,0:T(1,128)S(1)} %collective-permute-done.23.refs_3_, ...), custom_call_target="tpu_custom_call" | custom-call | tf_op jit(solution)/shard_map/sweep/pallas_call | solution.py:72
  83.4 3.3 %collective-permute-start.29 = (f32[1,2048]{1,0:T(1,128)S(1)}, f32[1,2048]{1,0:T(1,128)S(1)}, u32[]{:S(2)}, u32[]{:S(2)}) collective-permute-start(f32[1,2048]{1,0:T(1,128)S(1)} %collective-permute-done.28.refs_4_), channel_id=1, source_target_pairs={{0,8},{1,9},{2,10},{3,11},{4,12},{5,13},{6,14},{7,15},{8,0},{9,1},... | collective-permute-start | bytes 24584 | tf_op jit(solution)/shard_map/ppermute | solution.py:57
  87.6 1.8 %last_sweep.1 = (f32[1,1536]{1,0:T(1,128)S(1)}, f32[1,2048]{1,0:T(1,128)S(1)}) custom-call(f32[1,1536]{1,0:T(1,128)S(1)} %get-tuple-element.56.refs_0_, bf16[1536,2048]{1,0:T(8,128)(2,1)S(1)} %get-tuple-element.55.refs_1_.refs_2_, f32[1,2048]{1,0:T(1,128)S(1)} %join_cores.5.refs_2_, f32[1,2048]{1,0:T(1,128)S(1)} %collective-permute-done.27.refs_3_, ...), custom_call_target="tpu_custom_call" | custom-call | tf_op jit(solution)/shard_map/last_sweep/pallas_call | solution.py:72
  103.8 1.7 %collective-permute-start.35 = (bf16[512,256]{1,0:T(8,128)(2,1)S(1)}, bf16[512,256]{1,0:T(8,128)(2,1)S(1)}, u32[]{:S(2)}, u32[]{:S(2)}) collective-permute-start(bf16[512,256]{1,0:T(8,128)(2,1)S(1)} %get-tuple-element.73), channel_id=1, source_target_pairs={{0,8},{1,9},{2,10},{3,11},{4,12},{5,13},{6,14},{7,15},{8,0},{9,1},... | collective-permute-start | bytes 786440 | tf_op jit(solution)/shard_map/ppermute | solution.py:57
  105.8 3.8 %collective-permute-done.36.refs_0_ = bf16[528,256]{1,0:T(8,128)(2,1)S(1)} collective-permute-done((bf16[528,256]{1,0:T(8,128)(2,1)S(1)}, bf16[528,256]{1,0:T(8,128)(2,1)S(1)}, u32[]{:S(2)}, u32[]{:S(2)}) %collective-permute-start.36) | collective-permute-done | bytes 270368 | tf_op jit(solution)/shard_map/ppermute | solution.py:57
  111.0 2.9 %collective-permute-start.45 = (bf16[528,256]{1,0:T(8,128)(2,1)S(1)}, bf16[528,256]{1,0:T(8,128)(2,1)S(1)}, u32[]{:S(2)}, u32[]{:S(2)}) collective-permute-start(bf16[528,256]{1,0:T(8,128)(2,1)S(1)} %combine.15), channel_id=1, source_target_pairs={{0,0},{1,8},{2,2},{3,10},{4,4},{5,12},{6,6},{7,14},{8,1},{9,9},{10... | collective-permute-start | bytes 811016 | tf_op jit(solution)/shard_map/ppermute | solution.py:57
  113.9 1.7 %collective-permute-done.34.refs_0_ = bf16[512,256]{1,0:T(8,128)(2,1)S(1)} collective-permute-done((bf16[512,256]{1,0:T(8,128)(2,1)S(1)}, bf16[512,256]{1,0:T(8,128)(2,1)S(1)}, u32[]{:S(2)}, u32[]{:S(2)}) %collective-permute-start.34) | collective-permute-done | bytes 262176 | tf_op jit(solution)/shard_map/ppermute | solution.py:57
  115.8 3.9 %collective-permute-start.40 = (bf16[512,256]{1,0:T(8,128)(2,1)S(1)}, bf16[512,256]{1,0:T(8,128)(2,1)S(1)}, u32[]{:S(2)}, u32[]{:S(2)}) collective-permute-start(bf16[512,256]{1,0:T(8,128)(2,1)S(1)} %combine.13), channel_id=1, source_target_pairs={{0,0},{1,8},{2,2},{3,10},{4,4},{5,12},{6,6},{7,14},{8,1},{9,9},{10... | collective-permute-start | bytes 786440 | tf_op jit(solution)/shard_map/ppermute | solution.py:57
  119.8 1.6 %collective-permute-done.41.refs_0_ = bf16[528,256]{1,0:T(8,128)(2,1)S(1)} collective-permute-done((bf16[528,256]{1,0:T(8,128)(2,1)S(1)}, bf16[528,256]{1,0:T(8,128)(2,1)S(1)}, u32[]{:S(2)}, u32[]{:S(2)}) %collective-permute-start.41) | collective-permute-done | bytes 270368 | tf_op jit(solution)/shard_map/ppermute | solution.py:57
  121.6 6.6 %collective-permute-done.38.refs_0_ = bf16[512,256]{1,0:T(8,128)(2,1)S(1)} collective-permute-done((bf16[512,256]{1,0:T(8,128)(2,1)S(1)}, bf16[512,256]{1,0:T(8,128)(2,1)S(1)}, u32[]{:S(2)}, u32[]{:S(2)}) %collective-permute-start.38) | collective-permute-done | bytes 262176 | tf_op jit(solution)/shard_map/ppermute | solution.py:57
  128.2 5.5 %collective-permute-done.43.refs_2_ = bf16[528,256]{1,0:T(8,128)(2,1)S(1)} collective-permute-done((bf16[528,256]{1,0:T(8,128)(2,1)S(1)}, bf16[528,256]{1,0:T(8,128)(2,1)S(1)}, u32[]{:S(2)}, u32[]{:S(2)}) %collective-permute-start.43) | collective-permute-done | bytes 270368 | tf_op jit(solution)/shard_map/ppermute | solution.py:57
  (113 shorter events, 41.5 us)
Async XLA Ops:
  0.6 11.6 %collective-permute-start.3 = (bf16[256,1024]{1,0:T(8,128)(2,1)}, bf16[256,1024]{1,0:T(8,128)(2,1)S(1)}, u32[]{:S(2)}, u32[]{:S(2)}) collective-permute-start(bf16[256,1024]{1,0:T(8,128)(2,1)} %param.5), channel_id=1, source_target_pairs={{0,0},{1,8},{2,2},{3,10},{4,4},{5,12},{6,6},{7,14},{8,1},{9,9},{10... | collective-permute-start | bytes 1572872 | tf_op jit(solution)/shard_map/ppermute | solution.py:57
  12.4 6.4 %collective-permute-start.4 = (bf16[96,1024]{1,0:T(8,128)(2,1)S(1)}, bf16[96,1024]{1,0:T(8,128)(2,1)S(1)}, u32[]{:S(2)}, u32[]{:S(2)}) collective-permute-start(bf16[96,1024]{1,0:T(8,128)(2,1)S(1)} %get-tuple-element.41.refs_0_), channel_id=1, source_target_pairs={{0,2},{1,3},{2,4},{3,5},{4,6},{5,7},{6,0},{7,1},{8,10},{9,11},{10,... | collective-permute-start | bytes 589832 | tf_op jit(solution)/shard_map/ppermute | solution.py:57
  13.8 18.7 %collective-permute-start = (bf16[384,1024]{1,0:T(8,128)(2,1)S(1)}, bf16[384,1024]{1,0:T(8,128)(2,1)S(1)}, u32[]{:S(2)}, u32[]{:S(2)}) collective-permute-start(bf16[384,1024]{1,0:T(8,128)(2,1)S(1)} %pick_rows.5.refs_2_), channel_id=1, source_target_pairs={{0,1},{1,0},{2,3},{3,2},{4,5},{5,4},{6,7},{7,6},{8,9},{9,8},{10,11... | collective-permute-start | bytes 2359304 | tf_op jit(solution)/shard_map/ppermute | solution.py:57
  13.8 18.7 %collective-permute-start.1 = (bf16[384,1024]{1,0:T(8,128)(2,1)S(1)}, bf16[384,1024]{1,0:T(8,128)(2,1)S(1)}, u32[]{:S(2)}, u32[]{:S(2)}) collective-permute-start(bf16[384,1024]{1,0:T(8,128)(2,1)S(1)} %pick_rows.4.refs_2_), channel_id=1, source_target_pairs={{0,16},{1,17},{2,18},{3,19},{4,20},{5,21},{6,22},{7,23},{8,24},{9,... | collective-permute-start | bytes 2359304 | tf_op jit(solution)/shard_map/ppermute | solution.py:57
  15.0 8.3 %collective-permute-start.5 = (bf16[160,1024]{1,0:T(8,128)(2,1)S(1)}, bf16[160,1024]{1,0:T(8,128)(2,1)S(1)}, u32[]{:S(2)}, u32[]{:S(2)}) collective-permute-start(bf16[160,1024]{1,0:T(8,128)(2,1)S(1)} %get-tuple-element.42.refs_0_), channel_id=1, source_target_pairs={{0,2},{1,3},{2,4},{3,5},{4,6},{5,7},{6,0},{7,1},{8,10},{9,11},{10,... | collective-permute-start | bytes 983048 | tf_op jit(solution)/shard_map/ppermute | solution.py:57
  18.8 8.7 %collective-permute-start.8 = (bf16[96,1024]{1,0:T(8,128)(2,1)S(1)}, bf16[96,1024]{1,0:T(8,128)(2,1)S(1)}, u32[]{:S(2)}, u32[]{:S(2)}) collective-permute-start(bf16[96,1024]{1,0:T(8,128)(2,1)S(1)} %tie.16.refs_1_.refs_0_), channel_id=1, source_target_pairs={{0,2},{1,3},{2,4},{3,5},{4,6},{5,7},{6,0},{7,1},{8,10},{9,11},{10,... | collective-permute-start | bytes 589832 | tf_op jit(solution)/shard_map/ppermute | solution.py:57
  18.8 21.4 %collective-permute-start.6 = (bf16[96,1024]{1,0:T(8,128)(2,1)S(1)}, bf16[96,1024]{1,0:T(8,128)(2,1)S(1)}, u32[]{:S(2)}, u32[]{:S(2)}) collective-permute-start(bf16[96,1024]{1,0:T(8,128)(2,1)S(1)} %tie.17.refs_3_.refs_5_), channel_id=1, source_target_pairs={{0,8},{1,9},{2,10},{3,11},{4,12},{5,13},{6,14},{7,15},{8,0},{9,1},... | collective-permute-start | bytes 589832 | tf_op jit(solution)/shard_map/ppermute | solution.py:57
  23.3 13.1 %collective-permute-start.9 = (bf16[160,1024]{1,0:T(8,128)(2,1)S(1)}, bf16[160,1024]{1,0:T(8,128)(2,1)S(1)}, u32[]{:S(2)}, u32[]{:S(2)}) collective-permute-start(bf16[160,1024]{1,0:T(8,128)(2,1)S(1)} %tie.18.refs_1_.refs_0_), channel_id=1, source_target_pairs={{0,2},{1,3},{2,4},{3,5},{4,6},{5,7},{6,0},{7,1},{8,10},{9,11},{10,... | collective-permute-start | bytes 983048 | tf_op jit(solution)/shard_map/ppermute | solution.py:57
  27.6 12.8 %collective-permute-start.12 = (bf16[96,1024]{1,0:T(8,128)(2,1)S(1)}, bf16[96,1024]{1,0:T(8,128)(2,1)S(1)}, u32[]{:S(2)}, u32[]{:S(2)}) collective-permute-start(bf16[96,1024]{1,0:T(8,128)(2,1)S(1)} %tie.20.refs_1_.refs_0_), channel_id=1, source_target_pairs={{0,2},{1,3},{2,4},{3,5},{4,6},{5,7},{6,0},{7,1},{8,10},{9,11},{10,... | collective-permute-start | bytes 589832 | tf_op jit(solution)/shard_map/ppermute | solution.py:57
  32.5 18.3 %collective-permute-start.2 = (bf16[384,1024]{1,0:T(8,128)(2,1)S(1)}, bf16[384,1024]{1,0:T(8,128)(2,1)S(1)}, u32[]{:S(2)}, u32[]{:S(2)}) collective-permute-start(bf16[384,1024]{1,0:T(8,128)(2,1)S(1)} %tie.14), channel_id=1, source_target_pairs={{0,17},{1,16},{2,19},{3,18},{4,21},{5,20},{6,23},{7,22},{8,25},{9,... | collective-permute-start | bytes 2359304 | tf_op jit(solution)/shard_map/ppermute | solution.py:57
  34.6 7.8 %collective-permute-start.10 = (bf16[96,1024]{1,0:T(8,128)(2,1)S(1)}, bf16[96,1024]{1,0:T(8,128)(2,1)S(1)}, u32[]{:S(2)}, u32[]{:S(2)}) collective-permute-start(bf16[96,1024]{1,0:T(8,128)(2,1)S(1)} %tie.21.refs_7_.refs_9_), channel_id=1, source_target_pairs={{0,8},{1,9},{2,10},{3,11},{4,12},{5,13},{6,14},{7,15},{8,0},{9,1},... | collective-permute-start | bytes 589832 | tf_op jit(solution)/shard_map/ppermute | solution.py:57
  36.4 6.0 %collective-permute-start.7 = (bf16[160,1024]{1,0:T(8,128)(2,1)S(1)}, bf16[160,1024]{1,0:T(8,128)(2,1)S(1)}, u32[]{:S(2)}, u32[]{:S(2)}) collective-permute-start(bf16[160,1024]{1,0:T(8,128)(2,1)S(1)} %tie.19.refs_4_.refs_6_), channel_id=1, source_target_pairs={{0,8},{1,9},{2,10},{3,11},{4,12},{5,13},{6,14},{7,15},{8,0},{9,1},... | collective-permute-start | bytes 983048 | tf_op jit(solution)/shard_map/ppermute | solution.py:57
  40.3 5.9 %collective-permute-start.14 = (bf16[160,1024]{1,0:T(8,128)(2,1)S(1)}, bf16[160,1024]{1,0:T(8,128)(2,1)S(1)}, u32[]{:S(2)}, u32[]{:S(2)}) collective-permute-start(bf16[160,1024]{1,0:T(8,128)(2,1)S(1)} %tie.22.refs_1_.refs_5_.refs_14_), channel_id=1, source_target_pairs={{0,8},{1,9},{2,10},{3,11},{4,12},{5,13},{6,14},{7,15},{8,0},{9,1},... | collective-permute-start | bytes 983048 | tf_op jit(solution)/shard_map/ppermute | solution.py:57
  42.4 10.6 %collective-permute-start.15 = (bf16[160,1024]{1,0:T(8,128)(2,1)S(1)}, bf16[160,1024]{1,0:T(8,128)(2,1)S(1)}, u32[]{:S(2)}, u32[]{:S(2)}) collective-permute-start(bf16[160,1024]{1,0:T(8,128)(2,1)S(1)} %tie.22.refs_1_.refs_5_.refs_14_), channel_id=1, source_target_pairs={{0,2},{1,3},{2,4},{3,5},{4,6},{5,7},{6,0},{7,1},{8,10},{9,11},{10,... | collective-permute-start | bytes 983048 | tf_op jit(solution)/shard_map/ppermute | solution.py:57
  72.0 4.3 %collective-permute-start.23 = (f32[1,2048]{1,0:T(1,128)S(1)}, f32[1,2048]{1,0:T(1,128)S(1)}, u32[]{:S(2)}, u32[]{:S(2)}) collective-permute-start(f32[1,2048]{1,0:T(1,128)S(1)} %join_cores.4.refs_2_), channel_id=1, source_target_pairs={{0,4},{1,5},{2,6},{3,7},{4,0},{5,1},{6,2},{7,3},{8,12},{9,13},{10,... | collective-permute-start | bytes 24584 | tf_op jit(solution)/shard_map/ppermute | solution.py:57
  73.0 4.1 %collective-permute-start.25 = (f32[1,2048]{1,0:T(1,128)S(1)}, f32[1,2048]{1,0:T(1,128)S(1)}, u32[]{:S(2)}, u32[]{:S(2)}) collective-permute-start(f32[1,2048]{1,0:T(1,128)S(1)} %collective-permute-done.24.refs_4_), channel_id=1, source_target_pairs={{0,8},{1,9},{2,10},{3,11},{4,12},{5,13},{6,14},{7,15},{8,0},{9,1},... | collective-permute-start | bytes 24584 | tf_op jit(solution)/shard_map/ppermute | solution.py:57
  82.4 5.2 %collective-permute-start.27 = (f32[1,2048]{1,0:T(1,128)S(1)}, f32[1,2048]{1,0:T(1,128)S(1)}, u32[]{:S(2)}, u32[]{:S(2)}) collective-permute-start(f32[1,2048]{1,0:T(1,128)S(1)} %join_cores.5.refs_2_), channel_id=1, source_target_pairs={{0,4},{1,5},{2,6},{3,7},{4,0},{5,1},{6,2},{7,3},{8,12},{9,13},{10,... | collective-permute-start | bytes 24584 | tf_op jit(solution)/shard_map/ppermute | solution.py:57
  83.4 4.2 %collective-permute-start.29 = (f32[1,2048]{1,0:T(1,128)S(1)}, f32[1,2048]{1,0:T(1,128)S(1)}, u32[]{:S(2)}, u32[]{:S(2)}) collective-permute-start(f32[1,2048]{1,0:T(1,128)S(1)} %collective-permute-done.28.refs_4_), channel_id=1, source_target_pairs={{0,8},{1,9},{2,10},{3,11},{4,12},{5,13},{6,14},{7,15},{8,0},{9,1},... | collective-permute-start | bytes 24584 | tf_op jit(solution)/shard_map/ppermute | solution.py:57
  94.3 9.5 %collective-permute-start.31 = (bf16[512,256]{1,0:T(8,128)(2,1)S(1)}, bf16[512,256]{1,0:T(8,128)(2,1)S(1)}, u32[]{:S(2)}, u32[]{:S(2)}) collective-permute-start(bf16[512,256]{1,0:T(8,128)(2,1)S(1)} %combine.8.refs_3_.refs_5_.refs_4_), channel_id=1, source_target_pairs={{0,2},{1,3},{2,4},{3,5},{4,6},{5,7},{6,0},{7,1},{8,10},{9,11},{10,... | collective-permute-start | bytes 786440 | tf_op jit(solution)/shard_map/ppermute | solution.py:57
  97.7 7.8 %collective-permute-start.33 = (bf16[512,256]{1,0:T(8,128)(2,1)S(1)}, bf16[512,256]{1,0:T(8,128)(2,1)S(1)}, u32[]{:S(2)}, u32[]{:S(2)}) collective-permute-start(bf16[512,256]{1,0:T(8,128)(2,1)S(1)} %get-tuple-element.66), channel_id=1, source_target_pairs={{0,8},{1,9},{2,10},{3,11},{4,12},{5,13},{6,14},{7,15},{8,0},{9,1},... | collective-permute-start | bytes 786440 | tf_op jit(solution)/shard_map/ppermute | solution.py:57
  99.0 10.6 %collective-permute-start.36 = (bf16[528,256]{1,0:T(8,128)(2,1)S(1)}, bf16[528,256]{1,0:T(8,128)(2,1)S(1)}, u32[]{:S(2)}, u32[]{:S(2)}) collective-permute-start(bf16[528,256]{1,0:T(8,128)(2,1)S(1)} %combine.9.refs_4_.refs_5_), channel_id=1, source_target_pairs={{0,2},{1,3},{2,4},{3,5},{4,6},{5,7},{6,0},{7,1},{8,10},{9,11},{10,... | collective-permute-start | bytes 811016 | tf_op jit(solution)/shard_map/ppermute | solution.py:57
  99.3 6.4 %collective-permute-start.37 = (bf16[528,256]{1,0:T(8,128)(2,1)S(1)}, bf16[528,256]{1,0:T(8,128)(2,1)S(1)}, u32[]{:S(2)}, u32[]{:S(2)}) collective-permute-start(bf16[528,256]{1,0:T(8,128)(2,1)S(1)} %get-tuple-element.74), channel_id=1, source_target_pairs={{0,8},{1,9},{2,10},{3,11},{4,12},{5,13},{6,14},{7,15},{8,0},{9,1},... | collective-permute-start | bytes 811016 | tf_op jit(solution)/shard_map/ppermute | solution.py:57
  99.6 11.2 %collective-permute-start.44 = (bf16[528,256]{1,0:T(8,128)(2,1)S(1)}, bf16[528,256]{1,0:T(8,128)(2,1)S(1)}, u32[]{:S(2)}, u32[]{:S(2)}) collective-permute-start(bf16[528,256]{1,0:T(8,128)(2,1)S(1)} %get-tuple-element.77), channel_id=1, source_target_pairs={{0,8},{1,9},{2,10},{3,11},{4,12},{5,13},{6,14},{7,15},{8,0},{9,1},... | collective-permute-start | bytes 811016 | tf_op jit(solution)/shard_map/ppermute | solution.py:57
  103.8 7.1 %collective-permute-start.35 = (bf16[512,256]{1,0:T(8,128)(2,1)S(1)}, bf16[512,256]{1,0:T(8,128)(2,1)S(1)}, u32[]{:S(2)}, u32[]{:S(2)}) collective-permute-start(bf16[512,256]{1,0:T(8,128)(2,1)S(1)} %get-tuple-element.73), channel_id=1, source_target_pairs={{0,8},{1,9},{2,10},{3,11},{4,12},{5,13},{6,14},{7,15},{8,0},{9,1},... | collective-permute-start | bytes 786440 | tf_op jit(solution)/shard_map/ppermute | solution.py:57
  105.6 10.0 %collective-permute-start.34 = (bf16[512,256]{1,0:T(8,128)(2,1)S(1)}, bf16[512,256]{1,0:T(8,128)(2,1)S(1)}, u32[]{:S(2)}, u32[]{:S(2)}) collective-permute-start(bf16[512,256]{1,0:T(8,128)(2,1)S(1)} %combine.10.refs_3_.refs_2_), channel_id=1, source_target_pairs={{0,2},{1,3},{2,4},{3,5},{4,6},{5,7},{6,0},{7,1},{8,10},{9,11},{10,... | collective-permute-start | bytes 786440 | tf_op jit(solution)/shard_map/ppermute | solution.py:57
  105.7 14.1 %collective-permute-start.42 = (bf16[528,256]{1,0:T(8,128)(2,1)S(1)}, bf16[528,256]{1,0:T(8,128)(2,1)S(1)}, u32[]{:S(2)}, u32[]{:S(2)}) collective-permute-start(bf16[528,256]{1,0:T(8,128)(2,1)S(1)} %get-tuple-element.76), channel_id=1, source_target_pairs={{0,8},{1,9},{2,10},{3,11},{4,12},{5,13},{6,14},{7,15},{8,0},{9,1},... | collective-permute-start | bytes 811016 | tf_op jit(solution)/shard_map/ppermute | solution.py:57
  109.6 6.1 %collective-permute-start.39 = (bf16[512,256]{1,0:T(8,128)(2,1)S(1)}, bf16[512,256]{1,0:T(8,128)(2,1)S(1)}, u32[]{:S(2)}, u32[]{:S(2)}) collective-permute-start(bf16[512,256]{1,0:T(8,128)(2,1)S(1)} %get-tuple-element.75), channel_id=1, source_target_pairs={{0,8},{1,9},{2,10},{3,11},{4,12},{5,13},{6,14},{7,15},{8,0},{9,1},... | collective-permute-start | bytes 786440 | tf_op jit(solution)/shard_map/ppermute | solution.py:57
  110.8 10.6 %collective-permute-start.41 = (bf16[528,256]{1,0:T(8,128)(2,1)S(1)}, bf16[528,256]{1,0:T(8,128)(2,1)S(1)}, u32[]{:S(2)}, u32[]{:S(2)}) collective-permute-start(bf16[528,256]{1,0:T(8,128)(2,1)S(1)} %combine.11.refs_4_.refs_3_), channel_id=1, source_target_pairs={{0,2},{1,3},{2,4},{3,5},{4,6},{5,7},{6,0},{7,1},{8,10},{9,11},{10,... | collective-permute-start | bytes 811016 | tf_op jit(solution)/shard_map/ppermute | solution.py:57
  111.0 17.2 %collective-permute-start.45 = (bf16[528,256]{1,0:T(8,128)(2,1)S(1)}, bf16[528,256]{1,0:T(8,128)(2,1)S(1)}, u32[]{:S(2)}, u32[]{:S(2)}) collective-permute-start(bf16[528,256]{1,0:T(8,128)(2,1)S(1)} %combine.15), channel_id=1, source_target_pairs={{0,0},{1,8},{2,2},{3,10},{4,4},{5,12},{6,6},{7,14},{8,1},{9,9},{10... | collective-permute-start | bytes 811016 | tf_op jit(solution)/shard_map/ppermute | solution.py:57
  115.7 12.5 %collective-permute-start.38 = (bf16[512,256]{1,0:T(8,128)(2,1)S(1)}, bf16[512,256]{1,0:T(8,128)(2,1)S(1)}, u32[]{:S(2)}, u32[]{:S(2)}) collective-permute-start(bf16[512,256]{1,0:T(8,128)(2,1)S(1)} %combine.12.refs_3_), channel_id=1, source_target_pairs={{0,2},{1,10},{2,4},{3,12},{4,6},{5,14},{6,0},{7,8},{8,3},{9,11},{1... | collective-permute-start | bytes 786440 | tf_op jit(solution)/shard_map/ppermute | solution.py:57
  115.8 12.3 %collective-permute-start.40 = (bf16[512,256]{1,0:T(8,128)(2,1)S(1)}, bf16[512,256]{1,0:T(8,128)(2,1)S(1)}, u32[]{:S(2)}, u32[]{:S(2)}) collective-permute-start(bf16[512,256]{1,0:T(8,128)(2,1)S(1)} %combine.13), channel_id=1, source_target_pairs={{0,0},{1,8},{2,2},{3,10},{4,4},{5,12},{6,6},{7,14},{8,1},{9,9},{10... | collective-permute-start | bytes 786440 | tf_op jit(solution)/shard_map/ppermute | solution.py:57
  121.5 12.2 %collective-permute-start.43 = (bf16[528,256]{1,0:T(8,128)(2,1)S(1)}, bf16[528,256]{1,0:T(8,128)(2,1)S(1)}, u32[]{:S(2)}, u32[]{:S(2)}) collective-permute-start(bf16[528,256]{1,0:T(8,128)(2,1)S(1)} %combine.14), channel_id=1, source_target_pairs={{0,2},{1,10},{2,4},{3,12},{4,6},{5,14},{6,0},{7,8},{8,3},{9,11},{1... | collective-permute-start | bytes 811016 | tf_op jit(solution)/shard_map/ppermute | solution.py:57
  (16 other events, 35.5 us)
